TPU v7x, 128 devices: a whole 4x4x4 slice. The times are simulated.
128 devices in a mesh: seg: 16 (over z_lo, y, core), blk: 8 (over z_hi, x).
Axes of the slice: x: 4, y: 4, z: 4 (z_hi: 2, z_lo: 2; z = z_hi * 2 + z_lo), core: 2. Of those that a mesh axis runs over, the one named last changes fastest.
Arguments:
- queries: float32 [32768, 768], P(('seg', 'blk')), may hold values from -200 to 200
- keys: float32 [32768, 768], P(('seg', 'blk')), may hold values from -6 to 6
- values: float32 [32768, 768], P(('seg', 'blk')), may hold values from -6 to 6
- cotangent: float32 [32768, 768], P(('seg', 'blk')), may hold values from -24 to 24
- offsets: int32 [2, 12], replicated, may hold values from 0 to 31, as said below
Outputs:
- attended: float32 [32768, 768], P(('seg', 'blk'))
- grad_queries: float32 [32768, 768], P(('seg', 'blk'))
- grad_keys: float32 [32768, 768], P(('seg', 'blk'))
- grad_values: float32 [32768, 768], P(('seg', 'blk'))
Inputs may be any that keep to these rules, and one draw needn't show every extreme that they name: offsets[0] lies below 4 and offsets[1] below 32.
All inputs are finite; a program needn't handle non-finite values.
Results may differ from a plain program's by a relative error of at most 0.0003.
Values sent between devices are 32-bit elements; how exact they have to be, the bound alone decides.
No kernel may reach another device: no remote copies, remote signals or barrier semaphores. Data moves between devices by JAX's collectives and lax.ppermute only.
A program may use at most 128 MiB of HBM per device.

v0:
```python
import jax
import jax.numpy as jnp
from jax import lax
from jax.sharding import PartitionSpec as P

HEADS = 12
HD = 64
W1 = 256
R2 = 4
R3 = 32


EXACT_PRECISION = lax.Precision.HIGHEST
MASKED = -1e30


def pick_rows(source, stride, shifts):
    count = source.shape[0] // stride
    parts = source.reshape(count, stride, source.shape[1], source.shape[2])
    index = jnp.broadcast_to(shifts.reshape(1, 1, -1, 1), (count, 1, source.shape[1], 1))
    return jnp.transpose(jnp.take_along_axis(parts, index, axis=1)[:, 0], (1, 0, 2))


def spread_rows(source, stride, shifts, fill):
    head_count, count, extra = source.shape
    hits = jnp.arange(stride).reshape(1, stride, 1, 1) == shifts.reshape(1, 1, -1, 1)
    full = jnp.where(hits, jnp.transpose(source, (1, 0, 2))[:, None], fill)
    return full.reshape(count * stride, head_count, extra)


def forward_block(query_matrix, key_matrix, value_matrix, allowed, score_scale):
    attention_scores = (
        jnp.einsum("aif,ayf->aiy", query_matrix, key_matrix, precision=EXACT_PRECISION)
        * score_scale
    )
    attention_scores = jnp.where(allowed, attention_scores, MASKED)
    highest = jnp.max(attention_scores, axis=-1, keepdims=True)
    attention_weights = jnp.exp(attention_scores - highest)
    softmax_numerators = jnp.einsum(
        "tlo,ton->tln", attention_weights, value_matrix, precision=EXACT_PRECISION
    )
    return (highest, jnp.sum(attention_weights, axis=-1, keepdims=True), softmax_numerators)


def backward_block(
    query_matrix,
    key_matrix,
    value_matrix,
    gradient_rows,
    log_total,
    intersection,
    allowed,
    score_scale,
):
    attention_scores = (
        jnp.einsum("aif,ayf->aiy", query_matrix, key_matrix, precision=EXACT_PRECISION)
        * score_scale
    )
    attention_weights = jnp.exp(jnp.where(allowed, attention_scores, MASKED) - log_total)
    pulled_back = jnp.einsum("aif,ayf->aiy", gradient_rows, value_matrix, precision=EXACT_PRECISION)
    level_slopes = attention_weights * (pulled_back - intersection) * score_scale
    query_gradient = jnp.einsum("tlo,ton->tln", level_slopes, key_matrix, precision=EXACT_PRECISION)
    key_gradient = jnp.einsum("txf,txs->tfs", level_slopes, query_matrix, precision=EXACT_PRECISION)
    value_gradient = jnp.einsum(
        "txf,txs->tfs", attention_weights, gradient_rows, precision=EXACT_PRECISION
    )
    return (query_gradient, key_gradient, value_gradient)


def body(queries, keys, values, cotangent, offsets):
    row_count = queries.shape[0]
    score_scale = HD ** (-0.5)
    query_all = queries.reshape(row_count, HEADS, HD)
    key_all = keys.reshape(row_count, HEADS, HD)
    value_all = values.reshape(row_count, HEADS, HD)
    grad_all = cotangent.reshape(row_count, HEADS, HD)
    near_shift = offsets[0]
    far_shift = offsets[1]
    segments = row_count // W1

    def local_blocks(source):
        return jnp.transpose(source.reshape(segments, W1, HEADS, -1), (0, 2, 1, 3)).reshape(
            segments * HEADS, W1, source.shape[2]
        )

    def local_rows(source):
        return jnp.transpose(source.reshape(segments, HEADS, W1, -1), (0, 2, 1, 3)).reshape(
            row_count, HEADS, source.shape[2]
        )

    lower_local = jnp.tril(jnp.ones((W1, W1), bool))
    query_one = local_blocks(query_all)
    key_one = local_blocks(key_all)
    value_one = local_blocks(value_all)
    query_two = pick_rows(query_all, R2, near_shift)
    key_two = pick_rows(key_all, R2, near_shift)
    value_two = pick_rows(value_all, R2, near_shift)
    query_three = pick_rows(query_all, R3, far_shift)
    key_three = pick_rows(key_all, R3, far_shift)
    value_three = pick_rows(value_all, R3, far_shift)
    key_near, value_near = (
        lax.all_gather(key_two, "blk", axis=1, tiled=True),
        lax.all_gather(value_two, "blk", axis=1, tiled=True),
    )
    key_far, value_far = (
        lax.all_gather(key_three, ("seg", "blk"), axis=1, tiled=True),
        lax.all_gather(value_three, ("seg", "blk"), axis=1, tiled=True),
    )
    span_two = query_two.shape[1]
    span_three = query_three.shape[1]
    own_two = lax.axis_index("blk") * span_two + jnp.arange(span_two)
    allowed_two = jnp.arange(key_near.shape[1])[None, :] <= own_two[:, None]
    device_place = lax.axis_index("seg") * lax.axis_size("blk") + lax.axis_index("blk")
    own_three = device_place * span_three + jnp.arange(span_three)
    allowed_three = jnp.arange(key_far.shape[1])[None, :] <= own_three[:, None]
    max_one, total_one, num_one = forward_block(
        query_one, key_one, value_one, lower_local, score_scale
    )
    max_two, total_two, num_two = forward_block(
        query_two, key_near, value_near, allowed_two, score_scale
    )
    max_three, total_three, num_three = forward_block(
        query_three, key_far, value_far, allowed_three, score_scale
    )
    level_terms = [
        (local_rows(max_one), local_rows(total_one), local_rows(num_one)),
        (
            spread_rows(max_two, R2, near_shift, MASKED),
            spread_rows(total_two, R2, near_shift, 0.0),
            spread_rows(num_two, R2, near_shift, 0.0),
        ),
        (
            spread_rows(max_three, R3, far_shift, MASKED),
            spread_rows(total_three, R3, far_shift, 0.0),
            spread_rows(num_three, R3, far_shift, 0.0),
        ),
    ]
    highest = jnp.maximum(jnp.maximum(level_terms[0][0], level_terms[1][0]), level_terms[2][0])
    totals = jnp.zeros_like(highest)
    softmax_numerators = jnp.zeros_like(query_all)
    for level_max, level_total, level_num in level_terms:
        factor = jnp.exp(level_max - highest)
        totals = totals + level_total * factor
        softmax_numerators = softmax_numerators + level_num * factor
    attended = softmax_numerators / totals
    log_total = highest + jnp.log(totals)
    intersection = jnp.sum(grad_all * attended, axis=-1, keepdims=True)
    grad_q_one, grad_k_one, grad_v_one = backward_block(
        query_one,
        key_one,
        value_one,
        local_blocks(grad_all),
        local_blocks(log_total),
        local_blocks(intersection),
        lower_local,
        score_scale,
    )
    grad_q_two, grad_k_two, grad_v_two = backward_block(
        query_two,
        key_near,
        value_near,
        pick_rows(grad_all, R2, near_shift),
        pick_rows(log_total, R2, near_shift),
        pick_rows(intersection, R2, near_shift),
        allowed_two,
        score_scale,
    )
    grad_q_three, grad_k_three, grad_v_three = backward_block(
        query_three,
        key_far,
        value_far,
        pick_rows(grad_all, R3, far_shift),
        pick_rows(log_total, R3, far_shift),
        pick_rows(intersection, R3, far_shift),
        allowed_three,
        score_scale,
    )
    owned_k_two, owned_v_two = (
        lax.psum_scatter(grad_k_two, "blk", scatter_dimension=1, tiled=True),
        lax.psum_scatter(grad_v_two, "blk", scatter_dimension=1, tiled=True),
    )
    owned_k_three, owned_v_three = (
        lax.psum_scatter(grad_k_three, ("seg", "blk"), scatter_dimension=1, tiled=True),
        lax.psum_scatter(grad_v_three, ("seg", "blk"), scatter_dimension=1, tiled=True),
    )
    grad_queries = (
        local_rows(grad_q_one)
        + spread_rows(grad_q_two, R2, near_shift, 0.0)
        + spread_rows(grad_q_three, R3, far_shift, 0.0)
    )
    grad_keys = (
        local_rows(grad_k_one)
        + spread_rows(owned_k_two, R2, near_shift, 0.0)
        + spread_rows(owned_k_three, R3, far_shift, 0.0)
    )
    grad_values = (
        local_rows(grad_v_one)
        + spread_rows(owned_v_two, R2, near_shift, 0.0)
        + spread_rows(owned_v_three, R3, far_shift, 0.0)
    )
    width_all = HEADS * HD
    return (
        attended.reshape(row_count, width_all),
        grad_queries.reshape(row_count, width_all),
        grad_keys.reshape(row_count, width_all),
        grad_values.reshape(row_count, width_all),
    )


def solution(mesh):
    return jax.shard_map(
        body,
        mesh=mesh,
        in_specs=(
            P(("seg", "blk"), None),
            P(("seg", "blk"), None),
            P(("seg", "blk"), None),
            P(("seg", "blk"), None),
            P(),
        ),
        out_specs=(
            P(("seg", "blk"), None),
            P(("seg", "blk"), None),
            P(("seg", "blk"), None),
            P(("seg", "blk"), None),
        ),
        check_vma=False,
    )
```

profile of v0, /device:TPU:0, one launch (start us, length us, event | category | flops | bytes accessed | tf_op | source)
XLA Modules:
  0.0 2209.6 jit_solution(18265021390924738765)
XLA Ops:
  11.1 2.7 reshape_reshape.40
  13.9 2.3 copy.404
  16.2 4.0 gather_fusion.1
  21.0 1.8 reshape_reshape.43
  22.8 2.3 copy.425
  25.2 4.0 gather_fusion.4
  29.3 2.2 fusion.19
  32.4 1.8 reshape_reshape.42
  34.9 3.2 copy.414
  38.1 2.2 gather_fusion.3
  41.9 2.2 gather_fusion.5
  45.8 1.9 reshape_reshape.41
  47.7 1.9 reshape_reshape.39
  51.2 2.8 reshape_reshape.46
  55.1 2.4 copy.394
  57.5 2.3 copy.395
  60.9 3.2 copy.412
  64.1 2.2 gather_fusion.2
  68.0 2.2 gather_fusion.10
  70.3 2.3 copy.400
  72.6 4.0 gather_fusion
  77.4 2.3 copy.467
  79.8 4.4 gather_fusion.7
  85.0 4.3 fusion.77
  96.6 2.4 select_bitcast_fusion
  99.0 5.5 fusion.78
  107.9 53.0 %all-gather.9.cloned.1.call-done = f32[12,512,64]{2,1,0:T(8,128)} async-done(((f32[12,64,64]{2,1,0:T(8,128)}), f32[12,512,64]{2,1,0:T(8,128)}) %all-gather.9.cloned.1.call-update) | async-done | bytes 1572880 | tf_op jit(solution)/shard_map/all_gather | solution.py:103
  160.9 4.8 fusion.8
  168.0 2.8 copy.449
  170.7 257.2 %all-gather.7.cloned.1.call-done = f32[12,1024,64]{2,1,0:T(8,128)} async-done(((f32[12,8,64]{2,1,0:T(8,128)}), f32[12,1024,64]{2,1,0:T(8,128)}) %all-gather.7.cloned.1.call-update) | async-done | bytes 3145744 | tf_op jit(solution)/shard_map/all_gather | solution.py:106
  427.9 7.6 fusion.79
  444.4 7.2 gather_fusion.6
  452.5 242.9 %all-gather.11.cloned.1.call-done = f32[12,1024,64]{2,1,0:T(8,128)} async-done(((f32[12,8,64]{2,1,0:T(8,128)}), f32[12,1024,64]{2,1,0:T(8,128)}) %all-gather.11.cloned.1.call-update) | async-done | bytes 3145744 | tf_op jit(solution)/shard_map/all_gather | solution.py:107
  695.4 5.3 convolution_bitcast_fusion.2
  702.6 2.7 copy.450
  705.5 5.4 fusion.18
  713.1 6.6 gather_fusion.8
  720.7 6.0 multiply_multiply_fusion.1
  728.0 6.8 fusion.25
  734.9 8.5 fusion.7
  746.5 2.1 gather_fusion.11
  751.7 7.3 fusion.10
  759.8 11.9 fusion.45
  772.7 12.9 fusion.22
  787.1 1.9 copy.434
  790.4 1.9 copy.428
  795.3 2.5 broadcast_in_dim.383.clone
  797.8 2.7 broadcast_in_dim.384
  801.2 4.5 convolution_bitcast_fusion
  807.6 3.0 broadcast_in_dim.419
  810.9 4.7 multiply_multiply_fusion
  817.3 3.1 fusion.80
  820.4 2.3 copy.476
  822.6 6.2 fusion.81
  828.8 2.3 copy.495
  831.1 5.1 convolution_bitcast_fusion.1
  837.8 3.0 broadcast_in_dim.426
  840.8 5.5 fusion.2
  846.3 2.3 copy.503
  848.6 2.3 copy.419
  860.3 36.5 %reduce-scatter.9.cloned.1.call-done = f32[12,64,64]{2,1,0:T(8,128)} async-done(((f32[12,512,64]{2,1,0:T(8,128)}), f32[12,64,64]{2,1,0:T(8,128)}) %reduce-scatter.9.cloned.1.call-update) | async-done | bytes 196624 | tf_op jit(solution)/shard_map/reduce_scatter | solution.py:180
  899.6 648.3 %reduce-scatter.7.cloned.1.call-done = f32[12,8,64]{2,1,0:T(8,128)} async-done(((f32[12,1024,64]{2,1,0:T(8,128)}), f32[12,8,64]{2,1,0:T(8,128)}) %reduce-scatter.7.cloned.1.call-update) | async-done | bytes 24592 | tf_op jit(solution)/shard_map/reduce_scatter | solution.py:183
  1550.3 642.8 %reduce-scatter.11.cloned.1.call-done = f32[12,8,64]{2,1,0:T(8,128)} async-done(((f32[12,1024,64]{2,1,0:T(8,128)}), f32[12,8,64]{2,1,0:T(8,128)}) %reduce-scatter.11.cloned.1.call-update) | async-done | bytes 24592 | tf_op jit(solution)/shard_map/reduce_scatter | solution.py:184
  2195.5 6.8 select_add_fusion
  (321 shorter events, 82.1 us)
Async XLA Ops:
  7.2 91.8 %all-gather.5.cloned.1.call-start = ((), (), s32[]{:S(2)}) async-start(), calls=%async_computation.4 | async-start | bytes 3538944 | tf_op jit(solution)/shard_map/all_gather | solution.py:102
  8.0 26.7 %copy-start.73 = (s32[12]{0:T(128)}, s32[12]{0:T(128)S(1)}, u32[]{:S(2)}) copy-start(s32[12]{0:T(128)S(1)} %get-tuple-element.35) | copy-start | bytes 148
  10.7 5.5 copy-start.77
  16.2 4.9 copy-start.8
  25.1 7.2 copy-start.7
  31.6 129.4 %all-gather.9.cloned.1.call-start = ((), (), s32[]{:S(2)}) async-start(), calls=%async_computation.6 | async-start | bytes 3538944 | tf_op jit(solution)/shard_map/all_gather | solution.py:103
  32.3 395.6 %all-gather.7.cloned.1.call-start = ((), (), s32[]{:S(2)}) async-start(), calls=%async_computation.5 | async-start | bytes 6340608 | tf_op jit(solution)/shard_map/all_gather | solution.py:106
  38.1 6.1 copy-start.74
  38.1 7.8 copy-start.6
  45.0 650.4 %all-gather.11.cloned.1.call-start = ((), (), s32[]{:S(2)}) async-start(), calls=%async_computation.7 | async-start | bytes 6340608 | tf_op jit(solution)/shard_map/all_gather | solution.py:107
  45.6 811.9 %reduce-scatter.5.cloned.1.call-start = ((), (), s32[]{:S(2)}) async-start(), calls=%async_computation.8 | async-start | bytes 3538944 | tf_op jit(solution)/shard_map/reduce_scatter | solution.py:179
  55.1 4.7 copy-start.9
  89.3 9.6 copy-start.18
  89.4 4.3 copy-start.71
  89.8 14.7 copy-start.27
  92.2 12.4 copy-start.65
  94.4 10.2 copy-start.82
  104.6 61.2 %copy-start.41 = (f32[12,64]{1,0:T(8,128)}, f32[12,64]{1,0:T(8,128)S(1)}, u32[]{:S(2)}) copy-start(f32[12,64]{1,0:T(8,128)S(1)} %get-tuple-element.40) | copy-start | bytes 9220
  106.4 61.6 %copy-start.33 = (f32[64,12]{1,0:T(8,128)}, f32[64,12]{1,0:T(8,128)S(1)}, u32[]{:S(2)}) copy-start(f32[64,12]{1,0:T(8,128)S(1)} %copy.436) | copy-start | bytes 9220
  107.2 60.8 %copy-start.35 = (f32[64,12]{1,0:T(8,128)}, f32[64,12]{1,0:T(8,128)S(1)}, u32[]{:S(2)}) copy-start(f32[64,12]{1,0:T(8,128)S(1)} %copy.407) | copy-start | bytes 9220
  435.5 6.4 copy-start.3
  435.5 259.9 %copy-start.31 = (f32[12,8]{1,0:T(8,128)}, f32[12,8]{1,0:T(8,128)S(1)}, u32[]{:S(2)}) copy-start(f32[12,8]{1,0:T(8,128)S(1)} %get-tuple-element.42) | copy-start | bytes 1156
  444.4 7.9 copy-start.63
  444.4 8.0 copy-start.61
  701.3 4.1 copy-start.58
  701.3 4.1 copy-start.59
  701.3 4.1 copy-start.60
  705.4 5.4 copy-start.46
  705.4 5.4 copy-start.48
  705.4 5.4 copy-start.50
  705.5 5.4 copy-start.52
  713.1 6.7 copy-start.72
  720.7 7.2 copy-start.14
  734.8 8.7 copy-start.29
  734.8 9.4 copy-start.20
  734.8 10.0 copy-start.34
  734.8 10.0 copy-start.36
  734.8 10.0 copy-start.83
  734.8 162.0 %reduce-scatter.9.cloned.1.call-start = ((), (), s32[]{:S(2)}) async-start(), calls=%async_computation.10 | async-start | bytes 3538944 | tf_op jit(solution)/shard_map/reduce_scatter | solution.py:180
  743.4 5.4 copy-start.32
  743.4 5.4 copy-start.54
  743.4 5.3 copy-start.68
  743.4 804.5 %reduce-scatter.7.cloned.1.call-start = ((), (), s32[]{:S(2)}) async-start(), calls=%async_computation.9 | async-start | bytes 6340608 | tf_op jit(solution)/shard_map/reduce_scatter | solution.py:183
  744.9 6.5 copy-start.17
  751.6 7.4 copy-start.55
  751.7 8.1 copy-start.26
  771.7 1421.4 %reduce-scatter.11.cloned.1.call-start = ((), (), s32[]{:S(2)}) async-start(), calls=%async_computation.11 | async-start | bytes 6340608 | tf_op jit(solution)/shard_map/reduce_scatter | solution.py:184
  785.6 6.6 copy-start.13
  793.3 7.2 copy-start.24
  805.7 4.8 copy-start.62
  805.7 4.8 copy-start.64
  805.7 4.8 copy-start.66
  806.0 4.8 copy-start.30
  806.0 4.8 copy-start.39
  810.8 4.8 copy-start.44
  810.8 6.4 copy-start.5
  822.6 8.4 copy-start.11
  836.2 4.5 copy-start.45
  840.8 10.2 copy-start.53
  846.3 5.9 copy-start.51
  848.6 4.8 copy-start.49
  1550.3 645.2 %copy-start.15 = (f32[256,768]{1,0:T(8,128)S(1)}, f32[256,768]{1,0:T(8,128)}, u32[]{:S(2)}) copy-start(f32[256,768]{1,0:T(8,128)} %copy.476) | copy-start | bytes 2359300
  1550.3 645.2 %copy-start.21 = (pred[256,768]{1,0:T(8,128)(4,1)S(1)}, pred[256,768]{1,0:T(8,128)(4,1)}, u32[]{:S(2)}) copy-start(pred[256,768]{1,0:T(8,128)(4,1)} %copy.434) | copy-start | bytes 589828
  1550.3 645.2 %copy-start.22 = (pred[256,768]{1,0:T(8,128)(4,1)S(1)}, pred[256,768]{1,0:T(8,128)(4,1)}, u32[]{:S(2)}) copy-start(pred[256,768]{1,0:T(8,128)(4,1)} %copy.428) | copy-start | bytes 589828
  (28 other events, 61.5 us)
Sparse Core Ops, SparseCore 0:
  31.7 65.5 all-gather.4
  99.6 61.3 all-gather.8
  162.6 265.3 all-gather.6
  429.4 265.9 all-gather.10
  734.9 79.0 reduce-scatter.4
  818.3 78.4 reduce-scatter.8
  899.2 648.7 reduce-scatter.6
  1550.4 642.6 reduce-scatter.10
where the time goes:
time: 2220 us; the launch traced here: 2210 us
  waiting for transfers between devices  1880 us (85%)
  local copies, waits for them, and re-layouts  174 us (8%)
  matrix products  115 us (5%)
    reduce_scatter x1, waiting for transfers between devices, body(): lax.psum_scatter(grad_k_three, ('seg', 'blk'), scatter_dimension=1, tiled...  648 us
    reduce_scatter x1, waiting for transfers between devices, body(): lax.psum_scatter(grad_v_three, ('seg', 'blk'), scatter_dimension=1, tiled...  643 us
    all_gather x1, waiting for transfers between devices, body(): lax.all_gather(key_three, ('seg', 'blk'), axis=1, tiled=True)  257 us
    all_gather x1, waiting for transfers between devices, body(): lax.all_gather(value_three, ('seg', 'blk'), axis=1, tiled=True)  243 us
    all_gather x1, waiting for transfers between devices, body(): lax.all_gather(value_two, 'blk', axis=1, tiled=True)  53 us
    gather x27, local copies, waits for them, and re-layouts, pick_rows(): jnp.take_along_axis(parts, index, axis=1)[:, 0]  46.5 us
    broadcast_in_dim x43, local copies, waits for them, and re-layouts, spread_rows(): full = jnp.where(hits, jnp.transpose(source, (1, 0, 2))[:, None], fill)  45.8 us
  transfers between devices with their start and end apart: 8, of which 6 were waited for; matrix products, arithmetic and copies ran while one was open for 10% of the time, Pallas kernels for 0%

commit v1 on v0

v1 whole, which is shorter than its diff:
```python
import functools

import jax
import jax.numpy as jnp
from jax import lax
from jax.experimental import pallas as pl
from jax.experimental.pallas import tpu as pltpu
from jax.sharding import PartitionSpec as P

HEADS = 12
HD = 64
ROWS = 256
LIVE2 = 64
LIVE3 = 8
R2 = 4
R3 = 32
NEG = -1e30
SCALE = HD**-0.5
BF = jnp.bfloat16
F32 = jnp.float32
ALL = ("seg", "blk")
SEG_AT, BLK_AT = 24, 25
L1_AT, L2_AT, L3_AT, OWN_AT = 0, 16, 32, 48


def nt(a, b):
    return lax.dot_general(a, b, (((1,), (1,)), ((), ())), preferred_element_type=F32)


def nn(a, b):
    return lax.dot_general(a, b, (((1,), (0,)), ((), ())), preferred_element_type=F32)


def tn(a, b):
    return lax.dot_general(a, b, (((0,), (0,)), ((), ())), preferred_element_type=F32)


def exact(a, b, dims=((1,), (0,))):
    return lax.dot_general(
        a, b, (dims, ((), ())), preferred_element_type=F32, precision=lax.Precision.HIGHEST
    )


def iota(shape, axis):
    return lax.broadcasted_iota(jnp.int32, shape, axis)


def split2(x):
    first = x.astype(BF)
    return first, (x - first.astype(F32)).astype(BF)


def split3(x):
    first = x.astype(BF)
    rest = x - first.astype(F32)
    second = rest.astype(BF)
    return first, second, (rest - second.astype(F32)).astype(BF)


def cat(parts):
    return jnp.concatenate(parts, axis=1)


def pack_kq(k, q):
    k0, k1, k2 = split3(k)
    q0, q1, q2 = split3(q * SCALE)
    return cat([k0, k1, k0, k1, k0, k2]), cat([q0, q1, q1, q0, q2, q0])


def pack_vd(v, d):
    v0, v1 = split2(v)
    d0, d1 = split2(d)
    return cat([v0, v1, v0, v1]), cat([d0, d1, d1, d0])


def forward_core(ak, bq, av, bd, mask):
    s = jnp.where(mask, nt(ak, bq), NEG)
    dp = nt(av, bd)
    top = jnp.max(s, axis=0, keepdims=True)
    p = jnp.exp(s - top)
    total = jnp.sum(p, axis=0, keepdims=True)
    cross = jnp.sum(p * dp, axis=0, keepdims=True)
    return top + jnp.log(total), cross / total


def backward_core(ak, bq, av, bd, mask, lse, delta):
    p = jnp.exp(jnp.where(mask, nt(ak, bq), NEG) - lse)
    g = p * (nt(av, bd) - delta)
    p0, p1 = split2(p)
    g0, g1 = split2(g)
    d01, q01, v01, k01 = bd[:, :128], bq[:, :128], av[:, :128], ak[:, :128]
    dv = nn(p0, d01) + nn(p1, d01)
    dk = nn(g0, q01) + nn(g1, q01)
    at = tn(v01, p0) + tn(v01, p1)
    qt = tn(k01, g0) + tn(k01, g1)
    return dv, dk, at[:HD] + at[HD:], (qt[:HD] + qt[HD:]) * SCALE


def fold(x):
    return x + pltpu.roll(x, HD, 1)


def half_mask(rows):
    return iota((rows, 128), 1) < HD


def both(a, b):
    return jnp.where(half_mask(a.shape[0]), a, b)


def head_column(meta, base, shape):
    rows = iota(shape, 0)
    out = jnp.zeros(shape, jnp.int32)
    for h in range(HEADS):
        out = jnp.where(rows == h, meta[base + h], out)
    return out


def merge(levels):
    top = functools.reduce(jnp.maximum, [lse for lse, _ in levels])
    weights = [jnp.exp(lse - top) for lse, _ in levels]
    total = functools.reduce(jnp.add, weights)
    delta = functools.reduce(jnp.add, [w * d for w, (_, d) in zip(weights, levels)])
    return top + jnp.log(total), delta / total


def pick_kernel(meta, q, k, v, d, send2, send3, panel):
    for a, ref in enumerate((q, k, v, d)):
        for b in range(6):
            base = ROWS * (6 * a + b)
            panel[base : base + ROWS, :] = ref[:, 128 * b : 128 * b + 128]
            even = panel[pl.ds(base + meta[2 * b], LIVE2, stride=R2), :]
            odd = panel[pl.ds(base + meta[2 * b + 1], LIVE2, stride=R2), :]
            send2[b * 256 + a * LIVE2 : b * 256 + (a + 1) * LIVE2, :] = both(even, odd)
    for h in range(HEADS):
        take = [
            panel[pl.ds(ROWS * (6 * a + h // 2) + meta[HEADS + h], LIVE3, stride=R3), :]
            for a in range(4)
        ]
        if h % 2 == 0:
            take[2], take[3] = pltpu.roll(take[2], HD, 1), pltpu.roll(take[3], HD, 1)
        else:
            take[0], take[1] = pltpu.roll(take[0], HD, 1), pltpu.roll(take[1], HD, 1)
        kv = both(take[1], take[2])
        qd = both(take[0], take[3])
        for r in range(LIVE3):
            send3[72 * h + 9 * r : 72 * h + 9 * r + 8, :] = kv
        send3[pl.ds(72 * h + 8, LIVE3, stride=9), :] = qd


def pair_rows(shape, e, head_axis, pair_axis):
    return (iota(shape, head_axis) == 2 * iota(shape, pair_axis) + e).astype(F32)


def local_forward_kernel(meta, q, k, v, d, stats, near, small):
    stats[...] = jnp.zeros_like(stats)
    mask = iota((ROWS, ROWS), 0) <= iota((ROWS, ROWS), 1)

    def step(i, carry):
        cols = pl.ds(pl.multiple_of(i * 128, 128), 128)
        qp, kp, vp, dp = q[:, cols], k[:, cols], v[:, cols], d[:, cols]
        for e in range(2):
            at = slice(HD * e, HD * e + HD)
            ak, bq = pack_kq(kp[:, at], qp[:, at])
            av, bd = pack_vd(vp[:, at], dp[:, at])
            lse, delta = forward_core(ak, bq, av, bd, mask)
            stats[pl.ds(2 * i + e, 1), :ROWS] = lse
            stats[pl.ds(2 * i + e, 1), ROWS:] = delta
        return carry

    lax.fori_loop(0, 6, step, 0)
    shift2 = head_column(meta, 0, (16, ROWS))
    shift3 = head_column(meta, HEADS, (16, ROWS))
    row = iota((16, ROWS), 1)
    live2 = row % R2 == shift2
    live3 = row % R3 == shift3
    to_near = (iota((ROWS, 128), 0) // R2 == iota((ROWS, 128), 1) % LIVE2).astype(F32)
    far = jnp.zeros((16, 128), F32)
    for n in range(2):
        x = stats[:, ROWS * n : ROWS * n + ROWS]
        y = exact(jnp.where(live2, x, 0.0), to_near)
        even = exact(pair_rows((8, 16), 0, 1, 0), y)
        odd = exact(pair_rows((8, 16), 1, 1, 0), y)
        near[:, 128 * n : 128 * n + 128] = both(even, odd)
        place = (iota((ROWS, 128), 0) // R3 + L1_AT + 8 * n == iota((ROWS, 128), 1)).astype(F32)
        far = far + exact(jnp.where(live3, x, 0.0), place)
    rows_of = (iota((128, 16), 0) // 8 == iota((128, 16), 1)).astype(F32)
    small[...] = exact(rows_of, far)


def stack2(ref, a):
    return jnp.concatenate(
        [ref[b * 256 + a * LIVE2 : b * 256 + (a + 1) * LIVE2, :] for b in range(8)], axis=0
    )


def near_shift(meta, e):
    h = jnp.minimum(2 * meta[BLK_AT] + e, HEADS - 1)
    live = meta[HEADS + h] % R2 == meta[h]
    return live, meta[HEADS + h] // R2


def to_rows(x):
    return jnp.concatenate([x[:, HD * b : HD * b + HD] for b in range(8)], axis=0)


def near_forward_kernel(meta, got, own, small):
    qs, ks, vs, ds = [stack2(got, a) for a in range(4)]
    packs = []
    for e in range(2):
        at = slice(HD * e, HD * e + HD)
        ak, bq = pack_kq(ks[:, at], qs[:, at])
        av, bd = pack_vd(vs[:, at], ds[:, at])
        lses, deltas = [], []
        for j in range(2):
            keys = 256 * (j + 1)
            mask = iota((keys, 256), 0) <= iota((keys, 256), 1) + 256 * j
            lse, delta = forward_core(
                ak[:keys],
                bq[256 * j : 256 * j + 256],
                av[:keys],
                bd[256 * j : 256 * j + 256],
                mask,
            )
            lses.append(lse)
            deltas.append(delta)
        packs.append((to_rows(cat(lses)), to_rows(cat(deltas))))
    active = meta[BLK_AT] < 6
    lse = jnp.where(active, cat([packs[0][0], packs[1][0]]), 0.0)
    delta = jnp.where(active, cat([packs[0][1], packs[1][1]]), 0.0)
    own[:, :128] = lse
    own[:, 128:] = delta
    out = jnp.zeros((128, 128), F32)
    head = iota((128, 128), 0) // 8
    lane = iota((128, 128), 1)
    r, l = iota((8, 128), 0), iota((8, 128), 1)
    for e in range(2):
        live, shift = near_shift(meta, e)
        pick = ((l // HD == e) & (l % HD // 8 == r) & (l % 8 == shift)).astype(F32)
        total = jnp.zeros((8, 128), F32)
        for n, x in enumerate((lse, delta)):
            place = (l == L2_AT + 8 * n + r).astype(F32)
            total = total + exact(exact(pick, x, ((1,), (1,))), place)
        full = jnp.concatenate([total] * 16, axis=0)
        dead = jnp.where(lane < L2_AT + 8, NEG, 0.0)
        full = jnp.where(live, full, dead)
        here = (head == 2 * meta[BLK_AT] + e) & (lane >= L2_AT) & (lane < L2_AT + 16)
        out = out + jnp.where(here, full, 0.0)
    small[...] = out


def far_operands(meta, got):
    kv = jnp.concatenate([got[pl.ds(j, 128, stride=9), :] for j in range(8)], axis=0)
    qd = got[pl.ds(8, 128, stride=9), :]
    ak, bq = pack_kq(kv[:, :HD], qd[:, :HD])
    av, bd = pack_vd(kv[:, HD:], qd[:, HD:])
    key, query = iota((1024, 128), 0), iota((1024, 128), 1)
    mask = (key % 128) * 8 + key // 128 <= query * 8 + meta[BLK_AT]
    return ak, bq, av, bd, mask


def far_forward_kernel(meta, got, near1, small1, near2, small2, own, send):
    lse, delta = forward_core(*far_operands(meta, got))
    active = meta[SEG_AT] < HEADS
    lse = jnp.where(active, lse, 0.0)
    delta = jnp.where(active, delta, 0.0)
    own[0:1, :] = lse
    own[1:2, :] = delta
    sub, lane = iota((128, 128), 0), iota((128, 128), 1)
    out = small1[...] + small2[...]
    for n, x in enumerate((lse, delta)):
        column = jnp.sum(jnp.where(sub == lane, x, 0.0), axis=1, keepdims=True)
        out = out + jnp.where(lane == OWN_AT + n, column, 0.0)
        place = (lane == L3_AT + 8 * n + sub % 8).astype(F32)
        out = out + exact(jnp.where(sub // 8 == lane // 8, x, 0.0), place)
    for n in range(2):
        cols = slice(128 * n, 128 * n + 128)
        send[pl.ds(n, 128, stride=5), :] = jnp.concatenate([near1[:, cols]] * 16, axis=0)
        send[pl.ds(2 + n, 128, stride=5), :] = jnp.concatenate([near2[:, cols]] * 16, axis=0)
    send[pl.ds(4, 128, stride=5), :] = out


def far_backward_kernel(meta, got, own, stats, send):
    small = stats[pl.ds(4, 128, stride=5), :]
    sub, lane = iota((128, 128), 0), iota((128, 128), 1)
    r8, l8 = iota((8, 128), 0), iota((8, 128), 1)
    picks = ((l8 == L1_AT + 8 * r8 + meta[BLK_AT]) & (r8 < 2)).astype(F32)
    first = exact(picks, small, ((1,), (1,)))
    here = sub == 8 * (lane // 8) + meta[SEG_AT] // 2
    second = []
    for n in range(2):
        place = (sub == L2_AT + 8 * n + lane % 8).astype(F32)
        spread = exact(small, place)
        second.append(jnp.sum(jnp.where(here, spread, 0.0), axis=0, keepdims=True))
    lse, delta = merge(
        [(first[0:1], first[1:2]), (second[0], second[1]), (own[0:1, :], own[1:2, :])]
    )
    ak, bq, av, bd, mask = far_operands(meta, got)
    dv, dk, at, qt = backward_core(ak, bq, av, bd, mask, lse, delta)
    kv = both(fold(dk), fold(dv))
    for j in range(8):
        send[pl.ds(j, 128, stride=9), :] = kv[128 * j : 128 * j + 128]
    send[pl.ds(8, 128, stride=9), :] = jnp.concatenate([at, qt], axis=0).T


def near_backward_kernel(meta, got, own, stats, send):
    base = 40 * meta[SEG_AT]
    first = [stats[pl.ds(base + n, 8, stride=5), :] for n in range(2)]
    r, l = iota((8, 128), 0), iota((8, 128), 1)
    third = [jnp.zeros((8, 128), F32), jnp.zeros((8, 128), F32)]
    covered = jnp.zeros((8, 128), jnp.bool_)
    for e in range(2):
        live, shift = near_shift(meta, e)
        cover = (l // HD == e) & (l % 8 == shift) & live
        covered = covered | cover
        pick = (cover & (l % HD // 8 == r)).astype(F32)
        h = 2 * meta[BLK_AT] + e
        far = stats[pl.ds(40 * h + 4, 8, stride=5), :]
        for n in range(2):
            at = L3_AT + 8 * n
            third[n] = third[n] + exact(far[:, at : at + 8], pick, ((0,), (0,)))
    lse, delta = merge(
        [
            (first[0], first[1]),
            (own[:, :128], own[:, 128:]),
            (jnp.where(covered, third[0], NEG), jnp.where(covered, third[1], 0.0)),
        ]
    )
    qs, ks, vs, ds = [stack2(got, a) for a in range(4)]
    ats, qts, dks, dvs = [], [], [], []
    for e in range(2):
        at = slice(HD * e, HD * e + HD)
        ak, bq = pack_kq(ks[:, at], qs[:, at])
        av, bd = pack_vd(vs[:, at], ds[:, at])
        parts = []
        for j in range(2):
            keys = 256 * (j + 1)
            rows = slice(256 * j, 256 * j + 256)
            mask = iota((keys, 256), 0) <= iota((keys, 256), 1) + 256 * j
            lse_j = cat([lse[b : b + 1, at] for b in range(4 * j, 4 * j + 4)])
            delta_j = cat([delta[b : b + 1, at] for b in range(4 * j, 4 * j + 4)])
            parts.append(
                backward_core(ak[:keys], bq[rows], av[:keys], bd[rows], mask, lse_j, delta_j)
            )
        dvs.append(jnp.concatenate([parts[0][0] + parts[1][0][:256], parts[1][0][256:]], axis=0))
        dks.append(jnp.concatenate([parts[0][1] + parts[1][1][:256], parts[1][1][256:]], axis=0))
        ats.append(cat([parts[0][2], parts[1][2]]))
        qts.append(cat([parts[0][3], parts[1][3]]))
    results = (
        jnp.concatenate(ats, axis=0).T,
        jnp.concatenate(qts, axis=0).T,
        both(fold(dks[0]), fold(dks[1])),
        both(fold(dvs[0]), fold(dvs[1])),
    )
    for a, x in enumerate(results):
        for b in range(8):
            send[b * 256 + a * LIVE2 : b * 256 + (a + 1) * LIVE2, :] = x[LIVE2 * b : LIVE2 * b + LIVE2]


def local_backward_kernel(meta, q, k, v, d, own, stats, at_out, dq_out, dk_out, dv_out, joint):
    base = 40 * meta[SEG_AT]
    shift2 = head_column(meta, 0, (16, ROWS))
    shift3 = head_column(meta, HEADS, (16, ROWS))
    row = iota((16, ROWS), 1)
    live2 = row % R2 == shift2
    live3 = row % R3 == shift3
    small = stats[pl.ds(4, 128, stride=5), :]
    from_near = (iota((128, ROWS), 1) // R2 == iota((128, ROWS), 0) % LIVE2).astype(F32)
    group = (iota((16, 128), 0) == iota((16, 128), 1) // 8).astype(F32)
    spot = iota((128, ROWS), 0) % 8 == iota((128, ROWS), 1) // R3
    second, third = [], []
    for n in range(2):
        x = stats[pl.ds(base + 2 + n, 8, stride=5), :]
        halves = half_mask(16)
        y = jnp.where(halves, exact(pair_rows((16, 8), 0, 0, 1), x), 0.0)
        z = jnp.where(halves, 0.0, exact(pair_rows((16, 8), 1, 0, 1), x))
        second.append(jnp.where(live2, exact(y + z, from_near), 0.0 if n else NEG))
        column = jnp.where(spot, small[:, OWN_AT + n : OWN_AT + n + 1], 0.0)
        third.append(jnp.where(live3, exact(group, column), 0.0 if n else NEG))
    lse, delta = merge([(own[:, :ROWS], own[:, ROWS:]), tuple(second), tuple(third)])
    joint[:, :ROWS] = lse
    joint[:, ROWS:] = delta
    mask = iota((ROWS, ROWS), 0) <= iota((ROWS, ROWS), 1)

    def step(i, carry):
        cols = pl.ds(pl.multiple_of(i * 128, 128), 128)
        qp, kp, vp, dp = q[:, cols], k[:, cols], v[:, cols], d[:, cols]
        res = []
        for e in range(2):
            at = slice(HD * e, HD * e + HD)
            ak, bq = pack_kq(kp[:, at], qp[:, at])
            av, bd = pack_vd(vp[:, at], dp[:, at])
            lse_h = joint[pl.ds(2 * i + e, 1), :ROWS]
            delta_h = joint[pl.ds(2 * i + e, 1), ROWS:]
            res.append(backward_core(ak, bq, av, bd, mask, lse_h, delta_h))
        at_out[:, cols] = jnp.concatenate([res[0][2], res[1][2]], axis=0).T
        dq_out[:, cols] = jnp.concatenate([res[0][3], res[1][3]], axis=0).T
        dk_out[:, cols] = both(fold(res[0][1]), fold(res[1][1]))
        dv_out[:, cols] = both(fold(res[0][0]), fold(res[1][0]))
        return carry

    lax.fori_loop(0, 6, step, 0)


def combine_kernel(meta, at1, dq1, dk1, dv1, got2, got3, at_out, dq_out, dk_out, dv_out, panel):
    low = half_mask(LIVE2)
    for a, local in enumerate((at1, dq1, dk1, dv1)):
        for b in range(6):
            base = ROWS * (6 * a + b)
            panel[base : base + ROWS, :] = local[:, 128 * b : 128 * b + 128]
            x = got2[b * 256 + a * LIVE2 : b * 256 + (a + 1) * LIVE2, :]
            for e in range(2):
                rows = pl.ds(base + meta[2 * b + e], LIVE2, stride=R2)
                keep = low if e == 0 else ~low
                panel[rows, :] = panel[rows, :] + jnp.where(keep, x, 0.0)
    low = half_mask(LIVE3)
    for h in range(HEADS):
        kv = got3[72 * h : 72 * h + 8, :]
        for r in range(1, LIVE3):
            kv = kv + got3[72 * h + 9 * r : 72 * h + 9 * r + 8, :]
        aq = got3[pl.ds(72 * h + 8, LIVE3, stride=9), :]
        kv_turn, aq_turn = pltpu.roll(kv, HD, 1), pltpu.roll(aq, HD, 1)
        if h % 2 == 0:
            parts, keep = (aq, aq_turn, kv, kv_turn), low
        else:
            parts, keep = (aq_turn, aq, kv_turn, kv), ~low
        for a, x in enumerate(parts):
            rows = pl.ds(ROWS * (6 * a + h // 2) + meta[HEADS + h], LIVE3, stride=R3)
            panel[rows, :] = panel[rows, :] + jnp.where(keep, x, 0.0)
    for a, out in enumerate((at_out, dq_out, dk_out, dv_out)):
        for b in range(6):
            base = ROWS * (6 * a + b)
            out[:, 128 * b : 128 * b + 128] = panel[base : base + ROWS, :]


PANEL = [pltpu.VMEM((24 * ROWS, 128), F32)]


def call(kernel, name, outs, args, flops, scratch=()):
    specs = [pl.BlockSpec(memory_space=pltpu.SMEM)]
    specs += [pl.BlockSpec(memory_space=pltpu.VMEM)] * (len(args) - 1)
    return pl.pallas_call(
        kernel,
        name=name,
        out_shape=[jax.ShapeDtypeStruct(shape, F32) for shape in outs],
        in_specs=specs,
        out_specs=[pl.BlockSpec(memory_space=pltpu.VMEM)] * len(outs),
        scratch_shapes=list(scratch),
        compiler_params=pltpu.CompilerParams(vmem_limit_bytes=48 * 1024 * 1024),
        cost_estimate=pl.CostEstimate(flops=flops, bytes_accessed=4_000_000, transcendentals=0),
    )(*args)


def swap_near(x):
    return lax.all_to_all(x, "blk", 0, 0, tiled=True)


def swap_all(x):
    return lax.all_to_all(x.reshape(128, -1), ALL, 0, 0, tiled=True).reshape(-1, 128)


def body(q, k, v, d, offsets):
    place = jnp.stack([lax.axis_index("seg"), lax.axis_index("blk")]).astype(jnp.int32)
    meta = jnp.concatenate([offsets.reshape(-1), place])
    send2, send3 = call(pick_kernel, "pick", [(2048, 128), (1152, 128)], (meta, q, k, v, d), 10**9, PANEL)
    got2 = swap_near(send2)
    got3 = swap_all(send3)
    stats1, near1, small1 = call(
        local_forward_kernel,
        "local_forward",
        [(16, 2 * ROWS), (8, 256), (128, 128)],
        (meta, q, k, v, d),
        8 * 10**9,
    )
    near2, small2 = call(
        near_forward_kernel, "near_forward", [(8, 256), (128, 128)], (meta, got2), 4 * 10**9
    )
    own3, send_stats = call(
        far_forward_kernel,
        "far_forward",
        [(8, 128), (640, 128)],
        (meta, got3, near1, small1, near2, small2),
        2 * 10**9,
    )
    stats = swap_all(send_stats)
    (back3,) = call(
        far_backward_kernel, "far_backward", [(1152, 128)], (meta, got3, own3, stats), 3 * 10**9
    )
    home3 = swap_all(back3)
    (back2,) = call(
        near_backward_kernel, "near_backward", [(2048, 128)], (meta, got2, near2, stats), 8 * 10**9
    )
    home2 = swap_near(back2)
    full = [(ROWS, HEADS * HD)] * 4
    local = call(
        local_backward_kernel,
        "local_backward",
        full,
        (meta, q, k, v, d, stats1, stats),
        14 * 10**9,
        scratch=[pltpu.VMEM((16, 2 * ROWS), F32)],
    )
    return tuple(call(combine_kernel, "combine", full, (meta, *local, home2, home3), 2 * 10**9, PANEL))


def solution(mesh):
    rows = P(ALL, None)
    return jax.shard_map(
        body,
        mesh=mesh,
        in_specs=(rows, rows, rows, rows, P()),
        out_specs=(rows, rows, rows, rows),
        check_vma=False,
    )
```

time: 2220 us -> 123 us (0.06)
  waiting for transfers between devices: 1880 us -> 15.3 us
  local copies, waits for them, and re-layouts: 174 us -> 18.1 us
  matrix products: 115 us -> 0 us
  blocking collectives: 0 us -> 42.1 us
  Pallas kernels: 0 us -> 30.8 us
    reduce_scatter x4 -> x0, waiting for transfers between devices: 1330 us -> none  [the longest x1 648 us: body(): lax.psum_scatter(grad_k_three, ('seg', 'blk'), scatter_dimension=1, tiled...]
    all_gather x4 -> x0, waiting for transfers between devices: 553 us -> none  [the longest x1 257 us: body(): lax.all_gather(key_three, ('seg', 'blk'), axis=1, tiled=True)]
    dot_general x18 -> x0, matrix products: 115 us -> none  [the longest x3 26.9 us: backward_block(): jnp.einsum('txf,txs->tfs', attention_weights, gradient_rows, precision=EX...]
    gather x27 -> x0, local copies, waits for them, and re-layouts: 46.5 us -> none  [pick_rows(): jnp.take_along_axis(parts, index, axis=1)[:, 0]]
    broadcast_in_dim x43 -> x0, local copies, waits for them, and re-layouts: 45.8 us -> none  [spread_rows(): full = jnp.where(hits, jnp.transpose(source, (1, 0, 2))[:, None], fill)]
    all_to_all x0 -> x2, blocking collectives: none -> 42.1 us  [the longest x1 24.8 us: swap_near(): return lax.all_to_all(x, 'blk', 0, 0, tiled=True)]
    another operation x22 -> x0, local copies, waits for them, and re-layouts: 35.5 us -> none  [the longest x17 35.4 us: pick_rows(): parts = source.reshape(count, stride, source.shape[1], source.shape[2])]
    pallas_call x0 -> x8, Pallas kernels: none -> 30.8 us  [call(): pl.pallas_call(kernel, name=name, out_shape=[jax.ShapeDtypeStruct(shape,...]
  transfers between devices with their start and end apart: 8 -> 3, of which waited for: 6 -> 3; matrix products, arithmetic and copies ran while one was open for 10% -> 0% of each run, Pallas kernels for 0% -> 17%
where the time goes in v1:
time: 123 us; the launch traced here: 122 us
  blocking collectives  42.1 us (34%)
  Pallas kernels  30.8 us (25%)
  local copies, waits for them, and re-layouts  18.1 us (15%)
  waiting for transfers between devices  15.3 us (12%)
  starting transfers between devices  14.6 us (12%)
    pallas_call x8, Pallas kernels, call(): pl.pallas_call(kernel, name=name, out_shape=[jax.ShapeDtypeStruct(shape,...  30.8 us
    all_to_all x1, blocking collectives, swap_near(): return lax.all_to_all(x, 'blk', 0, 0, tiled=True)  24.8 us
    unnamed x40, local copies, waits for them, and re-layouts  18 us
    all_to_all x1, blocking collectives, swap_all(): lax.all_to_all(x.reshape(128, -1), ALL, 0, 0, tiled=True).reshape(-1, 128)  17.3 us
    all_to_all x2, waiting for transfers between devices, swap_all(): lax.all_to_all(x.reshape(128, -1), ALL, 0, 0, tiled=True).reshape(-1, 128)  12.7 us
    all_to_all x2, starting transfers between devices, swap_all(): lax.all_to_all(x.reshape(128, -1), ALL, 0, 0, tiled=True).reshape(-1, 128)  10.9 us
    all_to_all x1, starting transfers between devices, swap_near(): return lax.all_to_all(x, 'blk', 0, 0, tiled=True)  3.74 us
    all_to_all x1, waiting for transfers between devices, swap_near(): return lax.all_to_all(x, 'blk', 0, 0, tiled=True)  2.58 us
  transfers between devices with their start and end apart: 3, of which 3 were waited for; matrix products, arithmetic and copies ran while one was open for 0% of the time, Pallas kernels for 17%

profile of v1, /device:TPU:0, one launch (start us, length us, event | category | flops | bytes accessed | tf_op | source)
XLA Modules:
  0.0 121.8 jit_solution(15514240971834600335)
XLA Ops:
  0.6 0.0 copy-start.19
  0.6 0.7 copy-done.19
  1.3 0.1 reshape.39
  1.4 0.1 pad_add_fusion.meta
  1.5 0.0 copy-start
  1.5 1.1 copy-done
  2.6 0.0 copy-start.2
  2.6 1.1 copy-done.2
  3.7 0.0 copy-start.4
  3.7 1.1 copy-done.4
  4.9 0.0 copy-start.7
  4.9 1.1 copy-done.7
  6.0 2.1 %pick.1 = (f32[2048,128]{1,0:T(8,128)S(1)}, f32[1152,128]{1,0:T(8,128)}) custom-call(s32[26]{0:T(128)S(1)} %pad_add_fusion.meta, f32[256,768]{1,0:T(8,128)S(1)} %copy-done, f32[256,768]{1,0:T(8,128)S(1)} %copy-done.2, f32[256,768]{1,0:T(8,128)S(1)} %copy-done.4, f32[256,768]{1,0:T(8,128)S(1)} %copy-done.7), custom_call_target="tpu_custom_call" | custom-call | flops 1000000000 | bytes 4000000 | tf_op jit(solution)/shard_map/pick/pallas_call | solution.py:442
  8.1 0.0 copy-start.3
  8.1 24.8 %all_to_all.49 = f32[8,256,128]{2,1,0:T(8,128)S(1)} all-to-all(f32[8,256,128]{2,1,0:T(8,128)S(1)} %bitcast.15), channel_id=1, replica_groups=mesh['seg'=16,'blk'=8] {'blk'}, dimensions={0} | all-to-all | bytes 2097152 | tf_op jit(solution)/shard_map/all_to_all | solution.py:455
  32.9 0.0 copy-start.1
  32.9 6.3 %all-to-all-start = ((f32[128,1,1152]{2,1,0:T(1,128)}), f32[128,1,1152]{2,1,0:T(1,128)S(1)}, u32[]{:S(2)}, u32[]{:S(2)}) async-start(f32[128,1,1152]{2,1,0:T(1,128)} %bitcast.2), calls=%async_computation | async-start | bytes 1179648 | tf_op jit(solution)/shard_map/all_to_all | solution.py:459
  39.2 0.0 copy-done.3
  39.2 0.0 copy-done.1
  39.2 0.0 copy-start.5
  39.2 1.1 copy-done.5
  40.3 0.0 copy-start.8
  40.3 1.1 copy-done.8
  41.5 4.8 %local_forward.1 = (f32[16,512]{1,0:T(8,128)S(1)}, f32[8,256]{1,0:T(8,128)S(1)}, f32[128,128]{1,0:T(8,128)S(1)}) custom-call(s32[26]{0:T(128)S(1)} %pad_add_fusion.meta, f32[256,768]{1,0:T(8,128)S(1)} %copy-done.1, f32[256,768]{1,0:T(8,128)S(1)} %copy-done.3, f32[256,768]{1,0:T(8,128)S(1)} %copy-done.5, f32[256,768]{1,0:T(8,128)S(1)} %copy-done.8), custom_call_target="tpu_custom_call" | custom-call | flops 8000000000 | bytes 4000000 | tf_op jit(solution)/shard_map/local_forward/pallas_call | solution.py:442
  46.3 0.0 copy-start.17
  46.3 0.6 copy-done.17
  46.9 2.3 %near_forward.1 = (f32[8,256]{1,0:T(8,128)S(1)}, f32[128,128]{1,0:T(8,128)S(1)}) custom-call(s32[26]{0:T(128)S(1)} %pad_add_fusion.meta, f32[2048,128]{1,0:T(8,128)S(1)} %bitcast.12), custom_call_target="tpu_custom_call" | custom-call | flops 4000000000 | bytes 4000000 | tf_op jit(solution)/shard_map/near_forward/pallas_call | solution.py:442
  49.2 3.6 %all-to-all-done = f32[128,1,1152]{2,1,0:T(1,128)S(1)} async-done(((f32[128,1,1152]{2,1,0:T(1,128)}), f32[128,1,1152]{2,1,0:T(1,128)S(1)}, u32[]{:S(2)}, u32[]{:S(2)}) %all-to-all-start) | async-done | bytes 589856 | tf_op jit(solution)/shard_map/all_to_all | solution.py:459
  52.9 1.5 %far_forward.1 = (f32[8,128]{1,0:T(8,128)S(1)}, f32[640,128]{1,0:T(8,128)S(1)}) custom-call(s32[26]{0:T(128)S(1)} %pad_add_fusion.meta, f32[1152,128]{1,0:T(8,128)S(1)} %bitcast.17, f32[8,256]{1,0:T(8,128)S(1)} %get-tuple-element.19.near1, f32[128,128]{1,0:T(8,128)S(1)} %get-tuple-element.20.small1, f32[8,256]{1,0:T(8,128)S(1)} %get-tuple-element.22.near2.own, ...), custom_call_target="tpu_custom_call" | custom-call | flops 2000000000 | bytes 4000000 | tf_op jit(solution)/shard_map/far_forward/pallas_call | solution.py:442
  54.4 17.3 %all_to_all.50 = f32[128,1,640]{2,1,0:T(1,128)S(1)} all-to-all(f32[128,1,640]{2,1,0:T(1,128)S(1)} %bitcast.22), channel_id=1, replica_groups=mesh['seg'=16,'blk'=8] {'seg','blk'}, dimensions={0} | all-to-all | bytes 655360 | tf_op jit(solution)/shard_map/all_to_all | solution.py:459
  71.7 2.7 %far_backward.1 = f32[1152,128]{1,0:T(8,128)} custom-call(s32[26]{0:T(128)S(1)} %pad_add_fusion.meta, f32[1152,128]{1,0:T(8,128)S(1)} %bitcast.18, f32[8,128]{1,0:T(8,128)S(1)} %get-tuple-element.29.own, f32[640,128]{1,0:T(8,128)S(1)} %bitcast.19), custom_call_target="tpu_custom_call" | custom-call | flops 3000000000 | bytes 4000000 | tf_op jit(solution)/shard_map/far_backward/pallas_call | solution.py:442
  74.4 4.6 %all-to-all-start.4 = ((f32[128,1,1152]{2,1,0:T(1,128)}), f32[128,1,1152]{2,1,0:T(1,128)S(1)}, u32[]{:S(2)}, u32[]{:S(2)}) async-start(f32[128,1,1152]{2,1,0:T(1,128)} %bitcast.10), calls=%async_computation.4 | async-start | bytes 1179648 | tf_op jit(solution)/shard_map/all_to_all | solution.py:459
  79.0 4.6 %near_backward.1 = f32[2048,128]{1,0:T(8,128)} custom-call(s32[26]{0:T(128)S(1)} %pad_add_fusion.meta, f32[2048,128]{1,0:T(8,128)S(1)} %bitcast.13, f32[8,256]{1,0:T(8,128)S(1)} %get-tuple-element.22.near2.own, f32[640,128]{1,0:T(8,128)S(1)} %bitcast.20), custom_call_target="tpu_custom_call" | custom-call | flops 8000000000 | bytes 4000000 | tf_op jit(solution)/shard_map/near_backward/pallas_call | solution.py:442
  83.6 9.1 %all-to-all-done.4 = f32[128,1,1152]{2,1,0:T(1,128)S(1)} async-done(((f32[128,1,1152]{2,1,0:T(1,128)}), f32[128,1,1152]{2,1,0:T(1,128)S(1)}, u32[]{:S(2)}, u32[]{:S(2)}) %all-to-all-start.4) | async-done | bytes 589856 | tf_op jit(solution)/shard_map/all_to_all | solution.py:459
  92.7 3.7 %all-to-all-start.3 = ((f32[8,256,128]{2,1,0:T(8,128)}), f32[8,256,128]{2,1,0:T(8,128)S(1)}, u32[]{:S(2)}, u32[]{:S(2)}) async-start(f32[8,256,128]{2,1,0:T(8,128)} %bitcast.8), calls=%async_computation.3 | async-start | bytes 2097152 | tf_op jit(solution)/shard_map/all_to_all | solution.py:455
  96.5 0.0 copy-start.6
  96.5 1.1 copy-done.6
  97.6 0.0 copy-start.18
  97.6 0.8 copy-done.18
  98.3 9.6 %local_backward.1 = (f32[256,768]{1,0:T(8,128)S(1)}, f32[256,768]{1,0:T(8,128)S(1)}, f32[256,768]{1,0:T(8,128)S(1)}, f32[256,768]{1,0:T(8,128)S(1)}) custom-call(s32[26]{0:T(128)S(1)} %pad_add_fusion.meta, f32[256,768]{1,0:T(8,128)S(1)} %copy-done.1, f32[256,768]{1,0:T(8,128)S(1)} %copy-done.3, f32[256,768]{1,0:T(8,128)S(1)} %copy-done.6, f32[256,768]{1,0:T(8,128)} %d.5, ...), custom_call_target="tpu_custom_call" | custom-call | flops 14000000000 | bytes 4000000 | tf_op jit(solution)/shard_map/local_backward/pallas_call | solution.py:442
  107.9 0.0 copy-start.9
  107.9 0.9 copy-done.9
  108.8 0.0 copy-start.11
  108.8 0.9 copy-done.11
  109.7 0.0 copy-start.13
  109.7 0.9 copy-done.13
  110.6 0.0 copy-start.15
  110.6 0.9 copy-done.15
  111.4 2.6 %all-to-all-done.3 = f32[8,256,128]{2,1,0:T(8,128)S(1)} async-done(((f32[8,256,128]{2,1,0:T(8,128)}), f32[8,256,128]{2,1,0:T(8,128)S(1)}, u32[]{:S(2)}, u32[]{:S(2)}) %all-to-all-start.3) | async-done | bytes 1048608 | tf_op jit(solution)/shard_map/all_to_all | solution.py:455
  114.0 0.0 copy-start.10
  114.0 1.1 copy-done.10
  115.1 0.0 copy-start.12
  115.1 1.1 copy-done.12
  116.3 0.0 copy-start.14
  116.3 1.1 copy-done.14
  117.4 0.0 copy-start.16
  117.4 1.1 copy-done.16
  118.5 3.2 %combine.1 = (f32[256,768]{1,0:T(8,128)}, f32[256,768]{1,0:T(8,128)}, f32[256,768]{1,0:T(8,128)}, f32[256,768]{1,0:T(8,128)}) custom-call(s32[26]{0:T(128)S(1)} %pad_add_fusion.meta, f32[256,768]{1,0:T(8,128)S(1)} %copy-done.10, f32[256,768]{1,0:T(8,128)S(1)} %copy-done.12, f32[256,768]{1,0:T(8,128)S(1)} %copy-done.14, f32[256,768]{1,0:T(8,128)S(1)} %copy-done.16, ...), custom_call_target="tpu_custom_call" | custom-call | flops 2000000000 | bytes 4000000 | tf_op jit(solution)/shard_map/combine/pallas_call | solution.py:442
Async XLA Ops:
  0.6 0.7 copy-start.19
  1.5 1.1 copy-start
  2.6 1.1 copy-start.2
  3.7 1.1 copy-start.4
  4.9 1.1 copy-start.7
  8.1 31.1 %copy-start.3 = (f32[256,768]{1,0:T(8,128)S(1)}, f32[256,768]{1,0:T(8,128)}, u32[]{:S(2)}) copy-start(f32[256,768]{1,0:T(8,128)} %k.5) | copy-start | bytes 2359300
  32.9 6.3 %copy-start.1 = (f32[256,768]{1,0:T(8,128)S(1)}, f32[256,768]{1,0:T(8,128)}, u32[]{:S(2)}) copy-start(f32[256,768]{1,0:T(8,128)} %q.5) | copy-start | bytes 2359300
  32.9 20.0 %all-to-all-start = ((f32[128,1,1152]{2,1,0:T(1,128)}), f32[128,1,1152]{2,1,0:T(1,128)S(1)}, u32[]{:S(2)}, u32[]{:S(2)}) async-start(f32[128,1,1152]{2,1,0:T(1,128)} %bitcast.2), calls=%async_computation | async-start | bytes 1179648 | tf_op jit(solution)/shard_map/all_to_all | solution.py:459
  39.2 1.1 copy-start.5
  40.3 1.1 copy-start.8
  46.3 0.6 copy-start.17
  74.4 18.3 %all-to-all-start.4 = ((f32[128,1,1152]{2,1,0:T(1,128)}), f32[128,1,1152]{2,1,0:T(1,128)S(1)}, u32[]{:S(2)}, u32[]{:S(2)}) async-start(f32[128,1,1152]{2,1,0:T(1,128)} %bitcast.10), calls=%async_computation.4 | async-start | bytes 1179648 | tf_op jit(solution)/shard_map/all_to_all | solution.py:459
  92.7 21.3 %all-to-all-start.3 = ((f32[8,256,128]{2,1,0:T(8,128)}), f32[8,256,128]{2,1,0:T(8,128)S(1)}, u32[]{:S(2)}, u32[]{:S(2)}) async-start(f32[8,256,128]{2,1,0:T(8,128)} %bitcast.8), calls=%async_computation.3 | async-start | bytes 2097152 | tf_op jit(solution)/shard_map/all_to_all | solution.py:455
  96.5 1.1 copy-start.6
  97.6 0.8 copy-start.18
  107.9 0.9 copy-start.9
  108.8 0.9 copy-start.11
  109.7 0.9 copy-start.13
  110.6 0.9 copy-start.15
  114.0 1.1 copy-start.10
  115.1 1.1 copy-start.12
  116.3 1.1 copy-start.14
  117.4 1.1 copy-start.16

commit v2 on v1

--- a/solution.py
+++ b/solution.py
@@ -124,41 +124,77 @@
     return top + jnp.log(total), delta / total
 
 
-def pick_kernel(meta, q, k, v, d, send2, send3, panel):
-    for a, ref in enumerate((q, k, v, d)):
-        for b in range(6):
+def block(a, b):
+    at = ROWS * (6 * a + b)
+    return pl.ds(at if isinstance(b, int) else pl.multiple_of(at, ROWS), ROWS)
+
+
+def columns(b):
+    return pl.ds(128 * b if isinstance(b, int) else pl.multiple_of(128 * b, 128), 128)
+
+
+def inward(refs, panel, sems, b):
+    return [
+        pltpu.make_async_copy(
+            ref.at[:, columns(b)], panel.at[block(a, b), :], sems.at[6 * a + b]
+        )
+        for a, ref in enumerate(refs)
+    ]
+
+
+def fetch(refs, panel, sems):
+    for b in range(6):
+        for copy in inward(refs, panel, sems, b):
+            copy.start()
+
+
+def arrive(refs, panel, sems, b):
+    for copy in inward(refs, panel, sems, b):
+        copy.wait()
+
+
+def pick_near_kernel(offsets, q, k, v, d, send, panel, sems):
+    fetch((q, k, v, d), panel, sems)
+    for b in range(6):
+        arrive((q, k, v, d), panel, sems, b)
+        for a in range(4):
             base = ROWS * (6 * a + b)
-            panel[base : base + ROWS, :] = ref[:, 128 * b : 128 * b + 128]
-            even = panel[pl.ds(base + meta[2 * b], LIVE2, stride=R2), :]
-            odd = panel[pl.ds(base + meta[2 * b + 1], LIVE2, stride=R2), :]
-            send2[b * 256 + a * LIVE2 : b * 256 + (a + 1) * LIVE2, :] = both(even, odd)
-    for h in range(HEADS):
-        take = [
-            panel[pl.ds(ROWS * (6 * a + h // 2) + meta[HEADS + h], LIVE3, stride=R3), :]
-            for a in range(4)
-        ]
-        if h % 2 == 0:
-            take[2], take[3] = pltpu.roll(take[2], HD, 1), pltpu.roll(take[3], HD, 1)
-        else:
-            take[0], take[1] = pltpu.roll(take[0], HD, 1), pltpu.roll(take[1], HD, 1)
-        kv = both(take[1], take[2])
-        qd = both(take[0], take[3])
-        for r in range(LIVE3):
-            send3[72 * h + 9 * r : 72 * h + 9 * r + 8, :] = kv
-        send3[pl.ds(72 * h + 8, LIVE3, stride=9), :] = qd
+            even = panel[pl.ds(base + offsets[0, 2 * b], LIVE2, stride=R2), :]
+            odd = panel[pl.ds(base + offsets[0, 2 * b + 1], LIVE2, stride=R2), :]
+            send[b * 256 + a * LIVE2 : b * 256 + (a + 1) * LIVE2, :] = both(even, odd)
+
+
+def pick_far_kernel(meta, q, k, v, d, send, panel, sems):
+    fetch((q, k, v, d), panel, sems)
+    for b in range(6):
+        arrive((q, k, v, d), panel, sems, b)
+        for h in (2 * b, 2 * b + 1):
+            take = [
+                panel[pl.ds(ROWS * (6 * a + b) + meta[HEADS + h], LIVE3, stride=R3), :]
+                for a in range(4)
+            ]
+            if h % 2 == 0:
+                take[2], take[3] = pltpu.roll(take[2], HD, 1), pltpu.roll(take[3], HD, 1)
+            else:
+                take[0], take[1] = pltpu.roll(take[0], HD, 1), pltpu.roll(take[1], HD, 1)
+            kv = both(take[1], take[2])
+            for r in range(LIVE3):
+                send[72 * h + 9 * r : 72 * h + 9 * r + 8, :] = kv
+            send[pl.ds(72 * h + 8, LIVE3, stride=9), :] = both(take[0], take[3])
 
 
 def pair_rows(shape, e, head_axis, pair_axis):
     return (iota(shape, head_axis) == 2 * iota(shape, pair_axis) + e).astype(F32)
 
 
-def local_forward_kernel(meta, q, k, v, d, stats, near, small):
+def local_forward_kernel(meta, q, k, v, d, stats, near, small, panel, sems):
+    fetch((q, k, v, d), panel, sems)
     stats[...] = jnp.zeros_like(stats)
     mask = iota((ROWS, ROWS), 0) <= iota((ROWS, ROWS), 1)
 
     def step(i, carry):
-        cols = pl.ds(pl.multiple_of(i * 128, 128), 128)
-        qp, kp, vp, dp = q[:, cols], k[:, cols], v[:, cols], d[:, cols]
+        arrive((q, k, v, d), panel, sems, i)
+        qp, kp, vp, dp = [panel[block(a, i), :] for a in range(4)]
         for e in range(2):
             at = slice(HD * e, HD * e + HD)
             ak, bq = pack_kq(kp[:, at], qp[:, at])
@@ -357,7 +393,8 @@
             send[b * 256 + a * LIVE2 : b * 256 + (a + 1) * LIVE2, :] = x[LIVE2 * b : LIVE2 * b + LIVE2]
 
 
-def local_backward_kernel(meta, q, k, v, d, own, stats, at_out, dq_out, dk_out, dv_out, joint):
+def local_backward_kernel(meta, q, k, v, d, own, stats, home3, out, joint, panel, sems):
+    fetch((q, k, v, d), panel, sems)
     base = 40 * meta[SEG_AT]
     shift2 = head_column(meta, 0, (16, ROWS))
     shift3 = head_column(meta, HEADS, (16, ROWS))
@@ -381,10 +418,11 @@
     joint[:, :ROWS] = lse
     joint[:, ROWS:] = delta
     mask = iota((ROWS, ROWS), 0) <= iota((ROWS, ROWS), 1)
+    low = half_mask(LIVE3)
 
     def step(i, carry):
-        cols = pl.ds(pl.multiple_of(i * 128, 128), 128)
-        qp, kp, vp, dp = q[:, cols], k[:, cols], v[:, cols], d[:, cols]
+        arrive((q, k, v, d), panel, sems, i)
+        qp, kp, vp, dp = [panel[block(a, i), :] for a in range(4)]
         res = []
         for e in range(2):
             at = slice(HD * e, HD * e + HD)
@@ -393,60 +431,66 @@
             lse_h = joint[pl.ds(2 * i + e, 1), :ROWS]
             delta_h = joint[pl.ds(2 * i + e, 1), ROWS:]
             res.append(backward_core(ak, bq, av, bd, mask, lse_h, delta_h))
-        at_out[:, cols] = jnp.concatenate([res[0][2], res[1][2]], axis=0).T
-        dq_out[:, cols] = jnp.concatenate([res[0][3], res[1][3]], axis=0).T
-        dk_out[:, cols] = both(fold(res[0][1]), fold(res[1][1]))
-        dv_out[:, cols] = both(fold(res[0][0]), fold(res[1][0]))
+        out[block(0, i), :] = jnp.concatenate([res[0][2], res[1][2]], axis=0).T
+        out[block(1, i), :] = jnp.concatenate([res[0][3], res[1][3]], axis=0).T
+        out[block(2, i), :] = both(fold(res[0][1]), fold(res[1][1]))
+        out[block(3, i), :] = both(fold(res[0][0]), fold(res[1][0]))
+        for e in range(2):
+            h = 2 * i + e
+            kv = home3[pl.ds(72 * h, LIVE3), :]
+            for r in range(1, LIVE3):
+                kv = kv + home3[pl.ds(72 * h + 9 * r, LIVE3), :]
+            aq = home3[pl.ds(72 * h + 8, LIVE3, stride=9), :]
+            kv_turn, aq_turn = pltpu.roll(kv, HD, 1), pltpu.roll(aq, HD, 1)
+            parts = (aq, aq_turn, kv, kv_turn) if e == 0 else (aq_turn, aq, kv_turn, kv)
+            keep = low if e == 0 else ~low
+            for a, x in enumerate(parts):
+                rows = pl.ds(ROWS * (6 * a + i) + meta[HEADS + h], LIVE3, stride=R3)
+                out[rows, :] = out[rows, :] + jnp.where(keep, x, 0.0)
         return carry
 
     lax.fori_loop(0, 6, step, 0)
 
 
-def combine_kernel(meta, at1, dq1, dk1, dv1, got2, got3, at_out, dq_out, dk_out, dv_out, panel):
+def combine_kernel(meta, local, got, at_out, dq_out, dk_out, dv_out, panel, sems):
     low = half_mask(LIVE2)
-    for a, local in enumerate((at1, dq1, dk1, dv1)):
-        for b in range(6):
+    copies = []
+    for b in range(6):
+        for a, out in enumerate((at_out, dq_out, dk_out, dv_out)):
             base = ROWS * (6 * a + b)
-            panel[base : base + ROWS, :] = local[:, 128 * b : 128 * b + 128]
-            x = got2[b * 256 + a * LIVE2 : b * 256 + (a + 1) * LIVE2, :]
+            panel[base : base + ROWS, :] = local[base : base + ROWS, :]
+            x = got[b * 256 + a * LIVE2 : b * 256 + (a + 1) * LIVE2, :]
             for e in range(2):
                 rows = pl.ds(base + meta[2 * b + e], LIVE2, stride=R2)
                 keep = low if e == 0 else ~low
                 panel[rows, :] = panel[rows, :] + jnp.where(keep, x, 0.0)
-    low = half_mask(LIVE3)
-    for h in range(HEADS):
-        kv = got3[72 * h : 72 * h + 8, :]
-        for r in range(1, LIVE3):
-            kv = kv + got3[72 * h + 9 * r : 72 * h + 9 * r + 8, :]
-        aq = got3[pl.ds(72 * h + 8, LIVE3, stride=9), :]
-        kv_turn, aq_turn = pltpu.roll(kv, HD, 1), pltpu.roll(aq, HD, 1)
-        if h % 2 == 0:
-            parts, keep = (aq, aq_turn, kv, kv_turn), low
-        else:
-            parts, keep = (aq_turn, aq, kv_turn, kv), ~low
-        for a, x in enumerate(parts):
-            rows = pl.ds(ROWS * (6 * a + h // 2) + meta[HEADS + h], LIVE3, stride=R3)
-            panel[rows, :] = panel[rows, :] + jnp.where(keep, x, 0.0)
-    for a, out in enumerate((at_out, dq_out, dk_out, dv_out)):
-        for b in range(6):
-            base = ROWS * (6 * a + b)
-            out[:, 128 * b : 128 * b + 128] = panel[base : base + ROWS, :]
-
-
-PANEL = [pltpu.VMEM((24 * ROWS, 128), F32)]
-
-
-def call(kernel, name, outs, args, flops, scratch=()):
-    specs = [pl.BlockSpec(memory_space=pltpu.SMEM)]
-    specs += [pl.BlockSpec(memory_space=pltpu.VMEM)] * (len(args) - 1)
+            copies.append(
+                pltpu.make_async_copy(
+                    panel.at[block(a, b), :], out.at[:, columns(b)], sems.at[6 * a + b]
+                )
+            )
+            copies[-1].start()
+    for copy in copies:
+        copy.wait()
+
+
+SMEM = pl.BlockSpec(memory_space=pltpu.SMEM)
+HBM = pl.BlockSpec(memory_space=pltpu.HBM)
+VMEM = pl.BlockSpec(memory_space=pltpu.VMEM)
+PANEL = pltpu.VMEM((24 * ROWS, 128), F32)
+FETCH = [PANEL, pltpu.SemaphoreType.DMA((24,))]
+
+
+def call(kernel, name, outs, args, flops, mib, scratch=(), hbm=(), out_spec=VMEM):
+    shapes = [x if hasattr(x, "memory_space") else jax.ShapeDtypeStruct(x, F32) for x in outs]
     return pl.pallas_call(
         kernel,
         name=name,
-        out_shape=[jax.ShapeDtypeStruct(shape, F32) for shape in outs],
-        in_specs=specs,
-        out_specs=[pl.BlockSpec(memory_space=pltpu.VMEM)] * len(outs),
+        out_shape=shapes,
+        in_specs=[SMEM] + [HBM if i in hbm else VMEM for i in range(1, len(args))],
+        out_specs=[out_spec] * len(outs),
         scratch_shapes=list(scratch),
-        compiler_params=pltpu.CompilerParams(vmem_limit_bytes=48 * 1024 * 1024),
+        compiler_params=pltpu.CompilerParams(vmem_limit_bytes=mib * 1024 * 1024),
         cost_estimate=pl.CostEstimate(flops=flops, bytes_accessed=4_000_000, transcendentals=0),
     )(*args)
 
@@ -462,18 +506,28 @@
 def body(q, k, v, d, offsets):
     place = jnp.stack([lax.axis_index("seg"), lax.axis_index("blk")]).astype(jnp.int32)
     meta = jnp.concatenate([offsets.reshape(-1), place])
-    send2, send3 = call(pick_kernel, "pick", [(2048, 128), (1152, 128)], (meta, q, k, v, d), 10**9, PANEL)
+    rows = tuple(pltpu.with_memory_space_constraint(x, pltpu.HBM) for x in (q, k, v, d))
+    given = (1, 2, 3, 4)
+    (send2,) = call(
+        pick_near_kernel, "pick_near", [(2048, 128)], (offsets, *rows), 10**9, 16, FETCH, given
+    )
     got2 = swap_near(send2)
+    (send3,) = call(
+        pick_far_kernel, "pick_far", [(1152, 128)], (meta, *rows), 10**9, 16, FETCH, given
+    )
     got3 = swap_all(send3)
     stats1, near1, small1 = call(
         local_forward_kernel,
         "local_forward",
         [(16, 2 * ROWS), (8, 256), (128, 128)],
-        (meta, q, k, v, d),
+        (meta, *rows),
         8 * 10**9,
+        16,
+        FETCH,
+        given,
     )
     near2, small2 = call(
-        near_forward_kernel, "near_forward", [(8, 256), (128, 128)], (meta, got2), 4 * 10**9
+        near_forward_kernel, "near_forward", [(8, 256), (128, 128)], (meta, got2), 4 * 10**9, 24
     )
     own3, send_stats = call(
         far_forward_kernel,
@@ -481,26 +535,45 @@
         [(8, 128), (640, 128)],
         (meta, got3, near1, small1, near2, small2),
         2 * 10**9,
+        16,
     )
     stats = swap_all(send_stats)
     (back3,) = call(
-        far_backward_kernel, "far_backward", [(1152, 128)], (meta, got3, own3, stats), 3 * 10**9
+        far_backward_kernel, "far_backward", [(1152, 128)], (meta, got3, own3, stats), 3 * 10**9, 16
     )
     home3 = swap_all(back3)
     (back2,) = call(
-        near_backward_kernel, "near_backward", [(2048, 128)], (meta, got2, near2, stats), 8 * 10**9
+        near_backward_kernel,
+        "near_backward",
+        [(2048, 128)],
+        (meta, got2, near2, stats),
+        8 * 10**9,
+        24,
     )
     home2 = swap_near(back2)
-    full = [(ROWS, HEADS * HD)] * 4
-    local = call(
+    (local,) = call(
         local_backward_kernel,
         "local_backward",
-        full,
-        (meta, q, k, v, d, stats1, stats),
+        [PANEL],
+        (meta, *rows, stats1, stats, home3),
         14 * 10**9,
-        scratch=[pltpu.VMEM((16, 2 * ROWS), F32)],
-    )
-    return tuple(call(combine_kernel, "combine", full, (meta, *local, home2, home3), 2 * 10**9, PANEL))
+        20,
+        [pltpu.VMEM((16, 2 * ROWS), F32)] + FETCH,
+        given,
+    )
+    local = pltpu.with_memory_space_constraint(local, pltpu.VMEM)
+    return tuple(
+        call(
+            combine_kernel,
+            "combine",
+            [(ROWS, HEADS * HD)] * 4,
+            (meta, local, home2),
+            2 * 10**9,
+            16,
+            FETCH,
+            out_spec=HBM,
+        )
+    )
 
 
 def solution(mesh):

time: 123 us -> 115 us (0.935)
  blocking collectives: 42.1 us -> 16.1 us
  waiting for transfers between devices: 15.3 us -> 33.1 us
  local copies, waits for them, and re-layouts: 18.1 us -> 4.27 us
  starting transfers between devices: 14.6 us -> 22.2 us
  Pallas kernels: 30.8 us -> 37.7 us
    all_to_all x1 -> x0, blocking collectives: 24.8 us -> none  [swap_near(): return lax.all_to_all(x, 'blk', 0, 0, tiled=True)]
    all_to_all x1 -> x2, waiting for transfers between devices: 2.58 us -> 18.8 us  [swap_near(): return lax.all_to_all(x, 'blk', 0, 0, tiled=True)]
    unnamed x40 -> x8, local copies, waits for them, and re-layouts: 18 us -> 4.19 us
    all_to_all x1 -> x2, starting transfers between devices: 3.74 us -> 11.4 us  [swap_near(): return lax.all_to_all(x, 'blk', 0, 0, tiled=True)]
    pallas_call x8 -> x9, Pallas kernels: 30.8 us -> 37.7 us  [call(): pl.pallas_call(kernel, name=name, out_shape=shapes, in_specs=[SMEM] + [HB...]
    all_to_all x2, waiting for transfers between devices: 12.7 us -> 14.3 us  [swap_all(): lax.all_to_all(x.reshape(128, -1), ALL, 0, 0, tiled=True).reshape(-1, 128)]
  transfers between devices with their start and end apart: 3 -> 4, of which waited for: 3 -> 4; matrix products, arithmetic and copies ran while one was open for 0% -> 0% of each run, Pallas kernels for 17% -> 24%
where the time goes in v2:
time: 115 us; the launch traced here: 114 us
  Pallas kernels  37.7 us (33%)
  waiting for transfers between devices  33.1 us (29%)
  starting transfers between devices  22.2 us (19%)
  blocking collectives  16.1 us (14%)
  local copies, waits for them, and re-layouts  4.27 us (4%)
    pallas_call x9, Pallas kernels, call(): pl.pallas_call(kernel, name=name, out_shape=shapes, in_specs=[SMEM] + [HB...  37.7 us
    all_to_all x2, waiting for transfers between devices, swap_near(): return lax.all_to_all(x, 'blk', 0, 0, tiled=True)  18.8 us
    all_to_all x1, blocking collectives, swap_all(): lax.all_to_all(x.reshape(128, -1), ALL, 0, 0, tiled=True).reshape(-1, 128)  16.1 us
    all_to_all x2, waiting for transfers between devices, swap_all(): lax.all_to_all(x.reshape(128, -1), ALL, 0, 0, tiled=True).reshape(-1, 128)  14.3 us
    all_to_all x2, starting transfers between devices, swap_near(): return lax.all_to_all(x, 'blk', 0, 0, tiled=True)  11.4 us
    all_to_all x2, starting transfers between devices, swap_all(): lax.all_to_all(x.reshape(128, -1), ALL, 0, 0, tiled=True).reshape(-1, 128)  10.8 us
    unnamed x8, local copies, waits for them, and re-layouts  4.19 us
  transfers between devices with their start and end apart: 4, of which 4 were waited for; matrix products, arithmetic and copies ran while one was open for 0% of the time, Pallas kernels for 24%

profile of v2, /device:TPU:0, one launch (start us, length us, event | category | flops | bytes accessed | tf_op | source)
XLA Modules:
  0.0 114.1 jit_solution(3832849340929330298)
XLA Ops:
  0.6 0.0 copy-start
  0.6 0.7 copy-done
  1.3 0.0 copy-start.1
  1.3 3.7 %pick_near.1 = f32[2048,128]{1,0:T(8,128)} custom-call(s32[2,12]{1,0:T(2,128)S(1)} %copy-done, f32[256,768]{1,0:T(8,128)} %q.7, f32[256,768]{1,0:T(8,128)} %k.7, f32[256,768]{1,0:T(8,128)} %v.7, f32[256,768]{1,0:T(8,128)} %d.7), custom_call_target="tpu_custom_call" | custom-call | flops 1000000000 | bytes 4000000 | tf_op jit(solution)/shard_map/pick_near/pallas_call | solution.py:486
  5.1 7.7 %all-to-all-start.1 = ((f32[8,256,128]{2,1,0:T(8,128)}), f32[8,256,128]{2,1,0:T(8,128)S(1)}, u32[]{:S(2)}, u32[]{:S(2)}) async-start(f32[8,256,128]{2,1,0:T(8,128)} %bitcast.4), calls=%async_computation.1 | async-start | bytes 2097152 | tf_op jit(solution)/shard_map/all_to_all | solution.py:499
  12.8 0.0 copy-done.1
  12.8 0.1 reshape.39
  12.9 0.1 pad_add_fusion.meta
  12.9 3.6 %pick_far.1 = f32[1152,128]{1,0:T(8,128)} custom-call(s32[26]{0:T(128)S(1)} %pad_add_fusion.meta, f32[256,768]{1,0:T(8,128)} %q.7, f32[256,768]{1,0:T(8,128)} %k.7, f32[256,768]{1,0:T(8,128)} %v.7, f32[256,768]{1,0:T(8,128)} %d.7), custom_call_target="tpu_custom_call" | custom-call | flops 1000000000 | bytes 4000000 | tf_op jit(solution)/shard_map/pick_far/pallas_call | solution.py:486
  16.6 13.4 %all-to-all-done.1 = f32[8,256,128]{2,1,0:T(8,128)S(1)} async-done(((f32[8,256,128]{2,1,0:T(8,128)}), f32[8,256,128]{2,1,0:T(8,128)S(1)}, u32[]{:S(2)}, u32[]{:S(2)}) %all-to-all-start.1) | async-done | bytes 1048608 | tf_op jit(solution)/shard_map/all_to_all | solution.py:499
  30.0 6.2 %all-to-all-start = ((f32[128,1,1152]{2,1,0:T(1,128)}), f32[128,1,1152]{2,1,0:T(1,128)S(1)}, u32[]{:S(2)}, u32[]{:S(2)}) async-start(f32[128,1,1152]{2,1,0:T(1,128)} %bitcast.2), calls=%async_computation | async-start | bytes 1179648 | tf_op jit(solution)/shard_map/all_to_all | solution.py:503
  36.2 6.2 %local_forward.1 = (f32[16,512]{1,0:T(8,128)S(1)}, f32[8,256]{1,0:T(8,128)S(1)}, f32[128,128]{1,0:T(8,128)S(1)}) custom-call(s32[26]{0:T(128)S(1)} %pad_add_fusion.meta, f32[256,768]{1,0:T(8,128)} %q.7, f32[256,768]{1,0:T(8,128)} %k.7, f32[256,768]{1,0:T(8,128)} %v.7, f32[256,768]{1,0:T(8,128)} %d.7), custom_call_target="tpu_custom_call" | custom-call | flops 8000000000 | bytes 4000000 | tf_op jit(solution)/shard_map/local_forward/pallas_call | solution.py:486
  42.3 2.3 %near_forward.1 = (f32[8,256]{1,0:T(8,128)S(1)}, f32[128,128]{1,0:T(8,128)S(1)}) custom-call(s32[26]{0:T(128)S(1)} %pad_add_fusion.meta, f32[2048,128]{1,0:T(8,128)S(1)} %bitcast.12), custom_call_target="tpu_custom_call" | custom-call | flops 4000000000 | bytes 4000000 | tf_op jit(solution)/shard_map/near_forward/pallas_call | solution.py:486
  44.7 5.2 %all-to-all-done = f32[128,1,1152]{2,1,0:T(1,128)S(1)} async-done(((f32[128,1,1152]{2,1,0:T(1,128)}), f32[128,1,1152]{2,1,0:T(1,128)S(1)}, u32[]{:S(2)}, u32[]{:S(2)}) %all-to-all-start) | async-done | bytes 589856 | tf_op jit(solution)/shard_map/all_to_all | solution.py:503
  49.8 1.5 %far_forward.1 = (f32[8,128]{1,0:T(8,128)S(1)}, f32[640,128]{1,0:T(8,128)S(1)}) custom-call(s32[26]{0:T(128)S(1)} %pad_add_fusion.meta, f32[1152,128]{1,0:T(8,128)S(1)} %bitcast.15, f32[8,256]{1,0:T(8,128)S(1)} %get-tuple-element.12.near1, f32[128,128]{1,0:T(8,128)S(1)} %get-tuple-element.13.small1, f32[8,256]{1,0:T(8,128)S(1)} %get-tuple-element.14.near2.own, ...), custom_call_target="tpu_custom_call" | custom-call | flops 2000000000 | bytes 4000000 | tf_op jit(solution)/shard_map/far_forward/pallas_call | solution.py:486
  51.4 16.1 %all_to_all.49 = f32[128,1,640]{2,1,0:T(1,128)S(1)} all-to-all(f32[128,1,640]{2,1,0:T(1,128)S(1)} %bitcast.21), channel_id=1, replica_groups=mesh['seg'=16,'blk'=8] {'seg','blk'}, dimensions={0} | all-to-all | bytes 655360 | tf_op jit(solution)/shard_map/all_to_all | solution.py:503
  67.5 2.7 %far_backward.1 = f32[1152,128]{1,0:T(8,128)} custom-call(s32[26]{0:T(128)S(1)} %pad_add_fusion.meta, f32[1152,128]{1,0:T(8,128)S(1)} %bitcast.16, f32[8,128]{1,0:T(8,128)S(1)} %get-tuple-element.17.own, f32[640,128]{1,0:T(8,128)S(1)} %bitcast.18), custom_call_target="tpu_custom_call" | custom-call | flops 3000000000 | bytes 4000000 | tf_op jit(solution)/shard_map/far_backward/pallas_call | solution.py:486
  70.2 4.6 %all-to-all-start.3 = ((f32[128,1,1152]{2,1,0:T(1,128)}), f32[128,1,1152]{2,1,0:T(1,128)S(1)}, u32[]{:S(2)}, u32[]{:S(2)}) async-start(f32[128,1,1152]{2,1,0:T(1,128)} %bitcast.8), calls=%async_computation.3 | async-start | bytes 1179648 | tf_op jit(solution)/shard_map/all_to_all | solution.py:503
  74.8 4.6 %near_backward.1 = f32[2048,128]{1,0:T(8,128)} custom-call(s32[26]{0:T(128)S(1)} %pad_add_fusion.meta, f32[2048,128]{1,0:T(8,128)S(1)} %bitcast.13, f32[8,256]{1,0:T(8,128)S(1)} %get-tuple-element.14.near2.own, f32[640,128]{1,0:T(8,128)S(1)} %bitcast.19), custom_call_target="tpu_custom_call" | custom-call | flops 8000000000 | bytes 4000000 | tf_op jit(solution)/shard_map/near_backward/pallas_call | solution.py:486
  79.4 9.1 %all-to-all-done.3 = f32[128,1,1152]{2,1,0:T(1,128)S(1)} async-done(((f32[128,1,1152]{2,1,0:T(1,128)}), f32[128,1,1152]{2,1,0:T(1,128)S(1)}, u32[]{:S(2)}, u32[]{:S(2)}) %all-to-all-start.3) | async-done | bytes 589856 | tf_op jit(solution)/shard_map/all_to_all | solution.py:503
  88.5 3.6 %all-to-all-start.4 = ((f32[8,256,128]{2,1,0:T(8,128)}), f32[8,256,128]{2,1,0:T(8,128)S(1)}, u32[]{:S(2)}, u32[]{:S(2)}) async-start(f32[8,256,128]{2,1,0:T(8,128)} %bitcast.10), calls=%async_computation.4 | async-start | bytes 2097152 | tf_op jit(solution)/shard_map/all_to_all | solution.py:499
  92.1 10.6 %local_backward.1.local = f32[6144,128]{1,0:T(8,128)S(1)} custom-call(s32[26]{0:T(128)S(1)} %pad_add_fusion.meta, f32[256,768]{1,0:T(8,128)} %q.7, f32[256,768]{1,0:T(8,128)} %k.7, f32[256,768]{1,0:T(8,128)} %v.7, f32[256,768]{1,0:T(8,128)} %d.7, f32[16,512]{1,0:T(8,128)S(1)} %get-tuple-element.11.own, f32[640,128]{1,0:T(8,128)S(1)} %bitcast.20, ...), custom_call_target="tpu_custom_call" | custom-call | flops 14000000000 | bytes 4000000 | tf_op jit(solution)/shard_map/local_backward/pallas_call | solution.py:486
  102.7 0.0 copy-start.2
  102.8 1.6 %copy-done.2 = f32[6144,128]{1,0:T(8,128)} copy-done((f32[6144,128]{1,0:T(8,128)}, f32[6144,128]{1,0:T(8,128)S(1)}, u32[]{:S(2)}) %copy-start.2) | copy-done | bytes 3145752
  104.4 5.4 %all-to-all-done.4 = f32[8,256,128]{2,1,0:T(8,128)S(1)} async-done(((f32[8,256,128]{2,1,0:T(8,128)}), f32[8,256,128]{2,1,0:T(8,128)S(1)}, u32[]{:S(2)}, u32[]{:S(2)}) %all-to-all-start.4) | async-done | bytes 1048608 | tf_op jit(solution)/shard_map/all_to_all | solution.py:499
  109.8 0.0 copy-start.3
  109.8 1.9 %copy-done.3 = f32[6144,128]{1,0:T(8,128)S(1)} copy-done((f32[6144,128]{1,0:T(8,128)S(1)}, f32[6144,128]{1,0:T(8,128)}, u32[]{:S(2)}) %copy-start.3) | copy-done | bytes 3145752
  111.7 2.4 %combine.1 = (f32[256,768]{1,0:T(8,128)}, f32[256,768]{1,0:T(8,128)}, f32[256,768]{1,0:T(8,128)}, f32[256,768]{1,0:T(8,128)}) custom-call(s32[26]{0:T(128)S(1)} %pad_add_fusion.meta, f32[6144,128]{1,0:T(8,128)S(1)} %copy-done.3, f32[2048,128]{1,0:T(8,128)S(1)} %bitcast.14), custom_call_target="tpu_custom_call" | custom-call | flops 2000000000 | bytes 4000000 | tf_op jit(solution)/shard_map/combine/pallas_call | solution.py:486
Async XLA Ops:
  0.6 0.7 copy-start
  1.3 11.5 %copy-start.1 = (s32[2,12]{1,0:T(2,128)S(1)}, s32[2,12]{1,0:T(2,128)}, u32[]{:S(2)}) copy-start(s32[2,12]{1,0:T(2,128)} %offsets.1) | copy-start | bytes 292
  5.1 24.9 %all-to-all-start.1 = ((f32[8,256,128]{2,1,0:T(8,128)}), f32[8,256,128]{2,1,0:T(8,128)S(1)}, u32[]{:S(2)}, u32[]{:S(2)}) async-start(f32[8,256,128]{2,1,0:T(8,128)} %bitcast.4), calls=%async_computation.1 | async-start | bytes 2097152 | tf_op jit(solution)/shard_map/all_to_all | solution.py:499
  30.0 19.9 %all-to-all-start = ((f32[128,1,1152]{2,1,0:T(1,128)}), f32[128,1,1152]{2,1,0:T(1,128)S(1)}, u32[]{:S(2)}, u32[]{:S(2)}) async-start(f32[128,1,1152]{2,1,0:T(1,128)} %bitcast.2), calls=%async_computation | async-start | bytes 1179648 | tf_op jit(solution)/shard_map/all_to_all | solution.py:503
  70.2 18.3 %all-to-all-start.3 = ((f32[128,1,1152]{2,1,0:T(1,128)}), f32[128,1,1152]{2,1,0:T(1,128)S(1)}, u32[]{:S(2)}, u32[]{:S(2)}) async-start(f32[128,1,1152]{2,1,0:T(1,128)} %bitcast.8), calls=%async_computation.3 | async-start | bytes 1179648 | tf_op jit(solution)/shard_map/all_to_all | solution.py:503
  88.5 21.3 %all-to-all-start.4 = ((f32[8,256,128]{2,1,0:T(8,128)}), f32[8,256,128]{2,1,0:T(8,128)S(1)}, u32[]{:S(2)}, u32[]{:S(2)}) async-start(f32[8,256,128]{2,1,0:T(8,128)} %bitcast.10), calls=%async_computation.4 | async-start | bytes 2097152 | tf_op jit(solution)/shard_map/all_to_all | solution.py:499
  102.7 1.6 %copy-start.2 = (f32[6144,128]{1,0:T(8,128)}, f32[6144,128]{1,0:T(8,128)S(1)}, u32[]{:S(2)}) copy-start(f32[6144,128]{1,0:T(8,128)S(1)} %local_backward.1.local) | copy-start | bytes 9437188
  109.8 1.9 %copy-start.3 = (f32[6144,128]{1,0:T(8,128)S(1)}, f32[6144,128]{1,0:T(8,128)}, u32[]{:S(2)}) copy-start(f32[6144,128]{1,0:T(8,128)} %copy-done.2) | copy-start | bytes 9437188

commit v3 on v2

v3 whole, which is shorter than its diff:
```python
import functools

import jax
import jax.numpy as jnp
from jax import lax
from jax.experimental import pallas as pl
from jax.experimental.pallas import tpu as pltpu
from jax.sharding import PartitionSpec as P

HEADS = 12
HD = 64
ROWS = 256
LIVE2 = 64
LIVE3 = 8
R2 = 4
R3 = 32
NEG = -1e30
SCALE = HD**-0.5
BF = jnp.bfloat16
F32 = jnp.float32
ALL = ("seg", "blk")
SEG_AT, BLK_AT = 24, 25
FAR_AT, STAT_AT, MESSAGE = 256, 288, 296
PAIR = 72


def nt(a, b):
    return lax.dot_general(a, b, (((1,), (1,)), ((), ())), preferred_element_type=F32)


def nn(a, b):
    return lax.dot_general(a, b, (((1,), (0,)), ((), ())), preferred_element_type=F32)


def tn(a, b):
    return lax.dot_general(a, b, (((0,), (0,)), ((), ())), preferred_element_type=F32)


def exact(a, b, dims=((1,), (0,))):
    return lax.dot_general(
        a, b, (dims, ((), ())), preferred_element_type=F32, precision=lax.Precision.HIGHEST
    )


def iota(shape, axis):
    return lax.broadcasted_iota(jnp.int32, shape, axis)


def split2(x):
    first = x.astype(BF)
    return first, (x - first.astype(F32)).astype(BF)


def split3(x):
    first = x.astype(BF)
    rest = x - first.astype(F32)
    second = rest.astype(BF)
    return first, second, (rest - second.astype(F32)).astype(BF)


def cat(parts):
    return jnp.concatenate(parts, axis=1)


def pack_kq(k, q):
    k0, k1, k2 = split3(k)
    q0, q1, q2 = split3(q * SCALE)
    return cat([k0, k1, k0, k1, k0, k2]), cat([q0, q1, q1, q0, q2, q0])


def pack_vd(v, d):
    v0, v1 = split2(v)
    d0, d1 = split2(d)
    return cat([v0, v1, v0, v1]), cat([d0, d1, d1, d0])


def forward_core(ak, bq, av, bd, mask):
    s = jnp.where(mask, nt(ak, bq), NEG)
    dp = nt(av, bd)
    top = jnp.max(s, axis=0, keepdims=True)
    p = jnp.exp(s - top)
    total = jnp.sum(p, axis=0, keepdims=True)
    cross = jnp.sum(p * dp, axis=0, keepdims=True)
    return top, total, cross / total, p, dp


def backward_core(p, dp, delta, ak, bq, av, bd):
    g = p * (dp - delta)
    p0, p1 = split2(p)
    g0, g1 = split2(g)
    d01, q01, v01, k01 = bd[:, :128], bq[:, :128], av[:, :128], ak[:, :128]
    dv = nn(p0, d01) + nn(p1, d01)
    dk = nn(g0, q01) + nn(g1, q01)
    at = tn(v01, p0) + tn(v01, p1)
    qt = tn(k01, g0) + tn(k01, g1)
    return at[:HD] + at[HD:], (qt[:HD] + qt[HD:]) * SCALE, dk, dv


def fold(x):
    return x + pltpu.roll(x, HD, 1)


def half_mask(rows):
    return iota((rows, 128), 1) < HD


def both(a, b):
    return jnp.where(half_mask(a.shape[0]), a, b)


def merge(levels):
    top = functools.reduce(jnp.maximum, [lse for lse, _ in levels])
    weights = [jnp.exp(lse - top) for lse, _ in levels]
    total = functools.reduce(jnp.add, weights)
    delta = functools.reduce(jnp.add, [w * d for w, (_, d) in zip(weights, levels)])
    return top + jnp.log(total), delta / total


def block(a, b):
    at = ROWS * (6 * a + b)
    return pl.ds(at if isinstance(b, int) else pl.multiple_of(at, ROWS), ROWS)


def columns(b):
    return pl.ds(128 * b if isinstance(b, int) else pl.multiple_of(128 * b, 128), 128)


def inward(refs, panel, sems, b):
    return [
        pltpu.make_async_copy(
            ref.at[:, columns(b)], panel.at[block(a, b), :], sems.at[6 * a + b]
        )
        for a, ref in enumerate(refs)
    ]


def fetch(refs, panel, sems):
    for b in range(6):
        for copy in inward(refs, panel, sems, b):
            copy.start()


def arrive(refs, panel, sems, b):
    for copy in inward(refs, panel, sems, b):
        copy.wait()


def live_positions(near, far, skip_far=False):
    lane = iota((1, 128), 1)
    spot = jnp.where(lane < LIVE2, R2 * lane + near, R3 * (lane - LIVE2) + far)
    end = jnp.where(skip_far, LIVE2, LIVE2 + LIVE3)
    return jnp.where(lane < end, spot, -1)


def halves(x, e):
    return x[:, HD * e : HD * e + HD]


def turn(x):
    return pltpu.roll(x, HD, 1)


def open_kernel(offsets, q, k, v, d, send, live, panel, sems):
    fetch((q, k, v, d), panel, sems)

    def step(b, carry):
        arrive((q, k, v, d), panel, sems, b)
        out = pl.multiple_of(MESSAGE * b, 8)
        rows = []
        for a in range(4):
            base = ROWS * (6 * a + b)
            near = both(
                panel[pl.ds(base + offsets[0, 2 * b], LIVE2, stride=R2), :],
                panel[pl.ds(base + offsets[0, 2 * b + 1], LIVE2, stride=R2), :],
            )
            far = both(
                panel[pl.ds(base + offsets[1, 2 * b], LIVE3, stride=R3), :],
                panel[pl.ds(base + offsets[1, 2 * b + 1], LIVE3, stride=R3), :],
            )
            send[pl.ds(out + LIVE2 * a, LIVE2), :] = near
            send[pl.ds(out + FAR_AT + LIVE3 * a, LIVE3), :] = far
            rows.append((near, far))
        pad = jnp.zeros((56, 128), F32)
        keep = pl.multiple_of(2 * PAIR * b, 8)
        queries, grads = [], []
        for n, (a, group) in enumerate(((0, queries), (3, grads))):
            near, far = rows[a]
            live[pl.ds(keep + PAIR * n, LIVE2), :] = near
            live[pl.ds(keep + PAIR * n + LIVE2, LIVE3), :] = far
            group.append(jnp.concatenate([near, far, pad], axis=0))
        kp, vp = panel[block(1, b), :], panel[block(2, b), :]
        for e in range(2):
            ak, bq = pack_kq(halves(kp, e), halves(queries[0], e))
            av, bd = pack_vd(halves(vp, e), halves(grads[0], e))
            spot = live_positions(offsets[0, 2 * b + e], offsets[1, 2 * b + e])
            top, total, delta, _, _ = forward_core(ak, bq, av, bd, iota((ROWS, 128), 0) <= spot)
            send[pl.ds(out + STAT_AT + 2 * e, 1), :] = top + jnp.log(total)
            send[pl.ds(out + STAT_AT + 2 * e + 1, 1), :] = delta
        return carry

    lax.fori_loop(0, 6, step, 0)


def gather_rows(ref, at, count):
    return jnp.concatenate(
        [ref[MESSAGE * b + at : MESSAGE * b + at + count, :] for b in range(8)], axis=0
    )


def stat_rows(ref, n):
    return ref[pl.ds(STAT_AT + n, 8, stride=MESSAGE), :]


def spread_kernel(meta, got, send):
    k, v = gather_rows(got, FAR_AT + 8, 8), gather_rows(got, FAR_AT + 16, 8)
    kv = both(k, turn(v)), both(turn(k), v)
    for s in range(16):
        send[64 * s : 64 * s + 64, :] = kv[s % 2]


def near_shift(meta, e):
    h = jnp.minimum(2 * meta[BLK_AT] + e, HEADS - 1)
    live = meta[HEADS + h] % R2 == meta[h]
    return live, meta[HEADS + h] // R2


def to_rows(x):
    return jnp.concatenate([x[:, HD * b : HD * b + HD] for b in range(8)], axis=0)


def near_blocks(got):
    qs, ks, vs, ds = [gather_rows(got, a * LIVE2, LIVE2) for a in range(4)]
    for e in range(2):
        ak, bq = pack_kq(halves(ks, e), halves(qs, e))
        av, bd = pack_vd(halves(vs, e), halves(ds, e))
        parts = []
        for j in range(2):
            keys, rows = 256 * (j + 1), slice(256 * j, 256 * j + 256)
            mask = iota((keys, 256), 0) <= iota((keys, 256), 1) + 256 * j
            parts.append((ak[:keys], bq[rows], av[:keys], bd[rows], mask))
        yield parts


def near_forward_kernel(meta, got, own, mine, theirs):
    found = []
    for parts in near_blocks(got):
        lses, deltas = [], []
        for part in parts:
            top, total, delta, _, _ = forward_core(*part)
            lses.append(top + jnp.log(total))
            deltas.append(delta)
        found.append((to_rows(cat(lses)), to_rows(cat(deltas))))
    lse, delta = [cat([found[0][n], found[1][n]]) for n in range(2)]
    own[:, :128] = lse
    own[:, 128:] = delta
    sub, lane = iota((128, 128), 0), iota((128, 128), 1)
    spread = ((sub < 8) & (lane < 64) & (lane % 8 == sub)).astype(F32)
    diagonal = iota((8, 128), 0) == iota((8, 128), 1) // 8
    q, d = gather_rows(got, FAR_AT, 8), gather_rows(got, FAR_AT + 24, 8)
    qd = both(q, turn(d)), both(turn(q), d)
    blocks = []
    for e in range(2):
        live, shift = near_shift(meta, e)
        pick = (sub // HD == e) & (sub % HD // 8 == lane) & (sub % 8 == shift)
        pick = pick.astype(F32)
        merged = merge(
            [
                (turn(stat_rows(got, 2 * e)), turn(stat_rows(got, 2 * e + 1))),
                (jnp.where(live, exact(lse, pick), NEG), exact(delta, pick)),
            ]
        )
        flat = [
            jnp.sum(jnp.where(diagonal, exact(x, spread), 0.0), axis=0, keepdims=True)
            for x in merged
        ]
        blocks.append(jnp.concatenate([qd[e], *flat, jnp.zeros((6, 128), F32)], axis=0))
    first = meta[SEG_AT] % 2 == 0
    mine[...] = jnp.where(first, blocks[0], blocks[1])
    theirs[...] = jnp.where(first, blocks[1], blocks[0])


def far_kernel(meta, kv, mine, pair, send, keep, back):
    first = meta[SEG_AT] % 2 == 0
    x, y = mine[...], pair[...]
    low, high = jnp.where(first, x, y), jnp.where(first, y, x)
    qd = jnp.concatenate([low[:LIVE2], high[:LIVE2]], axis=0)
    known = [both(low[64 + n : 65 + n], turn(high[64 + n : 65 + n])) for n in range(2)]
    ak, bq = pack_kq(kv[:, :HD], qd[:, :HD])
    av, bd = pack_vd(kv[:, HD:], qd[:, HD:])
    start = 64 * (meta[SEG_AT] - meta[SEG_AT] % 2)
    mask = iota((1024, 128), 0) <= iota((1024, 128), 1) + start
    top, total, delta3, p, dp = forward_core(ak, bq, av, bd, mask)
    lse3 = top + jnp.log(total)
    lse, delta = merge([tuple(known), (lse3, delta3)])
    at, qt, dk, dv = backward_core(p * jnp.exp(top - lse), dp, delta, ak, bq, av, bd)
    send[...] = both(fold(dk), fold(dv))
    aq = jnp.concatenate([at, qt], axis=0).T
    stats = (lse3, delta3, lse, delta)
    front = jnp.concatenate([aq[:LIVE2], *stats, jnp.zeros((4, 128), F32)], axis=0)
    rear = jnp.concatenate([aq[LIVE2:], *[turn(x) for x in stats], jnp.zeros((4, 128), F32)], axis=0)
    keep[...] = jnp.where(first, front, rear)
    back[...] = jnp.where(first, rear, front)


def by_head(meta, keep, back):
    first = meta[SEG_AT] % 2 == 0
    x, y = keep[...], back[...]
    return jnp.where(first, x, y), jnp.where(first, y, x)


def near_backward_kernel(meta, got, own, keep, back, out):
    far = by_head(meta, keep, back)
    sub, lane = iota((128, 128), 0), iota((128, 128), 1)
    diagonal = iota((8, 128), 0) == iota((8, 128), 1) // 8
    known = [both(stat_rows(got, n), turn(stat_rows(got, 2 + n))) for n in range(2)]
    third = [jnp.zeros((8, 128), F32), jnp.zeros((8, 128), F32)]
    covered = jnp.zeros((8, 128), jnp.bool_)
    l = iota((8, 128), 1)
    for e in range(2):
        live, shift = near_shift(meta, e)
        covered = covered | ((l // HD == e) & (l % 8 == shift) & live)
        place = (sub < 64) & (sub % 8 == lane % HD // 8) & (lane // HD == e)
        place = place.astype(F32)
        for n in range(2):
            x = jnp.where(diagonal, far[e][64 + n : 65 + n], 0.0)
            third[n] = third[n] + exact(x, place)
    lse, delta = merge(
        [
            tuple(known),
            (own[:, :128], own[:, 128:]),
            (jnp.where(covered, third[0], NEG), jnp.where(covered, third[1], 0.0)),
        ]
    )
    tail = ((sub < 64) & (lane == LIVE2 + sub % 8)).astype(F32)
    for e in range(2):
        for n, x in enumerate((lse, delta)):
            rest = exact(jnp.where(diagonal, far[e][66 + n : 67 + n], 0.0), tail)
            near = x if e == 0 else turn(x)
            out[pl.ds(STAT_AT + 2 * e + n, 8, stride=MESSAGE), :] = both(near, rest)
    ats, qts, dks, dvs = [], [], [], []
    for e, parts in enumerate(near_blocks(got)):
        results = []
        for j, (ak, bq, av, bd, mask) in enumerate(parts):
            at = slice(HD * e, HD * e + HD)
            lse_j = cat([lse[b : b + 1, at] for b in range(4 * j, 4 * j + 4)])
            delta_j = cat([delta[b : b + 1, at] for b in range(4 * j, 4 * j + 4)])
            p = jnp.exp(jnp.where(mask, nt(ak, bq), NEG) - lse_j)
            results.append(backward_core(p, nt(av, bd), delta_j, ak, bq, av, bd))
        ats.append(cat([results[0][0], results[1][0]]))
        qts.append(cat([results[0][1], results[1][1]]))
        for group, n in ((dks, 2), (dvs, 3)):
            x, y = results[0][n], results[1][n]
            group.append(jnp.concatenate([x + y[:256], y[256:]], axis=0))
    finals = (
        jnp.concatenate(ats, axis=0).T,
        jnp.concatenate(qts, axis=0).T,
        both(fold(dks[0]), fold(dks[1])),
        both(fold(dvs[0]), fold(dvs[1])),
    )
    for a, x in enumerate(finals):
        for b in range(8):
            at = MESSAGE * b + a * LIVE2
            out[at : at + LIVE2, :] = x[LIVE2 * b : LIVE2 * b + LIVE2]


def merge_kernel(meta, near, parts, keep, back, out):
    aq = by_head(meta, keep, back)
    kv = []
    for e in range(2):
        total = parts[64 * e : 64 * e + 64, :]
        for s in range(e + 2, 16, 2):
            total = total + parts[64 * s : 64 * s + 64, :]
        kv.append(total)
    aq = [x[:LIVE2] for x in aq]
    far = (
        both(aq[0], turn(aq[1])),
        both(turn(aq[0]), aq[1]),
        both(kv[0], turn(kv[1])),
        both(turn(kv[0]), kv[1]),
    )
    for b in range(8):
        base = MESSAGE * b
        out[base : base + FAR_AT, :] = near[base : base + FAR_AT, :]
        out[base + STAT_AT : base + MESSAGE, :] = near[base + STAT_AT : base + MESSAGE, :]
        for a, x in enumerate(far):
            out[base + FAR_AT + 8 * a : base + FAR_AT + 8 * a + 8, :] = x[8 * b : 8 * b + 8]


def outward(panel, out, sems, a, b):
    return pltpu.make_async_copy(panel.at[block(a, b), :], out.at[block(a, b), :], sems.at[6 * a + b])


def local_kernel(meta, q, k, v, d, out, panel, sems, result, out_sems):
    fetch((q, k, v, d), panel, sems)
    mask = iota((ROWS, ROWS), 0) <= iota((ROWS, ROWS), 1)
    row = iota((1, ROWS), 1)

    def step(b, carry):
        arrive((q, k, v, d), panel, sems, b)
        qp, kp, vp, dp = [panel[block(a, b), :] for a in range(4)]
        res = []
        for e in range(2):
            ak, bq = pack_kq(halves(kp, e), halves(qp, e))
            av, bd = pack_vd(halves(vp, e), halves(dp, e))
            _, total, delta, p, w = forward_core(ak, bq, av, bd, mask)
            h = 2 * b + e
            live = (row % R2 == meta[h]) | (row % R3 == meta[HEADS + h])
            p = p * jnp.where(live, 0.0, 1.0 / total)
            res.append(backward_core(p, w, delta, ak, bq, av, bd))
        result[block(0, b), :] = jnp.concatenate([res[0][0], res[1][0]], axis=0).T
        result[block(1, b), :] = jnp.concatenate([res[0][1], res[1][1]], axis=0).T
        result[block(2, b), :] = both(fold(res[0][2]), fold(res[1][2]))
        result[block(3, b), :] = both(fold(res[0][3]), fold(res[1][3]))
        for a in range(4):
            outward(result, out, out_sems, a, b).start()
        return carry

    lax.fori_loop(0, 6, step, 0)
    for b in range(6):
        for a in range(4):
            outward(result, out, out_sems, a, b).wait()


def close_kernel(meta, k, v, local, live, got, at_out, dq_out, dk_out, dv_out, kv, sems, panel, in_sems, out_sems):
    outs = (at_out, dq_out, dk_out, dv_out)
    for b in range(6):
        for copy in inward((k, v), kv, sems, b):
            copy.start()
        for a in range(4):
            outward(local, panel, in_sems, a, b).start()
    low2, low3 = half_mask(LIVE2), half_mask(LIVE3)

    def home(a, b, out):
        return pltpu.make_async_copy(
            panel.at[block(a, b), :], out.at[:, columns(b)], out_sems.at[6 * a + b]
        )

    def step(b, carry):
        arrive((k, v), kv, sems, b)
        kp, vp = kv[block(0, b), :], kv[block(1, b), :]
        pad = jnp.zeros((56, 128), F32)
        keep = pl.multiple_of(2 * PAIR * b, 8)
        qp, dp = [
            jnp.concatenate([live[pl.ds(keep + PAIR * n, PAIR), :], pad], axis=0) for n in range(2)
        ]
        base = pl.multiple_of(MESSAGE * b, 8)
        res = []
        for e in range(2):
            h = 2 * b + e
            near, far = meta[h], meta[HEADS + h]
            ak, bq = pack_kq(halves(kp, e), halves(qp, e))
            av, bd = pack_vd(halves(vp, e), halves(dp, e))
            mask = iota((ROWS, 128), 0) <= live_positions(near, far, far % R2 == near)
            lse = got[pl.ds(base + STAT_AT + 2 * e, 1), :]
            delta = got[pl.ds(base + STAT_AT + 2 * e + 1, 1), :]
            p = jnp.exp(jnp.where(mask, nt(ak, bq) - lse, NEG))
            res.append(backward_core(p, nt(av, bd), delta, ak, bq, av, bd))
        rows = [jnp.concatenate([res[0][n], res[1][n]], axis=0).T for n in range(2)]
        dense = [both(fold(res[0][n]), fold(res[1][n])) for n in (2, 3)]
        for a, out in enumerate(outs):
            outward(local, panel, in_sems, a, b).wait()
            near = got[pl.ds(base + LIVE2 * a, LIVE2), :]
            far = got[pl.ds(base + FAR_AT + LIVE3 * a, LIVE3), :]
            if a < 2:
                near = near + rows[a][:LIVE2]
                far = far + rows[a][LIVE2 : LIVE2 + LIVE3]
            else:
                panel[block(a, b), :] = panel[block(a, b), :] + dense[a - 2]
            at = ROWS * (6 * a + b)
            for e in range(2):
                spot = pl.ds(at + meta[2 * b + e], LIVE2, stride=R2)
                panel[spot, :] = panel[spot, :] + jnp.where(low2 if e == 0 else ~low2, near, 0.0)
                spot = pl.ds(at + meta[HEADS + 2 * b + e], LIVE3, stride=R3)
                panel[spot, :] = panel[spot, :] + jnp.where(low3 if e == 0 else ~low3, far, 0.0)
            home(a, b, out).start()
        return carry

    lax.fori_loop(0, 6, step, 0)
    for b in range(6):
        for a, out in enumerate(outs):
            home(a, b, out).wait()


SMEM = pl.BlockSpec(memory_space=pltpu.SMEM)
HBM = pl.BlockSpec(memory_space=pltpu.HBM)
VMEM = pl.BlockSpec(memory_space=pltpu.VMEM)
PANEL = pltpu.VMEM((24 * ROWS, 128), F32)
COPIES = pltpu.SemaphoreType.DMA((24,))


def call(kernel, name, outs, args, flops, mib, scratch=(), hbm=(), out_spec=VMEM):
    return pl.pallas_call(
        kernel,
        name=name,
        out_shape=[jax.ShapeDtypeStruct(x, F32) if isinstance(x, tuple) else x for x in outs],
        in_specs=[SMEM] + [HBM if i in hbm else VMEM for i in range(1, len(args))],
        out_specs=[out_spec] * len(outs),
        scratch_shapes=list(scratch),
        compiler_params=pltpu.CompilerParams(vmem_limit_bytes=mib * 1024 * 1024),
        cost_estimate=pl.CostEstimate(flops=flops, bytes_accessed=4_000_000, transcendentals=0),
    )(*args)


def in_hbm(x):
    return pltpu.with_memory_space_constraint(x, pltpu.HBM)


def swap(x, axis):
    return lax.all_to_all(x, axis, 0, 0, tiled=True)


def swap_cores(x):
    return lax.ppermute(x, "seg", [(s, s ^ 1) for s in range(lax.axis_size("seg"))])


def body(q, k, v, d, offsets):
    place = jnp.stack([lax.axis_index("seg"), lax.axis_index("blk")]).astype(jnp.int32)
    meta = jnp.concatenate([offsets.reshape(-1), place])
    rows = tuple(in_hbm(x) for x in (q, k, v, d))
    given = (1, 2, 3, 4)
    message, pair, far = (8 * MESSAGE, 128), (PAIR, 128), (1024, 128)
    send, live = call(
        open_kernel,
        "open",
        [message, (12 * PAIR, 128)],
        (offsets, *rows),
        3 * 10**9,
        16,
        [PANEL, COPIES],
        given,
    )
    got = swap(send, "blk")
    (keys,) = call(spread_kernel, "spread", [far], (meta, got), 10**8, 8)
    all_keys = swap(keys, "seg")
    own, mine, theirs = call(
        near_forward_kernel, "near_forward", [(8, 256), pair, pair], (meta, got), 4 * 10**9, 24
    )
    partner = swap_cores(theirs)
    parts, keep, back = call(
        far_kernel, "far", [far, pair, pair], (meta, all_keys, mine, partner), 4 * 10**9, 24
    )
    sums = swap(parts, "seg")
    back = swap_cores(back)
    (near,) = call(
        near_backward_kernel,
        "near_backward",
        [message],
        (meta, got, own, keep, back),
        8 * 10**9,
        24,
    )
    (reply,) = call(merge_kernel, "merge", [message], (meta, near, sums, keep, back), 10**8, 12)
    home = swap(reply, "blk")
    (local,) = call(
        local_kernel,
        "local",
        [pltpu.HBM((24 * ROWS, 128), F32)],
        (meta, *rows),
        16 * 10**9,
        24,
        [PANEL, COPIES, PANEL, COPIES],
        given,
        HBM,
    )
    return tuple(
        call(
            close_kernel,
            "close",
            [(ROWS, HEADS * HD)] * 4,
            (meta, rows[1], rows[2], in_hbm(local), live, home),
            6 * 10**9,
            24,
            [pltpu.VMEM((12 * ROWS, 128), F32), pltpu.SemaphoreType.DMA((12,)), PANEL, COPIES, COPIES],
            (1, 2, 3),
            HBM,
        )
    )


def solution(mesh):
    rows = P(ALL, None)
    return jax.shard_map(
        body,
        mesh=mesh,
        in_specs=(rows, rows, rows, rows, P()),
        out_specs=(rows, rows, rows, rows),
        check_vma=False,
    )
```

time: 115 us -> 104 us (0.904)
  blocking collectives: 16.1 us -> 0 us
  waiting for transfers between devices: 33.1 us -> 40.5 us
  local copies, waits for them, and re-layouts: 4.27 us -> 0.76 us
  Pallas kernels: 37.7 us -> 40.6 us
  starting transfers between devices: 22.2 us -> 20.3 us
    all_to_all x1 -> x0, blocking collectives: 16.1 us -> none  [swap_all(): lax.all_to_all(x.reshape(128, -1), ALL, 0, 0, tiled=True).reshape(-1, 128)]
    all_to_all x4, waiting for transfers between devices: 33.1 us -> 39.6 us  [swap(): return lax.all_to_all(x, axis, 0, 0, tiled=True)]
    unnamed x8 -> x4, local copies, waits for them, and re-layouts: 4.19 us -> 0.68 us
    pallas_call x9 -> x8, Pallas kernels: 37.7 us -> 40.6 us  [call(): pl.pallas_call(kernel, name=name, out_shape=[jax.ShapeDtypeStruct(x, F32)...]
    all_to_all x4, starting transfers between devices: 22.2 us -> 19.9 us  [swap(): return lax.all_to_all(x, axis, 0, 0, tiled=True)]
  transfers between devices with their start and end apart: 4 -> 6, of which waited for: 4 -> 5; matrix products, arithmetic and copies ran while one was open for 0% -> 0% of each run, Pallas kernels for 24% -> 18%
where the time goes in v3:
time: 104 us; the launch traced here: 103 us
  Pallas kernels  40.6 us (39%)
  waiting for transfers between devices  40.5 us (39%)
  starting transfers between devices  20.3 us (20%)
    pallas_call x8, Pallas kernels, call(): pl.pallas_call(kernel, name=name, out_shape=[jax.ShapeDtypeStruct(x, F32)...  40.6 us
    all_to_all x4, waiting for transfers between devices, swap(): return lax.all_to_all(x, axis, 0, 0, tiled=True)  39.6 us
    all_to_all x4, starting transfers between devices, swap(): return lax.all_to_all(x, axis, 0, 0, tiled=True)  19.9 us
  transfers between devices with their start and end apart: 6, of which 5 were waited for; matrix products, arithmetic and copies ran while one was open for 0% of the time, Pallas kernels for 18%

profile of v3, /device:TPU:0, one launch (start us, length us, event | category | flops | bytes accessed | tf_op | source)
XLA Modules:
  0.0 102.9 jit_solution(9548466153972483284)
XLA Ops:
  0.6 0.0 copy-start
  0.6 0.7 copy-done
  1.3 6.0 %open.1 = (f32[2368,128]{1,0:T(8,128)}, f32[864,128]{1,0:T(8,128)S(1)}) custom-call(s32[2,12]{1,0:T(2,128)S(1)} %copy-done, f32[256,768]{1,0:T(8,128)} %q.3, f32[256,768]{1,0:T(8,128)} %k.5, f32[256,768]{1,0:T(8,128)} %v.5, f32[256,768]{1,0:T(8,128)} %d.3), custom_call_target="tpu_custom_call" | custom-call | flops 3000000000 | bytes 4000000 | tf_op jit(solution)/shard_map/open/pallas_call | solution.py:492
  7.3 0.0 copy-start.1
  7.3 7.7 %all-to-all-start = ((f32[8,296,128]{2,1,0:T(8,128)}), f32[8,296,128]{2,1,0:T(8,128)S(1)}, u32[]{:S(2)}, u32[]{:S(2)}) async-start(f32[8,296,128]{2,1,0:T(8,128)} %bitcast.2), calls=%async_computation | async-start | bytes 2424832 | tf_op jit(solution)/shard_map/all_to_all | solution.py:509
  15.0 0.0 copy-done.1
  15.0 0.1 reshape.19
  15.1 0.1 pad_add_fusion.meta
  15.2 18.8 %all-to-all-done = f32[8,296,128]{2,1,0:T(8,128)S(1)} async-done(((f32[8,296,128]{2,1,0:T(8,128)}), f32[8,296,128]{2,1,0:T(8,128)S(1)}, u32[]{:S(2)}, u32[]{:S(2)}) %all-to-all-start) | async-done | bytes 1212448 | tf_op jit(solution)/shard_map/all_to_all | solution.py:509
  34.0 1.4 %spread.1 = f32[1024,128]{1,0:T(8,128)} custom-call(s32[26]{0:T(128)S(1)} %pad_add_fusion.meta, f32[2368,128]{1,0:T(8,128)S(1)} %bitcast.10), custom_call_target="tpu_custom_call" | custom-call | flops 100000000 | bytes 4000000 | tf_op jit(solution)/shard_map/spread/pallas_call | solution.py:492
  35.4 5.0 %all-to-all-start.1 = ((f32[16,64,128]{2,1,0:T(8,128)}), f32[16,64,128]{2,1,0:T(8,128)S(1)}, u32[]{:S(2)}, u32[]{:S(2)}) async-start(f32[16,64,128]{2,1,0:T(8,128)} %bitcast.4), calls=%async_computation.1 | async-start | bytes 1048576 | tf_op jit(solution)/shard_map/all_to_all | solution.py:509
  40.4 2.4 %near_forward.1 = (f32[8,256]{1,0:T(8,128)S(1)}, f32[72,128]{1,0:T(8,128)S(1)}, f32[72,128]{1,0:T(8,128)S(1)}) custom-call(s32[26]{0:T(128)S(1)} %pad_add_fusion.meta, f32[2368,128]{1,0:T(8,128)S(1)} %bitcast.11), custom_call_target="tpu_custom_call" | custom-call | flops 4000000000 | bytes 4000000 | tf_op jit(solution)/shard_map/near_forward/pallas_call | solution.py:492
  42.9 0.4 collective-permute-start
  43.3 0.9 collective-permute-done.pair
  44.1 7.2 %all-to-all-done.1 = f32[16,64,128]{2,1,0:T(8,128)S(1)} async-done(((f32[16,64,128]{2,1,0:T(8,128)}), f32[16,64,128]{2,1,0:T(8,128)S(1)}, u32[]{:S(2)}, u32[]{:S(2)}) %all-to-all-start.1) | async-done | bytes 524320 | tf_op jit(solution)/shard_map/all_to_all | solution.py:509
  51.3 2.8 %far.1 = (f32[1024,128]{1,0:T(8,128)}, f32[72,128]{1,0:T(8,128)S(1)}, f32[72,128]{1,0:T(8,128)S(1)}) custom-call(s32[26]{0:T(128)S(1)} %pad_add_fusion.meta, f32[1024,128]{1,0:T(8,128)S(1)} %bitcast.15, f32[72,128]{1,0:T(8,128)S(1)} %get-tuple-element.15.mine, f32[72,128]{1,0:T(8,128)S(1)} %collective-permute-done.pair), custom_call_target="tpu_custom_call" | custom-call | flops 4000000000 | bytes 4000000 | tf_op jit(solution)/shard_map/far/pallas_call | solution.py:492
  54.1 0.0 collective-permute-start.1
  54.1 3.6 %all-to-all-start.2 = ((f32[16,64,128]{2,1,0:T(8,128)}), f32[16,64,128]{2,1,0:T(8,128)S(1)}, u32[]{:S(2)}, u32[]{:S(2)}) async-start(f32[16,64,128]{2,1,0:T(8,128)} %bitcast.6), calls=%async_computation.2 | async-start | bytes 1048576 | tf_op jit(solution)/shard_map/all_to_all | solution.py:509
  57.7 0.0 collective-permute-done.1.back
  57.7 3.6 %near_backward.1.near = f32[2368,128]{1,0:T(8,128)S(1)} custom-call(s32[26]{0:T(128)S(1)} %pad_add_fusion.meta, f32[2368,128]{1,0:T(8,128)S(1)} %bitcast.12, f32[8,256]{1,0:T(8,128)S(1)} %get-tuple-element.14.own, f32[72,128]{1,0:T(8,128)S(1)} %get-tuple-element.17.keep, f32[72,128]{1,0:T(8,128)S(1)} %collective-permute-done.1.back), custom_call_target="tpu_custom_call" | custom-call | flops 8000000000 | bytes 4000000 | tf_op jit(solution)/shard_map/near_backward/pallas_call | solution.py:492
  61.3 7.2 %all-to-all-done.2 = f32[16,64,128]{2,1,0:T(8,128)S(1)} async-done(((f32[16,64,128]{2,1,0:T(8,128)}), f32[16,64,128]{2,1,0:T(8,128)S(1)}, u32[]{:S(2)}, u32[]{:S(2)}) %all-to-all-start.2) | async-done | bytes 524320 | tf_op jit(solution)/shard_map/all_to_all | solution.py:509
  68.5 1.7 %merge.1 = f32[2368,128]{1,0:T(8,128)} custom-call(s32[26]{0:T(128)S(1)} %pad_add_fusion.meta, f32[2368,128]{1,0:T(8,128)S(1)} %near_backward.1.near, f32[1024,128]{1,0:T(8,128)S(1)} %bitcast.13, f32[72,128]{1,0:T(8,128)S(1)} %get-tuple-element.17.keep, f32[72,128]{1,0:T(8,128)S(1)} %collective-permute-done.1.back), custom_call_target="tpu_custom_call" | custom-call | flops 100000000 | bytes 4000000 | tf_op jit(solution)/shard_map/merge/pallas_call | solution.py:492
  70.2 3.6 %all-to-all-start.3 = ((f32[8,296,128]{2,1,0:T(8,128)}), f32[8,296,128]{2,1,0:T(8,128)S(1)}, u32[]{:S(2)}, u32[]{:S(2)}) async-start(f32[8,296,128]{2,1,0:T(8,128)} %bitcast.8), calls=%async_computation.3 | async-start | bytes 2424832 | tf_op jit(solution)/shard_map/all_to_all | solution.py:509
  73.8 12.4 %local.1 = f32[6144,128]{1,0:T(8,128)} custom-call(s32[26]{0:T(128)S(1)} %pad_add_fusion.meta, f32[256,768]{1,0:T(8,128)} %q.3, f32[256,768]{1,0:T(8,128)} %k.5, f32[256,768]{1,0:T(8,128)} %v.5, f32[256,768]{1,0:T(8,128)} %d.3), custom_call_target="tpu_custom_call" | custom-call | flops 16000000000 | bytes 4000000 | tf_op jit(solution)/shard_map/local/pallas_call | solution.py:492
  86.2 6.4 %all-to-all-done.3 = f32[8,296,128]{2,1,0:T(8,128)S(1)} async-done(((f32[8,296,128]{2,1,0:T(8,128)}), f32[8,296,128]{2,1,0:T(8,128)S(1)}, u32[]{:S(2)}, u32[]{:S(2)}) %all-to-all-start.3) | async-done | bytes 1212448 | tf_op jit(solution)/shard_map/all_to_all | solution.py:509
  92.6 10.3 %close.1 = (f32[256,768]{1,0:T(8,128)}, f32[256,768]{1,0:T(8,128)}, f32[256,768]{1,0:T(8,128)}, f32[256,768]{1,0:T(8,128)}) custom-call(s32[26]{0:T(128)S(1)} %pad_add_fusion.meta, f32[256,768]{1,0:T(8,128)} %k.5, f32[256,768]{1,0:T(8,128)} %v.5, f32[6144,128]{1,0:T(8,128)} %local.1, f32[864,128]{1,0:T(8,128)S(1)} %get-tuple-element.12.live, ...), custom_call_target="tpu_custom_call" | custom-call | flops 6000000000 | bytes 4000000 | tf_op jit(solution)/shard_map/close/pallas_call | solution.py:492
Async XLA Ops:
  0.6 0.7 copy-start
  7.3 7.7 %copy-start.1 = (s32[2,12]{1,0:T(2,128)S(1)}, s32[2,12]{1,0:T(2,128)}, u32[]{:S(2)}) copy-start(s32[2,12]{1,0:T(2,128)} %offsets.1) | copy-start | bytes 292
  7.3 26.7 %all-to-all-start = ((f32[8,296,128]{2,1,0:T(8,128)}), f32[8,296,128]{2,1,0:T(8,128)S(1)}, u32[]{:S(2)}, u32[]{:S(2)}) async-start(f32[8,296,128]{2,1,0:T(8,128)} %bitcast.2), calls=%async_computation | async-start | bytes 2424832 | tf_op jit(solution)/shard_map/all_to_all | solution.py:509
  35.4 15.9 %all-to-all-start.1 = ((f32[16,64,128]{2,1,0:T(8,128)}), f32[16,64,128]{2,1,0:T(8,128)S(1)}, u32[]{:S(2)}, u32[]{:S(2)}) async-start(f32[16,64,128]{2,1,0:T(8,128)} %bitcast.4), calls=%async_computation.1 | async-start | bytes 1048576 | tf_op jit(solution)/shard_map/all_to_all | solution.py:509
  42.9 1.3 %collective-permute-start = (f32[72,128]{1,0:T(8,128)S(1)}, f32[72,128]{1,0:T(8,128)S(1)}, u32[]{:S(2)}, u32[]{:S(2)}) collective-permute-start(f32[72,128]{1,0:T(8,128)S(1)} %get-tuple-element.16), channel_id=1, source_target_pairs={{0,8},{8,0},{16,24},{24,16},{32,40},{40,32},{48,56},{56,48},{64,72... | collective-permute-start | bytes 110600 | tf_op jit(solution)/shard_map/ppermute | solution.py:513
  54.1 3.6 %collective-permute-start.1 = (f32[72,128]{1,0:T(8,128)S(1)}, f32[72,128]{1,0:T(8,128)S(1)}, u32[]{:S(2)}, u32[]{:S(2)}) collective-permute-start(f32[72,128]{1,0:T(8,128)S(1)} %get-tuple-element.18), channel_id=1, source_target_pairs={{0,8},{8,0},{16,24},{24,16},{32,40},{40,32},{48,56},{56,48},{64,72... | collective-permute-start | bytes 110600 | tf_op jit(solution)/shard_map/ppermute | solution.py:513
  54.1 14.4 %all-to-all-start.2 = ((f32[16,64,128]{2,1,0:T(8,128)}), f32[16,64,128]{2,1,0:T(8,128)S(1)}, u32[]{:S(2)}, u32[]{:S(2)}) async-start(f32[16,64,128]{2,1,0:T(8,128)} %bitcast.6), calls=%async_computation.2 | async-start | bytes 1048576 | tf_op jit(solution)/shard_map/all_to_all | solution.py:509
  70.2 22.4 %all-to-all-start.3 = ((f32[8,296,128]{2,1,0:T(8,128)}), f32[8,296,128]{2,1,0:T(8,128)S(1)}, u32[]{:S(2)}, u32[]{:S(2)}) async-start(f32[8,296,128]{2,1,0:T(8,128)} %bitcast.8), calls=%async_computation.3 | async-start | bytes 2424832 | tf_op jit(solution)/shard_map/all_to_all | solution.py:509

commit v4 on v3

--- a/solution.py
+++ b/solution.py
@@ -145,11 +145,52 @@
         copy.wait()
 
 
-def live_positions(near, far, skip_far=False):
+def near_positions(meta, b):
     lane = iota((1, 128), 1)
-    spot = jnp.where(lane < LIVE2, R2 * lane + near, R3 * (lane - LIVE2) + far)
-    end = jnp.where(skip_far, LIVE2, LIVE2 + LIVE3)
-    return jnp.where(lane < end, spot, -1)
+    return R2 * (lane % LIVE2) + jnp.where(lane < LIVE2, meta[2 * b], meta[2 * b + 1])
+
+
+def far_positions(meta, alone):
+    lane = iota((1, 128), 1)
+    spot = jnp.full((1, 128), -1, jnp.int32)
+    for h in range(HEADS):
+        near, far = meta[h], meta[HEADS + h]
+        start = jnp.where(far % R2 == near, -1, far) if alone else far
+        here = lane // LIVE3 == h
+        spot = jnp.where(here & (start >= 0), start + R3 * (lane % LIVE3), spot)
+    return spot
+
+
+def apart(x):
+    low = half_mask(x.shape[0])
+    return [jnp.where(low, x, 0.0), jnp.where(low, 0.0, x)]
+
+
+def live_block(near, far, b):
+    parts = apart(near)
+    if b:
+        parts.append(jnp.zeros((16 * b, 128), F32))
+    parts += apart(far)
+    parts.append(jnp.zeros((112 - 16 * b, 128), F32))
+    return jnp.concatenate(parts, axis=0)
+
+
+def live_products(k, v, q, d):
+    k0, k1, k2 = split3(k)
+    q0, q1, q2 = split3(q * SCALE)
+    v0, v1 = split2(v)
+    d0, d1 = split2(d)
+    s = nt(cat([k0, k1, k0, k1, k0, k2]), cat([q0, q1, q1, q0, q2, q0]))
+    return s, nt(cat([v0, v1, v0, v1]), cat([d0, d1, d1, d0]))
+
+
+def live_forward(s, dp, spot):
+    s = jnp.where(iota((ROWS, 128), 0) <= spot, s, NEG)
+    top = jnp.max(s, axis=0, keepdims=True)
+    p = jnp.exp(s - top)
+    total = jnp.sum(p, axis=0, keepdims=True)
+    delta = jnp.sum(p * dp, axis=0, keepdims=True) / total
+    return top + jnp.log(total), delta, p / total
 
 
 def halves(x, e):
@@ -160,45 +201,121 @@
     return pltpu.roll(x, HD, 1)
 
 
-def open_kernel(offsets, q, k, v, d, send, live, panel, sems):
+class Flat:
+    def __init__(self, ref):
+        self.ref = ref
+
+    def __getitem__(self, i):
+        return self.ref[i // HEADS, i % HEADS]
+
+
+def open_kernel(offsets, q, k, v, d, out, live, panel, sems, send, out_sems, shifts, shift_sem):
+    shifting = pltpu.make_async_copy(offsets, shifts, shift_sem)
+    shifting.start()
     fetch((q, k, v, d), panel, sems)
-
-    def step(b, carry):
+    shifting.wait()
+    meta = Flat(shifts)
+    copies, rows = [], []
+
+    def leave(at, count):
+        at = pl.ds(at, count)
+        copies.append(pltpu.make_async_copy(send.at[at, :], out.at[at, :], out_sems.at[len(copies)]))
+        copies[-1].start()
+
+    for b in range(6):
         arrive((q, k, v, d), panel, sems, b)
-        out = pl.multiple_of(MESSAGE * b, 8)
-        rows = []
+        at = MESSAGE * b
+        found = []
         for a in range(4):
             base = ROWS * (6 * a + b)
             near = both(
-                panel[pl.ds(base + offsets[0, 2 * b], LIVE2, stride=R2), :],
-                panel[pl.ds(base + offsets[0, 2 * b + 1], LIVE2, stride=R2), :],
+                panel[pl.ds(base + meta[2 * b], LIVE2, stride=R2), :],
+                panel[pl.ds(base + meta[2 * b + 1], LIVE2, stride=R2), :],
             )
             far = both(
-                panel[pl.ds(base + offsets[1, 2 * b], LIVE3, stride=R3), :],
-                panel[pl.ds(base + offsets[1, 2 * b + 1], LIVE3, stride=R3), :],
+                panel[pl.ds(base + meta[HEADS + 2 * b], LIVE3, stride=R3), :],
+                panel[pl.ds(base + meta[HEADS + 2 * b + 1], LIVE3, stride=R3), :],
             )
-            send[pl.ds(out + LIVE2 * a, LIVE2), :] = near
-            send[pl.ds(out + FAR_AT + LIVE3 * a, LIVE3), :] = far
-            rows.append((near, far))
-        pad = jnp.zeros((56, 128), F32)
-        keep = pl.multiple_of(2 * PAIR * b, 8)
-        queries, grads = [], []
-        for n, (a, group) in enumerate(((0, queries), (3, grads))):
-            near, far = rows[a]
-            live[pl.ds(keep + PAIR * n, LIVE2), :] = near
-            live[pl.ds(keep + PAIR * n + LIVE2, LIVE3), :] = far
-            group.append(jnp.concatenate([near, far, pad], axis=0))
-        kp, vp = panel[block(1, b), :], panel[block(2, b), :]
-        for e in range(2):
-            ak, bq = pack_kq(halves(kp, e), halves(queries[0], e))
-            av, bd = pack_vd(halves(vp, e), halves(grads[0], e))
-            spot = live_positions(offsets[0, 2 * b + e], offsets[1, 2 * b + e])
-            top, total, delta, _, _ = forward_core(ak, bq, av, bd, iota((ROWS, 128), 0) <= spot)
-            send[pl.ds(out + STAT_AT + 2 * e, 1), :] = top + jnp.log(total)
-            send[pl.ds(out + STAT_AT + 2 * e + 1, 1), :] = delta
-        return carry
-
-    lax.fori_loop(0, 6, step, 0)
+            send[at + LIVE2 * a : at + LIVE2 * a + LIVE2, :] = near
+            send[at + FAR_AT + LIVE3 * a : at + FAR_AT + LIVE3 * a + LIVE3, :] = far
+            found.append((near, far))
+        leave(at, STAT_AT)
+        for n, (near, far) in enumerate((found[0], found[3])):
+            keep = PAIR * (2 * b + n)
+            live[keep : keep + LIVE2, :] = near
+            live[keep + LIVE2 : keep + PAIR, :] = far
+        rows.append((found[0], found[3]))
+    far_s = far_dp = jnp.zeros((ROWS, 128), F32)
+    known = []
+    for b in range(6):
+        s, dp = live_products(
+            panel[block(1, b), :],
+            panel[block(2, b), :],
+            live_block(*rows[b][0], b),
+            live_block(*rows[b][1], b),
+        )
+        far_s, far_dp = far_s + s[:, 128:], far_dp + dp[:, 128:]
+        known.append(live_forward(s[:, :128], dp[:, :128], near_positions(meta, b))[:2])
+    far = live_forward(far_s, far_dp, far_positions(meta, False))[:2]
+    for b in range(6):
+        at = MESSAGE * b + STAT_AT
+        turned = [pltpu.roll(x, (128 - 16 * b) % 128, 1) for x in far]
+        send[at : at + 8, :] = jnp.concatenate([*known[b], *turned, jnp.zeros((4, 128), F32)], axis=0)
+        leave(at, 8)
+    for copy in copies:
+        copy.wait()
+
+
+def live_kernel(meta, k, v, live, weights, slopes, out_rows, stats, panel, sems, kept, rows_kept, out_sems):
+    fetch((k, v), panel, sems)
+    stats[...] = jnp.zeros_like(stats)
+    far_s = far_dp = jnp.zeros((ROWS, 128), F32)
+    copies = []
+
+    def record(n, s, dp, spot):
+        lse, delta, p = live_forward(s, dp, spot)
+        pair = cat(split2(p)), cat(split2(p * (dp - delta)))
+        for m, (x, out) in enumerate(zip(pair, (weights, slopes))):
+            at = pl.ds(ROWS * n, ROWS)
+            kept[m, at, :] = x
+            copies.append(pltpu.make_async_copy(kept.at[m, at, :], out.at[at, :], out_sems.at[7 * m + n]))
+            copies[-1].start()
+        stats[n : n + 1, :] = lse
+        stats[8 + n : 9 + n, :] = delta
+        return pair
+
+    def products(b, p, h):
+        kb, vb = cat(split2(panel[block(0, b), :] * SCALE)), cat(split2(panel[block(1, b), :]))
+        both_sides = tn(p, cat([vb, kb]))
+        for n, x in enumerate((both_sides[:, :256], tn(h, kb), both_sides[:, 256:])):
+            yield 6 * PAIR * n + PAIR * b, x[:128, :128] + x[:128, 128:] + x[128:, :128] + x[128:, 128:]
+
+    for b in range(6):
+        arrive((k, v), panel, sems, b)
+    for b in range(6):
+        rows = []
+        for n in range(2):
+            keep = PAIR * (2 * b + n)
+            rows.append((live[keep : keep + LIVE2, :], live[keep + LIVE2 : keep + PAIR, :]))
+        s, dp = live_products(
+            panel[block(0, b), :],
+            panel[block(1, b), :],
+            live_block(*rows[0], b),
+            live_block(*rows[1], b),
+        )
+        far_s, far_dp = far_s + s[:, 128:], far_dp + dp[:, 128:]
+        p, h = record(b, s[:, :128], dp[:, :128], near_positions(meta, b))
+        for at, x in products(b, p, h):
+            rows_kept[at : at + LIVE2, :] = both(x[:LIVE2], x[LIVE2:])
+    p, h = record(6, far_s, far_dp, far_positions(meta, True))
+    for b in range(6):
+        for at, x in products(b, p, h):
+            low, high = x[16 * b : 16 * b + 8], x[16 * b + 8 : 16 * b + 16]
+            rows_kept[at + LIVE2 : at + PAIR, :] = both(low, high)
+    copies.append(pltpu.make_async_copy(rows_kept, out_rows, out_sems.at[14]))
+    copies[-1].start()
+    for copy in copies:
+        copy.wait()
 
 
 def gather_rows(ref, at, count):
@@ -211,11 +328,18 @@
     return ref[pl.ds(STAT_AT + n, 8, stride=MESSAGE), :]
 
 
-def spread_kernel(meta, got, send):
+def spread_kernel(meta, got, out, kv, sems):
     k, v = gather_rows(got, FAR_AT + 8, 8), gather_rows(got, FAR_AT + 16, 8)
-    kv = both(k, turn(v)), both(turn(k), v)
-    for s in range(16):
-        send[64 * s : 64 * s + 64, :] = kv[s % 2]
+    kv[0] = both(k, turn(v))
+    kv[1] = both(turn(k), v)
+    copies = [
+        pltpu.make_async_copy(kv.at[s % 2], out.at[pl.ds(64 * s, 64), :], sems.at[s])
+        for s in range(16)
+    ]
+    for copy in copies:
+        copy.start()
+    for copy in copies:
+        copy.wait()
 
 
 def near_shift(meta, e):
@@ -265,7 +389,7 @@
         pick = pick.astype(F32)
         merged = merge(
             [
-                (turn(stat_rows(got, 2 * e)), turn(stat_rows(got, 2 * e + 1))),
+                tuple(pltpu.roll(stat_rows(got, 2 + n), 120 * e, 1) for n in range(2)),
                 (jnp.where(live, exact(lse, pick), NEG), exact(delta, pick)),
             ]
         )
@@ -312,7 +436,7 @@
     far = by_head(meta, keep, back)
     sub, lane = iota((128, 128), 0), iota((128, 128), 1)
     diagonal = iota((8, 128), 0) == iota((8, 128), 1) // 8
-    known = [both(stat_rows(got, n), turn(stat_rows(got, 2 + n))) for n in range(2)]
+    known = [stat_rows(got, n) for n in range(2)]
     third = [jnp.zeros((8, 128), F32), jnp.zeros((8, 128), F32)]
     covered = jnp.zeros((8, 128), jnp.bool_)
     l = iota((8, 128), 1)
@@ -331,12 +455,13 @@
             (jnp.where(covered, third[0], NEG), jnp.where(covered, third[1], 0.0)),
         ]
     )
-    tail = ((sub < 64) & (lane == LIVE2 + sub % 8)).astype(F32)
-    for e in range(2):
-        for n, x in enumerate((lse, delta)):
-            rest = exact(jnp.where(diagonal, far[e][66 + n : 67 + n], 0.0), tail)
-            near = x if e == 0 else turn(x)
-            out[pl.ds(STAT_AT + 2 * e + n, 8, stride=MESSAGE), :] = both(near, rest)
+    for n, x in enumerate((lse, delta)):
+        rest = jnp.zeros((8, 128), F32)
+        for e in range(2):
+            tail = ((sub < 64) & (lane == LIVE3 * e + sub % 8)).astype(F32)
+            rest = rest + exact(jnp.where(diagonal, far[e][66 + n : 67 + n], 0.0), tail)
+        out[pl.ds(STAT_AT + n, 8, stride=MESSAGE), :] = x
+        out[pl.ds(STAT_AT + 2 + n, 8, stride=MESSAGE), :] = rest
     ats, qts, dks, dvs = [], [], [], []
     for e, parts in enumerate(near_blocks(got)):
         results = []
@@ -386,11 +511,7 @@
             out[base + FAR_AT + 8 * a : base + FAR_AT + 8 * a + 8, :] = x[8 * b : 8 * b + 8]
 
 
-def outward(panel, out, sems, a, b):
-    return pltpu.make_async_copy(panel.at[block(a, b), :], out.at[block(a, b), :], sems.at[6 * a + b])
-
-
-def local_kernel(meta, q, k, v, d, out, panel, sems, result, out_sems):
+def local_kernel(meta, q, k, v, d, at_out, dq_out, dk_out, dv_out, panel, sems):
     fetch((q, k, v, d), panel, sems)
     mask = iota((ROWS, ROWS), 0) <= iota((ROWS, ROWS), 1)
     row = iota((1, ROWS), 1)
@@ -407,78 +528,103 @@
             live = (row % R2 == meta[h]) | (row % R3 == meta[HEADS + h])
             p = p * jnp.where(live, 0.0, 1.0 / total)
             res.append(backward_core(p, w, delta, ak, bq, av, bd))
-        result[block(0, b), :] = jnp.concatenate([res[0][0], res[1][0]], axis=0).T
-        result[block(1, b), :] = jnp.concatenate([res[0][1], res[1][1]], axis=0).T
-        result[block(2, b), :] = both(fold(res[0][2]), fold(res[1][2]))
-        result[block(3, b), :] = both(fold(res[0][3]), fold(res[1][3]))
-        for a in range(4):
-            outward(result, out, out_sems, a, b).start()
+        at_out[block(0, b), :] = jnp.concatenate([res[0][0], res[1][0]], axis=0).T
+        dq_out[block(0, b), :] = jnp.concatenate([res[0][1], res[1][1]], axis=0).T
+        dk_out[block(0, b), :] = both(fold(res[0][2]), fold(res[1][2]))
+        dv_out[block(0, b), :] = both(fold(res[0][3]), fold(res[1][3]))
         return carry
 
     lax.fori_loop(0, 6, step, 0)
+
+
+def close_kernel(
+    meta, at1, dq1, dk1, dv1, live, weights, slopes, products, stats, got,
+    at_out, dq_out, dk_out, dv_out, panel, sems, held, held_sem,
+):
+    coming = pltpu.make_async_copy(products, held, held_sem)
+    coming.start()
+    outs, local = (at_out, dq_out, dk_out, dv_out), (at1, dq1, dk1, dv1)
+    first = iota((1, 128), 1) < 16
+    far = [jnp.zeros((1, 128), F32), jnp.zeros((1, 128), F32)]
+    scales, shifts = [], []
+    for b in range(7):
+        if b < 6:
+            at = MESSAGE * b + STAT_AT
+            lse, delta = got[at : at + 1, :], got[at + 1 : at + 2, :]
+            for n in range(2):
+                x = jnp.where(first, got[at + 2 + n : at + 3 + n, :], 0.0)
+                far[n] = far[n] + pltpu.roll(x, 16 * b, 1)
+        else:
+            lse, delta = far
+        scales.append(jnp.exp(stats[b : b + 1, :] - lse))
+        shifts.append(delta - stats[8 + b : 9 + b, :])
+    zero = jnp.zeros((1, 128), F32)
+    table = jnp.concatenate([*scales, zero, *shifts, zero], axis=0).T
+    low2, low3 = half_mask(LIVE2), half_mask(LIVE3)
+    far_p, far_h = weights[6 * ROWS :, :], slopes[6 * ROWS :, :]
+    copies = []
     for b in range(6):
-        for a in range(4):
-            outward(result, out, out_sems, a, b).wait()
-
-
-def close_kernel(meta, k, v, local, live, got, at_out, dq_out, dk_out, dv_out, kv, sems, panel, in_sems, out_sems):
-    outs = (at_out, dq_out, dk_out, dv_out)
-    for b in range(6):
-        for copy in inward((k, v), kv, sems, b):
-            copy.start()
-        for a in range(4):
-            outward(local, panel, in_sems, a, b).start()
-    low2, low3 = half_mask(LIVE2), half_mask(LIVE3)
-
-    def home(a, b, out):
-        return pltpu.make_async_copy(
-            panel.at[block(a, b), :], out.at[:, columns(b)], out_sems.at[6 * a + b]
-        )
-
-    def step(b, carry):
-        arrive((k, v), kv, sems, b)
-        kp, vp = kv[block(0, b), :], kv[block(1, b), :]
-        pad = jnp.zeros((56, 128), F32)
-        keep = pl.multiple_of(2 * PAIR * b, 8)
-        qp, dp = [
-            jnp.concatenate([live[pl.ds(keep + PAIR * n, PAIR), :], pad], axis=0) for n in range(2)
+        rows = []
+        for n in range(2):
+            keep = PAIR * (2 * b + n)
+            rows.append((live[keep : keep + LIVE2, :], live[keep + LIVE2 : keep + PAIR, :]))
+        scale = jnp.concatenate([table[:, b : b + 1], table[:, 6:7]], axis=0)
+        shift = jnp.concatenate([table[:, 8 + b : 9 + b], table[:, 14:15]], axis=0)
+        d = live_block(*rows[1], b) * scale
+        q = live_block(*rows[0], b) * (scale * SCALE)
+        d, q, t = [cat(split2(x)) for x in (d, q, q * (-shift))]
+        own_p, own_h = weights[ROWS * b : ROWS * b + ROWS, :], slopes[ROWS * b : ROWS * b + ROWS, :]
+        dense = [jnp.zeros((ROWS, 256), F32), jnp.zeros((ROWS, 256), F32)]
+        for n in range(2):
+            at = slice(128 * n, 128 * n + 128)
+            p, h = cat([own_p[:, at], far_p[:, at]]), cat([own_h[:, at], far_h[:, at]])
+            dense[0] = dense[0] + nn(h, q) + nn(p, t)
+            dense[1] = dense[1] + nn(p, d)
+        spread = [
+            (
+                jnp.where(low2, table[:LIVE2, n + b : n + b + 1], table[LIVE2:, n + b : n + b + 1]),
+                jnp.where(
+                    low3,
+                    table[16 * b : 16 * b + 8, n + 6 : n + 7],
+                    table[16 * b + 8 : 16 * b + 16, n + 6 : n + 7],
+                ),
+            )
+            for n in (0, 8)
         ]
-        base = pl.multiple_of(MESSAGE * b, 8)
-        res = []
-        for e in range(2):
-            h = 2 * b + e
-            near, far = meta[h], meta[HEADS + h]
-            ak, bq = pack_kq(halves(kp, e), halves(qp, e))
-            av, bd = pack_vd(halves(vp, e), halves(dp, e))
-            mask = iota((ROWS, 128), 0) <= live_positions(near, far, far % R2 == near)
-            lse = got[pl.ds(base + STAT_AT + 2 * e, 1), :]
-            delta = got[pl.ds(base + STAT_AT + 2 * e + 1, 1), :]
-            p = jnp.exp(jnp.where(mask, nt(ak, bq) - lse, NEG))
-            res.append(backward_core(p, nt(av, bd), delta, ak, bq, av, bd))
-        rows = [jnp.concatenate([res[0][n], res[1][n]], axis=0).T for n in range(2)]
-        dense = [both(fold(res[0][n]), fold(res[1][n])) for n in (2, 3)]
-        for a, out in enumerate(outs):
-            outward(local, panel, in_sems, a, b).wait()
-            near = got[pl.ds(base + LIVE2 * a, LIVE2), :]
-            far = got[pl.ds(base + FAR_AT + LIVE3 * a, LIVE3), :]
-            if a < 2:
-                near = near + rows[a][:LIVE2]
-                far = far + rows[a][LIVE2 : LIVE2 + LIVE3]
+        for a in (2, 3, 0, 1):
+            if b == 0 and a == 0:
+                coming.wait()
+            at = MESSAGE * b + LIVE2 * a
+            near = got[at : at + LIVE2, :]
+            at = MESSAGE * b + FAR_AT + LIVE3 * a
+            far = got[at : at + LIVE3, :]
+            base = ROWS * (6 * a + b)
+            kept = local[a][ROWS * b : ROWS * b + ROWS, :]
+            if a == 0:
+                z = held[PAIR * b : PAIR * b + PAIR, :]
+                near = near + spread[0][0] * z[:LIVE2]
+                far = far + spread[0][1] * z[LIVE2:]
+            elif a == 1:
+                x, y = [held[PAIR * (6 * n + b) : PAIR * (6 * n + b + 1), :] for n in (1, 2)]
+                near = near + spread[0][0] * (x[:LIVE2] - spread[1][0] * y[:LIVE2])
+                far = far + spread[0][1] * (x[LIVE2:] - spread[1][1] * y[LIVE2:])
             else:
-                panel[block(a, b), :] = panel[block(a, b), :] + dense[a - 2]
-            at = ROWS * (6 * a + b)
+                x = dense[a - 2]
+                kept = kept + (x[:, :128] + x[:, 128:])
+            panel[base : base + ROWS, :] = kept
             for e in range(2):
-                spot = pl.ds(at + meta[2 * b + e], LIVE2, stride=R2)
+                spot = pl.ds(base + meta[2 * b + e], LIVE2, stride=R2)
                 panel[spot, :] = panel[spot, :] + jnp.where(low2 if e == 0 else ~low2, near, 0.0)
-                spot = pl.ds(at + meta[HEADS + 2 * b + e], LIVE3, stride=R3)
+                spot = pl.ds(base + meta[HEADS + 2 * b + e], LIVE3, stride=R3)
                 panel[spot, :] = panel[spot, :] + jnp.where(low3 if e == 0 else ~low3, far, 0.0)
-            home(a, b, out).start()
-        return carry
-
-    lax.fori_loop(0, 6, step, 0)
-    for b in range(6):
-        for a, out in enumerate(outs):
-            home(a, b, out).wait()
+            copies.append(
+                pltpu.make_async_copy(
+                    panel.at[block(a, b), :], outs[a].at[:, columns(b)], sems.at[6 * a + b]
+                )
+            )
+            copies[-1].start()
+    for copy in copies:
+        copy.wait()
 
 
 SMEM = pl.BlockSpec(memory_space=pltpu.SMEM)
@@ -493,11 +639,11 @@
         kernel,
         name=name,
         out_shape=[jax.ShapeDtypeStruct(x, F32) if isinstance(x, tuple) else x for x in outs],
-        in_specs=[SMEM] + [HBM if i in hbm else VMEM for i in range(1, len(args))],
-        out_specs=[out_spec] * len(outs),
+        in_specs=[HBM if i in hbm else VMEM if i else SMEM for i in range(len(args))],
+        out_specs=out_spec if isinstance(out_spec, list) else [out_spec] * len(outs),
         scratch_shapes=list(scratch),
         compiler_params=pltpu.CompilerParams(vmem_limit_bytes=mib * 1024 * 1024),
-        cost_estimate=pl.CostEstimate(flops=flops, bytes_accessed=4_000_000, transcendentals=0),
+        cost_estimate=pl.CostEstimate(flops=flops, bytes_accessed=100_000, transcendentals=0),
     )(*args)
 
 
@@ -522,22 +668,69 @@
     send, live = call(
         open_kernel,
         "open",
-        [message, (12 * PAIR, 128)],
-        (offsets, *rows),
-        3 * 10**9,
+        [pltpu.HBM(message, F32), (12 * PAIR, 128)],
+        (in_hbm(offsets), *rows),
+        10**8,
         16,
+        [
+            PANEL,
+            COPIES,
+            pltpu.VMEM(message, F32),
+            pltpu.SemaphoreType.DMA((12,)),
+            pltpu.SMEM((2, HEADS), jnp.int32),
+            pltpu.SemaphoreType.DMA,
+        ],
+        (0, *given),
+        [HBM, VMEM],
+    )
+    got = swap(send, "blk")
+    local = call(
+        local_kernel,
+        "local",
+        [(6 * ROWS, 128)] * 4,
+        (meta, *rows),
+        10**8,
+        24,
         [PANEL, COPIES],
         given,
     )
-    got = swap(send, "blk")
-    (keys,) = call(spread_kernel, "spread", [far], (meta, got), 10**8, 8)
+    got, *local = lax.optimization_barrier((got, *local))
+    (keys,) = call(
+        spread_kernel,
+        "spread",
+        [pltpu.HBM(far, F32)],
+        (meta, got),
+        10**8,
+        8,
+        [pltpu.VMEM((2, 64, 128), F32), pltpu.SemaphoreType.DMA((16,))],
+        out_spec=HBM,
+    )
     all_keys = swap(keys, "seg")
     own, mine, theirs = call(
-        near_forward_kernel, "near_forward", [(8, 256), pair, pair], (meta, got), 4 * 10**9, 24
-    )
+        near_forward_kernel, "near_forward", [(8, 256), pair, pair], (meta, got), 10**8, 24
+    )
+    rest = call(
+        live_kernel,
+        "live",
+        [pltpu.HBM((7 * ROWS, 256), BF)] * 2 + [pltpu.HBM((18 * PAIR, 128), F32), (16, 128)],
+        (meta, rows[1], rows[2], live),
+        10**8,
+        16,
+        [
+            pltpu.VMEM((12 * ROWS, 128), F32),
+            pltpu.SemaphoreType.DMA((12,)),
+            pltpu.VMEM((2, 7 * ROWS, 256), BF),
+            pltpu.VMEM((18 * PAIR, 128), F32),
+            pltpu.SemaphoreType.DMA((15,)),
+        ],
+        (1, 2),
+        [HBM] * 3 + [VMEM],
+    )
+    all_keys, *rest = lax.optimization_barrier((all_keys, *rest))
+    rest[2] = in_hbm(rest[2])
     partner = swap_cores(theirs)
     parts, keep, back = call(
-        far_kernel, "far", [far, pair, pair], (meta, all_keys, mine, partner), 4 * 10**9, 24
+        far_kernel, "far", [far, pair, pair], (meta, all_keys, mine, partner), 10**8, 24
     )
     sums = swap(parts, "seg")
     back = swap_cores(back)
@@ -546,32 +739,21 @@
         "near_backward",
         [message],
         (meta, got, own, keep, back),
-        8 * 10**9,
+        10**8,
         24,
     )
     (reply,) = call(merge_kernel, "merge", [message], (meta, near, sums, keep, back), 10**8, 12)
     home = swap(reply, "blk")
-    (local,) = call(
-        local_kernel,
-        "local",
-        [pltpu.HBM((24 * ROWS, 128), F32)],
-        (meta, *rows),
-        16 * 10**9,
-        24,
-        [PANEL, COPIES, PANEL, COPIES],
-        given,
-        HBM,
-    )
     return tuple(
         call(
             close_kernel,
             "close",
             [(ROWS, HEADS * HD)] * 4,
-            (meta, rows[1], rows[2], in_hbm(local), live, home),
-            6 * 10**9,
-            24,
-            [pltpu.VMEM((12 * ROWS, 128), F32), pltpu.SemaphoreType.DMA((12,)), PANEL, COPIES, COPIES],
-            (1, 2, 3),
+            (meta, *local, live, *rest, home),
+            10**8,
+            16,
+            [PANEL, COPIES, pltpu.VMEM((18 * PAIR, 128), F32), pltpu.SemaphoreType.DMA],
+            (8,),
             HBM,
         )
     )

time: 104 us -> 95.6 us (0.919)
  waiting for transfers between devices: 40.5 us -> 12.4 us
  blocking collectives: 0 us -> 22 us
  starting transfers between devices: 20.3 us -> 18.3 us
  local copies, waits for them, and re-layouts: 0.76 us -> 2.75 us
  Pallas kernels: 40.6 us -> 38.7 us
    all_to_all x4 -> x3, waiting for transfers between devices: 39.6 us -> 11.4 us  [swap(): return lax.all_to_all(x, axis, 0, 0, tiled=True)]
    all_to_all x0 -> x1, blocking collectives: none -> 22 us  [swap(): return lax.all_to_all(x, axis, 0, 0, tiled=True)]
    all_to_all x4 -> x3, starting transfers between devices: 19.9 us -> 17.5 us  [swap(): return lax.all_to_all(x, axis, 0, 0, tiled=True)]
    unnamed x4 -> x22, local copies, waits for them, and re-layouts: 0.68 us -> 2.66 us
    pallas_call x8 -> x9, Pallas kernels: 40.6 us -> 38.7 us  [call(): pl.pallas_call(kernel, name=name, out_shape=[jax.ShapeDtypeStruct(x, F32)...]
  transfers between devices with their start and end apart: 6 -> 5, of which waited for: 5 -> 4; matrix products, arithmetic and copies ran while one was open for 0% -> 0% of each run, Pallas kernels for 18% -> 26%
where the time goes in v4:
time: 95.6 us; the launch traced here: 95.1 us
  Pallas kernels  38.7 us (40%)
  blocking collectives  22 us (23%)
  starting transfers between devices  18.3 us (19%)
  waiting for transfers between devices  12.4 us (13%)
  local copies, waits for them, and re-layouts  2.75 us (3%)
    pallas_call x9, Pallas kernels, call(): pl.pallas_call(kernel, name=name, out_shape=[jax.ShapeDtypeStruct(x, F32)...  38.7 us
    all_to_all x1, blocking collectives, swap(): return lax.all_to_all(x, axis, 0, 0, tiled=True)  22 us
    all_to_all x3, starting transfers between devices, swap(): return lax.all_to_all(x, axis, 0, 0, tiled=True)  17.5 us
    all_to_all x3, waiting for transfers between devices, swap(): return lax.all_to_all(x, axis, 0, 0, tiled=True)  11.4 us
    unnamed x22, local copies, waits for them, and re-layouts  2.66 us
  transfers between devices with their start and end apart: 5, of which 4 were waited for; matrix products, arithmetic and copies ran while one was open for 0% of the time, Pallas kernels for 26%

profile of v4, /device:TPU:0, one launch (start us, length us, event | category | flops | bytes accessed | tf_op | source)
XLA Modules:
  0.0 95.1 jit_solution(12353273357985543850)
XLA Ops:
  0.6 4.3 %open.1 = (f32[2368,128]{1,0:T(8,128)}, f32[864,128]{1,0:T(8,128)S(1)}) custom-call(s32[2,12]{1,0:T(2,128)} %offsets.1, f32[256,768]{1,0:T(8,128)} %q.3, f32[256,768]{1,0:T(8,128)} %k.5, f32[256,768]{1,0:T(8,128)} %v.5, f32[256,768]{1,0:T(8,128)} %d.3), custom_call_target="tpu_custom_call" | custom-call | flops 100000000 | bytes 100000 | tf_op jit(solution)/shard_map/open/pallas_call | solution.py:638
  5.0 0.0 copy-start.10
  5.0 7.7 %all-to-all-start = ((f32[8,296,128]{2,1,0:T(8,128)}), f32[8,296,128]{2,1,0:T(8,128)S(1)}, u32[]{:S(2)}, u32[]{:S(2)}) async-start(f32[8,296,128]{2,1,0:T(8,128)} %bitcast.18), calls=%async_computation | async-start | bytes 2424832 | tf_op jit(solution)/shard_map/all_to_all | solution.py:655
  12.7 0.0 copy-done.10
  12.7 0.1 reshape.19
  12.8 0.1 pad_add_fusion.meta
  12.8 11.3 %local.1 = (f32[1536,128]{1,0:T(8,128)S(1)}, f32[1536,128]{1,0:T(8,128)S(1)}, f32[1536,128]{1,0:T(8,128)S(1)}, f32[1536,128]{1,0:T(8,128)S(1)}) custom-call(s32[26]{0:T(128)S(1)} %pad_add_fusion.meta, f32[256,768]{1,0:T(8,128)} %q.3, f32[256,768]{1,0:T(8,128)} %k.5, f32[256,768]{1,0:T(8,128)} %v.5, f32[256,768]{1,0:T(8,128)} %d.3), custom_call_target="tpu_custom_call" | custom-call | flops 100000000 | bytes 100000 | tf_op jit(solution)/shard_map/local/pallas_call | solution.py:638
  24.2 0.0 copy-start.2
  24.2 0.9 copy-done.2
  25.1 0.0 copy-start.4
  25.1 0.9 copy-done.4
  26.0 0.0 copy-start.6
  26.0 0.9 copy-done.6
  26.8 0.0 copy-start.8
  26.8 4.8 %all-to-all-done = f32[8,296,128]{2,1,0:T(8,128)S(1)} async-done(((f32[8,296,128]{2,1,0:T(8,128)}), f32[8,296,128]{2,1,0:T(8,128)S(1)}, u32[]{:S(2)}, u32[]{:S(2)}) %all-to-all-start) | async-done | bytes 1212448 | tf_op jit(solution)/shard_map/all_to_all | solution.py:655
  31.6 1.6 %spread.1 = f32[1024,128]{1,0:T(8,128)} custom-call(s32[26]{0:T(128)S(1)} %pad_add_fusion.meta, f32[2368,128]{1,0:T(8,128)S(1)} %bitcast.10), custom_call_target="tpu_custom_call" | custom-call | flops 100000000 | bytes 100000 | tf_op jit(solution)/shard_map/spread/pallas_call | solution.py:638
  33.2 0.0 copy-done.8
  33.2 5.0 %all-to-all-start.1 = ((f32[16,64,128]{2,1,0:T(8,128)}), f32[16,64,128]{2,1,0:T(8,128)S(1)}, u32[]{:S(2)}, u32[]{:S(2)}) async-start(f32[16,64,128]{2,1,0:T(8,128)} %bitcast.17), calls=%async_computation.1 | async-start | bytes 1048576 | tf_op jit(solution)/shard_map/all_to_all | solution.py:655
  38.3 2.4 %near_forward.1 = (f32[8,256]{1,0:T(8,128)S(1)}, f32[72,128]{1,0:T(8,128)S(1)}, f32[72,128]{1,0:T(8,128)S(1)}) custom-call(s32[26]{0:T(128)S(1)} %pad_add_fusion.meta, f32[2368,128]{1,0:T(8,128)S(1)} %bitcast.11), custom_call_target="tpu_custom_call" | custom-call | flops 100000000 | bytes 100000 | tf_op jit(solution)/shard_map/near_forward/pallas_call | solution.py:638
  40.7 0.4 collective-permute-start
  41.1 7.3 %live.1 = (bf16[1792,256]{1,0:T(8,128)(2,1)}, bf16[1792,256]{1,0:T(8,128)(2,1)}, f32[1296,128]{1,0:T(8,128)}, f32[16,128]{1,0:T(8,128)S(1)}) custom-call(s32[26]{0:T(128)S(1)} %pad_add_fusion.meta, f32[256,768]{1,0:T(8,128)} %k.5, f32[256,768]{1,0:T(8,128)} %v.5, f32[864,128]{1,0:T(8,128)S(1)} %get-tuple-element.39.live), custom_call_target="tpu_custom_call" | custom-call | flops 100000000 | bytes 100000 | tf_op jit(solution)/shard_map/live/pallas_call | solution.py:638
  48.4 0.8 all-to-all-done.1
  49.1 0.0 collective-permute-done.pair
  49.1 2.9 %far.1 = (f32[1024,128]{1,0:T(8,128)}, f32[72,128]{1,0:T(8,128)S(1)}, f32[72,128]{1,0:T(8,128)S(1)}) custom-call(s32[26]{0:T(128)S(1)} %pad_add_fusion.meta, f32[1024,128]{1,0:T(8,128)S(1)} %bitcast.16, f32[72,128]{1,0:T(8,128)S(1)} %get-tuple-element.51.mine, f32[72,128]{1,0:T(8,128)S(1)} %collective-permute-done.pair), custom_call_target="tpu_custom_call" | custom-call | flops 100000000 | bytes 100000 | tf_op jit(solution)/shard_map/far/pallas_call | solution.py:638
  52.0 4.7 %all-to-all-start.2 = ((f32[16,64,128]{2,1,0:T(8,128)}), f32[16,64,128]{2,1,0:T(8,128)S(1)}, u32[]{:S(2)}, u32[]{:S(2)}) async-start(f32[16,64,128]{2,1,0:T(8,128)} %bitcast.6), calls=%async_computation.2 | async-start | bytes 1048576 | tf_op jit(solution)/shard_map/all_to_all | solution.py:655
  56.7 0.4 collective-permute-start.1
  57.1 1.1 %collective-permute-done.1.back = f32[72,128]{1,0:T(8,128)S(1)} collective-permute-done((f32[72,128]{1,0:T(8,128)S(1)}, f32[72,128]{1,0:T(8,128)S(1)}, u32[]{:S(2)}, u32[]{:S(2)}) %collective-permute-start.1) | collective-permute-done | bytes 36896 | tf_op jit(solution)/shard_map/ppermute | solution.py:659
  58.2 3.6 %near_backward.1.near = f32[2368,128]{1,0:T(8,128)S(1)} custom-call(s32[26]{0:T(128)S(1)} %pad_add_fusion.meta, f32[2368,128]{1,0:T(8,128)S(1)} %bitcast.12, f32[8,256]{1,0:T(8,128)S(1)} %get-tuple-element.49.own, f32[72,128]{1,0:T(8,128)S(1)} %get-tuple-element.53.keep, f32[72,128]{1,0:T(8,128)S(1)} %collective-permute-done.1.back), custom_call_target="tpu_custom_call" | custom-call | flops 100000000 | bytes 100000 | tf_op jit(solution)/shard_map/near_backward/pallas_call | solution.py:638
  61.8 5.8 %all-to-all-done.2 = f32[16,64,128]{2,1,0:T(8,128)S(1)} async-done(((f32[16,64,128]{2,1,0:T(8,128)}), f32[16,64,128]{2,1,0:T(8,128)S(1)}, u32[]{:S(2)}, u32[]{:S(2)}) %all-to-all-start.2) | async-done | bytes 524320 | tf_op jit(solution)/shard_map/all_to_all | solution.py:655
  67.6 0.0 copy-start.3
  67.6 0.0 copy-start.5
  67.6 0.0 copy-start.7
  67.6 0.0 copy-start.9
  67.6 0.7 merge.1
  68.3 0.0 copy-start
  68.3 0.0 copy-start.1
  68.3 22.0 %all_to_all.46 = f32[8,296,128]{2,1,0:T(8,128)S(1)} all-to-all(f32[8,296,128]{2,1,0:T(8,128)S(1)} %bitcast.13), channel_id=1, replica_groups=mesh['seg'=16,'blk'=8] {'blk'}, dimensions={0} | all-to-all | bytes 2424832 | tf_op jit(solution)/shard_map/all_to_all | solution.py:655
  90.3 0.0 copy-done.3
  90.3 0.0 copy-done.5
  90.3 0.0 copy-done.7
  90.3 0.0 copy-done.9
  90.3 0.0 copy-done
  90.3 0.0 copy-done.1
  90.3 4.7 %close.1 = (f32[256,768]{1,0:T(8,128)}, f32[256,768]{1,0:T(8,128)}, f32[256,768]{1,0:T(8,128)}, f32[256,768]{1,0:T(8,128)}) custom-call(s32[26]{0:T(128)S(1)} %pad_add_fusion.meta, f32[1536,128]{1,0:T(8,128)S(1)} %copy-done.3, f32[1536,128]{1,0:T(8,128)S(1)} %copy-done.5, f32[1536,128]{1,0:T(8,128)S(1)} %copy-done.7, f32[1536,128]{1,0:T(8,128)S(1)} %copy-done.9, ...), custom_call_target="tpu_custom_call" | custom-call | flops 100000000 | bytes 100000 | tf_op jit(solution)/shard_map/close/pallas_call | solution.py:638
Async XLA Ops:
  5.0 7.7 %copy-start.10 = (s32[2,12]{1,0:T(2,128)S(1)}, s32[2,12]{1,0:T(2,128)}, u32[]{:S(2)}) copy-start(s32[2,12]{1,0:T(2,128)} %offsets.1) | copy-start | bytes 292
  5.0 26.7 %all-to-all-start = ((f32[8,296,128]{2,1,0:T(8,128)}), f32[8,296,128]{2,1,0:T(8,128)S(1)}, u32[]{:S(2)}, u32[]{:S(2)}) async-start(f32[8,296,128]{2,1,0:T(8,128)} %bitcast.18), calls=%async_computation | async-start | bytes 2424832 | tf_op jit(solution)/shard_map/all_to_all | solution.py:655
  24.2 0.9 copy-start.2
  25.1 0.9 copy-start.4
  26.0 0.9 copy-start.6
  26.8 6.4 %copy-start.8 = (f32[1536,128]{1,0:T(8,128)}, f32[1536,128]{1,0:T(8,128)S(1)}, u32[]{:S(2)}) copy-start(f32[1536,128]{1,0:T(8,128)S(1)} %get-tuple-element.38.dv1) | copy-start | bytes 2359300
  33.2 15.9 %all-to-all-start.1 = ((f32[16,64,128]{2,1,0:T(8,128)}), f32[16,64,128]{2,1,0:T(8,128)S(1)}, u32[]{:S(2)}, u32[]{:S(2)}) async-start(f32[16,64,128]{2,1,0:T(8,128)} %bitcast.17), calls=%async_computation.1 | async-start | bytes 1048576 | tf_op jit(solution)/shard_map/all_to_all | solution.py:655
  40.7 8.4 %collective-permute-start = (f32[72,128]{1,0:T(8,128)S(1)}, f32[72,128]{1,0:T(8,128)S(1)}, u32[]{:S(2)}, u32[]{:S(2)}) collective-permute-start(f32[72,128]{1,0:T(8,128)S(1)} %get-tuple-element.52), channel_id=1, source_target_pairs={{0,8},{8,0},{16,24},{24,16},{32,40},{40,32},{48,56},{56,48},{64,72... | collective-permute-start | bytes 110600 | tf_op jit(solution)/shard_map/ppermute | solution.py:659
  52.0 15.6 %all-to-all-start.2 = ((f32[16,64,128]{2,1,0:T(8,128)}), f32[16,64,128]{2,1,0:T(8,128)S(1)}, u32[]{:S(2)}, u32[]{:S(2)}) async-start(f32[16,64,128]{2,1,0:T(8,128)} %bitcast.6), calls=%async_computation.2 | async-start | bytes 1048576 | tf_op jit(solution)/shard_map/all_to_all | solution.py:655
  56.7 1.5 %collective-permute-start.1 = (f32[72,128]{1,0:T(8,128)S(1)}, f32[72,128]{1,0:T(8,128)S(1)}, u32[]{:S(2)}, u32[]{:S(2)}) collective-permute-start(f32[72,128]{1,0:T(8,128)S(1)} %get-tuple-element.54), channel_id=1, source_target_pairs={{0,8},{8,0},{16,24},{24,16},{32,40},{40,32},{48,56},{56,48},{64,72... | collective-permute-start | bytes 110600 | tf_op jit(solution)/shard_map/ppermute | solution.py:659
  67.6 22.7 %copy-start.3 = (f32[1536,128]{1,0:T(8,128)S(1)}, f32[1536,128]{1,0:T(8,128)}, u32[]{:S(2)}) copy-start(f32[1536,128]{1,0:T(8,128)} %copy-done.2) | copy-start | bytes 2359300
  67.6 22.7 %copy-start.5 = (f32[1536,128]{1,0:T(8,128)S(1)}, f32[1536,128]{1,0:T(8,128)}, u32[]{:S(2)}) copy-start(f32[1536,128]{1,0:T(8,128)} %copy-done.4) | copy-start | bytes 2359300
  67.6 22.7 %copy-start.7 = (f32[1536,128]{1,0:T(8,128)S(1)}, f32[1536,128]{1,0:T(8,128)}, u32[]{:S(2)}) copy-start(f32[1536,128]{1,0:T(8,128)} %copy-done.6) | copy-start | bytes 2359300
  67.6 22.7 %copy-start.9 = (f32[1536,128]{1,0:T(8,128)S(1)}, f32[1536,128]{1,0:T(8,128)}, u32[]{:S(2)}) copy-start(f32[1536,128]{1,0:T(8,128)} %copy-done.8) | copy-start | bytes 2359300
  68.3 22.0 %copy-start = (bf16[1792,256]{1,0:T(8,128)(2,1)S(1)}, bf16[1792,256]{1,0:T(8,128)(2,1)}, u32[]{:S(2)}) copy-start(bf16[1792,256]{1,0:T(8,128)(2,1)} %get-tuple-element.45.weights) | copy-start | bytes 2752516
  68.3 22.0 %copy-start.1 = (bf16[1792,256]{1,0:T(8,128)(2,1)S(1)}, bf16[1792,256]{1,0:T(8,128)(2,1)}, u32[]{:S(2)}) copy-start(bf16[1792,256]{1,0:T(8,128)(2,1)} %get-tuple-element.46.slopes) | copy-start | bytes 2752516

commit v5 on v4

--- a/solution.py
+++ b/solution.py
@@ -22,6 +22,7 @@
 SEG_AT, BLK_AT = 24, 25
 FAR_AT, STAT_AT, MESSAGE = 256, 288, 296
 PAIR = 72
+ROW_AT = 14 * ROWS
 
 
 def nt(a, b):
@@ -161,25 +162,36 @@
     return spot
 
 
-def apart(x):
-    low = half_mask(x.shape[0])
-    return [jnp.where(low, x, 0.0), jnp.where(low, 0.0, x)]
-
-
-def live_block(near, far, b):
-    parts = apart(near)
+def pieces(x, count):
+    out = []
+    for _ in range(count - 1):
+        out.append(x.astype(BF).astype(F32))
+        x = x - out[-1]
+    return [*out, x]
+
+
+def place(near, far, b):
+    def apart(x):
+        low = half_mask(x.shape[0])
+        return [jnp.where(low, x, 0.0), jnp.where(low, 0.0, x)]
+
+    rows = [x.astype(BF) for x in apart(near)]
     if b:
-        parts.append(jnp.zeros((16 * b, 128), F32))
-    parts += apart(far)
-    parts.append(jnp.zeros((112 - 16 * b, 128), F32))
-    return jnp.concatenate(parts, axis=0)
-
-
-def live_products(k, v, q, d):
+        rows.append(jnp.zeros((16 * b, 128), BF))
+    rows.append(jnp.concatenate(apart(far), axis=0).astype(BF))
+    rows.append(jnp.zeros((112 - 16 * b, 128), BF))
+    return jnp.concatenate(rows, axis=0)
+
+
+def live_pieces(near, far, b, count):
+    return [place(x, y, b) for x, y in zip(pieces(near, count), pieces(far, count))]
+
+
+def live_products(k, v, q, d, b):
     k0, k1, k2 = split3(k)
-    q0, q1, q2 = split3(q * SCALE)
+    q0, q1, q2 = live_pieces(q[0] * SCALE, q[1] * SCALE, b, 3)
     v0, v1 = split2(v)
-    d0, d1 = split2(d)
+    d0, d1 = live_pieces(*d, b, 2)
     s = nt(cat([k0, k1, k0, k1, k0, k2]), cat([q0, q1, q1, q0, q2, q0]))
     return s, nt(cat([v0, v1, v0, v1]), cat([d0, d1, d1, d0]))
 
@@ -251,8 +263,8 @@
         s, dp = live_products(
             panel[block(1, b), :],
             panel[block(2, b), :],
-            live_block(*rows[b][0], b),
-            live_block(*rows[b][1], b),
+            *rows[b],
+            b,
         )
         far_s, far_dp = far_s + s[:, 128:], far_dp + dp[:, 128:]
         known.append(live_forward(s[:, :128], dp[:, :128], near_positions(meta, b))[:2])
@@ -266,7 +278,7 @@
         copy.wait()
 
 
-def live_kernel(meta, k, v, live, weights, slopes, out_rows, stats, panel, sems, kept, rows_kept, out_sems):
+def live_kernel(meta, k, v, live, weights, stats, panel, sems, kept, out_sems):
     fetch((k, v), panel, sems)
     stats[...] = jnp.zeros_like(stats)
     far_s = far_dp = jnp.zeros((ROWS, 128), F32)
@@ -275,10 +287,10 @@
     def record(n, s, dp, spot):
         lse, delta, p = live_forward(s, dp, spot)
         pair = cat(split2(p)), cat(split2(p * (dp - delta)))
-        for m, (x, out) in enumerate(zip(pair, (weights, slopes))):
-            at = pl.ds(ROWS * n, ROWS)
-            kept[m, at, :] = x
-            copies.append(pltpu.make_async_copy(kept.at[m, at, :], out.at[at, :], out_sems.at[7 * m + n]))
+        for m, x in enumerate(pair):
+            at = pl.ds(ROWS * (7 * m + n), ROWS)
+            kept[at, :] = x
+            copies.append(pltpu.make_async_copy(kept.at[at, :], weights.at[at, :], out_sems.at[7 * m + n]))
             copies[-1].start()
         stats[n : n + 1, :] = lse
         stats[8 + n : 9 + n, :] = delta
@@ -288,7 +300,7 @@
         kb, vb = cat(split2(panel[block(0, b), :] * SCALE)), cat(split2(panel[block(1, b), :]))
         both_sides = tn(p, cat([vb, kb]))
         for n, x in enumerate((both_sides[:, :256], tn(h, kb), both_sides[:, 256:])):
-            yield 6 * PAIR * n + PAIR * b, x[:128, :128] + x[:128, 128:] + x[128:, :128] + x[128:, 128:]
+            yield ROW_AT + 80 * (6 * n + b), x[:128, :128] + x[:128, 128:] + x[128:, :128] + x[128:, 128:]
 
     for b in range(6):
         arrive((k, v), panel, sems, b)
@@ -300,19 +312,21 @@
         s, dp = live_products(
             panel[block(0, b), :],
             panel[block(1, b), :],
-            live_block(*rows[0], b),
-            live_block(*rows[1], b),
+            *rows,
+            b,
         )
         far_s, far_dp = far_s + s[:, 128:], far_dp + dp[:, 128:]
         p, h = record(b, s[:, :128], dp[:, :128], near_positions(meta, b))
         for at, x in products(b, p, h):
-            rows_kept[at : at + LIVE2, :] = both(x[:LIVE2], x[LIVE2:])
+            kept[at : at + LIVE2, :] = cat(split2(both(x[:LIVE2], x[LIVE2:])))
     p, h = record(6, far_s, far_dp, far_positions(meta, True))
     for b in range(6):
         for at, x in products(b, p, h):
             low, high = x[16 * b : 16 * b + 8], x[16 * b + 8 : 16 * b + 16]
-            rows_kept[at + LIVE2 : at + PAIR, :] = both(low, high)
-    copies.append(pltpu.make_async_copy(rows_kept, out_rows, out_sems.at[14]))
+            x = jnp.concatenate([both(low, high), jnp.zeros((8, 128), F32)], axis=0)
+            kept[at + LIVE2 : at + 80, :] = cat(split2(x))
+    at = pl.ds(ROW_AT, 18 * 80)
+    copies.append(pltpu.make_async_copy(kept.at[at, :], weights.at[at, :], out_sems.at[14]))
     copies[-1].start()
     for copy in copies:
         copy.wait()
@@ -403,7 +417,7 @@
     theirs[...] = jnp.where(first, blocks[1], blocks[0])
 
 
-def far_kernel(meta, kv, mine, pair, send, keep, back):
+def far_kernel(meta, kv, mine, pair, send, keep, back, parts, sem):
     first = meta[SEG_AT] % 2 == 0
     x, y = mine[...], pair[...]
     low, high = jnp.where(first, x, y), jnp.where(first, y, x)
@@ -417,13 +431,16 @@
     lse3 = top + jnp.log(total)
     lse, delta = merge([tuple(known), (lse3, delta3)])
     at, qt, dk, dv = backward_core(p * jnp.exp(top - lse), dp, delta, ak, bq, av, bd)
-    send[...] = both(fold(dk), fold(dv))
+    parts[...] = both(fold(dk), fold(dv))
+    leaving = pltpu.make_async_copy(parts, send, sem)
+    leaving.start()
     aq = jnp.concatenate([at, qt], axis=0).T
     stats = (lse3, delta3, lse, delta)
     front = jnp.concatenate([aq[:LIVE2], *stats, jnp.zeros((4, 128), F32)], axis=0)
     rear = jnp.concatenate([aq[LIVE2:], *[turn(x) for x in stats], jnp.zeros((4, 128), F32)], axis=0)
     keep[...] = jnp.where(first, front, rear)
     back[...] = jnp.where(first, rear, front)
+    leaving.wait()
 
 
 def by_head(meta, keep, back):
@@ -538,12 +555,15 @@
 
 
 def close_kernel(
-    meta, at1, dq1, dk1, dv1, live, weights, slopes, products, stats, got,
-    at_out, dq_out, dk_out, dv_out, panel, sems, held, held_sem,
+    meta, at1, dq1, dk1, dv1, live, weights, stats, got,
+    at_out, dq_out, dk_out, dv_out, panel, sems,
 ):
-    coming = pltpu.make_async_copy(products, held, held_sem)
-    coming.start()
     outs, local = (at_out, dq_out, dk_out, dv_out), (at1, dq1, dk1, dv1)
+
+    def products(n):
+        x = weights[ROW_AT + 80 * n : ROW_AT + 80 * n + 80, :].astype(F32)
+        return (x[:, :128] + x[:, 128:])[:PAIR]
+
     first = iota((1, 128), 1) < 16
     far = [jnp.zeros((1, 128), F32), jnp.zeros((1, 128), F32)]
     scales, shifts = [], []
@@ -561,25 +581,29 @@
     zero = jnp.zeros((1, 128), F32)
     table = jnp.concatenate([*scales, zero, *shifts, zero], axis=0).T
     low2, low3 = half_mask(LIVE2), half_mask(LIVE3)
-    far_p, far_h = weights[6 * ROWS :, :], slopes[6 * ROWS :, :]
-    copies = []
-    for b in range(6):
-        rows = []
-        for n in range(2):
-            keep = PAIR * (2 * b + n)
-            rows.append((live[keep : keep + LIVE2, :], live[keep + LIVE2 : keep + PAIR, :]))
-        scale = jnp.concatenate([table[:, b : b + 1], table[:, 6:7]], axis=0)
-        shift = jnp.concatenate([table[:, 8 + b : 9 + b], table[:, 14:15]], axis=0)
-        d = live_block(*rows[1], b) * scale
-        q = live_block(*rows[0], b) * (scale * SCALE)
-        d, q, t = [cat(split2(x)) for x in (d, q, q * (-shift))]
-        own_p, own_h = weights[ROWS * b : ROWS * b + ROWS, :], slopes[ROWS * b : ROWS * b + ROWS, :]
-        dense = [jnp.zeros((ROWS, 256), F32), jnp.zeros((ROWS, 256), F32)]
-        for n in range(2):
-            at = slice(128 * n, 128 * n + 128)
-            p, h = cat([own_p[:, at], far_p[:, at]]), cat([own_h[:, at], far_h[:, at]])
-            dense[0] = dense[0] + nn(h, q) + nn(p, t)
-            dense[1] = dense[1] + nn(p, d)
+    far_p, far_h = weights[6 * ROWS : 7 * ROWS, :], weights[13 * ROWS : ROW_AT, :]
+    copies, spreads = [], []
+
+    def finish(a, b, near, far, kept):
+        base = ROWS * (6 * a + b)
+        panel[base : base + ROWS, :] = kept
+        for e in range(2):
+            spot = pl.ds(base + meta[2 * b + e], LIVE2, stride=R2)
+            panel[spot, :] = panel[spot, :] + jnp.where(low2 if e == 0 else ~low2, near, 0.0)
+            spot = pl.ds(base + meta[HEADS + 2 * b + e], LIVE3, stride=R3)
+            panel[spot, :] = panel[spot, :] + jnp.where(low3 if e == 0 else ~low3, far, 0.0)
+        copies.append(
+            pltpu.make_async_copy(
+                panel.at[block(a, b), :], outs[a].at[:, columns(b)], sems.at[6 * a + b]
+            )
+        )
+        copies[-1].start()
+
+    def arrived(a, b):
+        near, far = MESSAGE * b + LIVE2 * a, MESSAGE * b + FAR_AT + LIVE3 * a
+        return got[near : near + LIVE2, :], got[far : far + LIVE3, :]
+
+    for b in range(6):
         spread = [
             (
                 jnp.where(low2, table[:LIVE2, n + b : n + b + 1], table[LIVE2:, n + b : n + b + 1]),
@@ -591,38 +615,35 @@
             )
             for n in (0, 8)
         ]
-        for a in (2, 3, 0, 1):
-            if b == 0 and a == 0:
-                coming.wait()
-            at = MESSAGE * b + LIVE2 * a
-            near = got[at : at + LIVE2, :]
-            at = MESSAGE * b + FAR_AT + LIVE3 * a
-            far = got[at : at + LIVE3, :]
-            base = ROWS * (6 * a + b)
-            kept = local[a][ROWS * b : ROWS * b + ROWS, :]
+        spreads.append(spread)
+        z, x, y = products(b), products(6 + b), products(12 + b)
+        for a in range(2):
+            near, far = arrived(a, b)
             if a == 0:
-                z = held[PAIR * b : PAIR * b + PAIR, :]
-                near = near + spread[0][0] * z[:LIVE2]
-                far = far + spread[0][1] * z[LIVE2:]
-            elif a == 1:
-                x, y = [held[PAIR * (6 * n + b) : PAIR * (6 * n + b + 1), :] for n in (1, 2)]
+                near, far = near + spread[0][0] * z[:LIVE2], far + spread[0][1] * z[LIVE2:]
+            else:
                 near = near + spread[0][0] * (x[:LIVE2] - spread[1][0] * y[:LIVE2])
                 far = far + spread[0][1] * (x[LIVE2:] - spread[1][1] * y[LIVE2:])
-            else:
-                x = dense[a - 2]
-                kept = kept + (x[:, :128] + x[:, 128:])
-            panel[base : base + ROWS, :] = kept
-            for e in range(2):
-                spot = pl.ds(base + meta[2 * b + e], LIVE2, stride=R2)
-                panel[spot, :] = panel[spot, :] + jnp.where(low2 if e == 0 else ~low2, near, 0.0)
-                spot = pl.ds(base + meta[HEADS + 2 * b + e], LIVE3, stride=R3)
-                panel[spot, :] = panel[spot, :] + jnp.where(low3 if e == 0 else ~low3, far, 0.0)
-            copies.append(
-                pltpu.make_async_copy(
-                    panel.at[block(a, b), :], outs[a].at[:, columns(b)], sems.at[6 * a + b]
-                )
-            )
-            copies[-1].start()
+            finish(a, b, near, far, local[a][ROWS * b : ROWS * b + ROWS, :])
+    for b in range(6):
+        rows = []
+        for n in range(2):
+            keep = PAIR * (2 * b + n)
+            rows.append((live[keep : keep + LIVE2, :], live[keep + LIVE2 : keep + PAIR, :]))
+        d = [x * w for x, w in zip(rows[1], spreads[b][0])]
+        q = [x * (w * SCALE) for x, w in zip(rows[0], spreads[b][0])]
+        t = [-x * w for x, w in zip(q, spreads[b][1])]
+        d, q, t = [cat(live_pieces(*x, b, 2)) for x in (d, q, t)]
+        own_p, own_h = [weights[ROWS * n : ROWS * n + ROWS, :] for n in (b, 7 + b)]
+        dense = [jnp.zeros((ROWS, 256), F32), jnp.zeros((ROWS, 256), F32)]
+        for n in range(2):
+            at = slice(128 * n, 128 * n + 128)
+            p, h = cat([own_p[:, at], far_p[:, at]]), cat([own_h[:, at], far_h[:, at]])
+            dense[0] = dense[0] + nn(h, q) + nn(p, t)
+            dense[1] = dense[1] + nn(p, d)
+        for a, x in zip((2, 3), dense):
+            kept = local[a][ROWS * b : ROWS * b + ROWS, :] + (x[:, :128] + x[:, 128:])
+            finish(a, b, *arrived(a, b), kept)
     for copy in copies:
         copy.wait()
 
@@ -712,25 +733,30 @@
     rest = call(
         live_kernel,
         "live",
-        [pltpu.HBM((7 * ROWS, 256), BF)] * 2 + [pltpu.HBM((18 * PAIR, 128), F32), (16, 128)],
+        [pltpu.HBM((ROW_AT + 18 * 80, 256), BF), (16, 128)],
         (meta, rows[1], rows[2], live),
         10**8,
         16,
         [
             pltpu.VMEM((12 * ROWS, 128), F32),
             pltpu.SemaphoreType.DMA((12,)),
-            pltpu.VMEM((2, 7 * ROWS, 256), BF),
-            pltpu.VMEM((18 * PAIR, 128), F32),
+            pltpu.VMEM((ROW_AT + 18 * 80, 256), BF),
             pltpu.SemaphoreType.DMA((15,)),
         ],
         (1, 2),
-        [HBM] * 3 + [VMEM],
+        [HBM, VMEM],
     )
     all_keys, *rest = lax.optimization_barrier((all_keys, *rest))
-    rest[2] = in_hbm(rest[2])
     partner = swap_cores(theirs)
     parts, keep, back = call(
-        far_kernel, "far", [far, pair, pair], (meta, all_keys, mine, partner), 10**8, 24
+        far_kernel,
+        "far",
+        [pltpu.HBM(far, F32), pair, pair],
+        (meta, all_keys, mine, partner),
+        10**8,
+        24,
+        [pltpu.VMEM(far, F32), pltpu.SemaphoreType.DMA],
+        out_spec=[HBM, VMEM, VMEM],
     )
     sums = swap(parts, "seg")
     back = swap_cores(back)
@@ -742,7 +768,7 @@
         10**8,
         24,
     )
-    (reply,) = call(merge_kernel, "merge", [message], (meta, near, sums, keep, back), 10**8, 12)
+    (reply,) = call(merge_kernel, "merge", [message], (meta, near, sums, keep, back), 2 * 10**10, 12)
     home = swap(reply, "blk")
     return tuple(
         call(
@@ -752,9 +778,8 @@
             (meta, *local, live, *rest, home),
             10**8,
             16,
-            [PANEL, COPIES, pltpu.VMEM((18 * PAIR, 128), F32), pltpu.SemaphoreType.DMA],
-            (8,),
-            HBM,
+            [PANEL, COPIES],
+            out_spec=HBM,
         )
     )
 

time: 95.6 us -> 95.1 us (level)
  Pallas kernels: 38.7 us -> 37.6 us
    pallas_call x9, Pallas kernels: 38.7 us -> 37.6 us  [call(): pl.pallas_call(kernel, name=name, out_shape=[jax.ShapeDtypeStruct(x, F32)...]
    unnamed x22 -> x20, local copies, waits for them, and re-layouts: 2.66 us -> 3.54 us
where the time goes in v5:
time: 95.1 us; the launch traced here: 94.6 us
  Pallas kernels  37.6 us (40%)
  blocking collectives  22.5 us (24%)
  starting transfers between devices  18.3 us (19%)
  waiting for transfers between devices  11.5 us (12%)
  local copies, waits for them, and re-layouts  3.62 us (4%)
    pallas_call x9, Pallas kernels, call(): pl.pallas_call(kernel, name=name, out_shape=[jax.ShapeDtypeStruct(x, F32)...  37.6 us
    all_to_all x1, blocking collectives, swap(): return lax.all_to_all(x, axis, 0, 0, tiled=True)  22.5 us
    all_to_all x3, starting transfers between devices, swap(): return lax.all_to_all(x, axis, 0, 0, tiled=True)  17.5 us
    all_to_all x3, waiting for transfers between devices, swap(): return lax.all_to_all(x, axis, 0, 0, tiled=True)  10.5 us
    unnamed x20, local copies, waits for them, and re-layouts  3.54 us
  transfers between devices with their start and end apart: 5, of which 4 were waited for; matrix products, arithmetic and copies ran while one was open for 0% of the time, Pallas kernels for 26%

profile of v5, /device:TPU:0, one launch (start us, length us, event | category | flops | bytes accessed | tf_op | source)
XLA Modules:
  0.0 94.6 jit_solution(5991497280185863542)
XLA Ops:
  0.6 4.3 %open.1 = (f32[2368,128]{1,0:T(8,128)}, f32[864,128]{1,0:T(8,128)S(1)}) custom-call(s32[2,12]{1,0:T(2,128)} %offsets.1, f32[256,768]{1,0:T(8,128)} %q.3, f32[256,768]{1,0:T(8,128)} %k.5, f32[256,768]{1,0:T(8,128)} %v.5, f32[256,768]{1,0:T(8,128)} %d.3), custom_call_target="tpu_custom_call" | custom-call | flops 100000000 | bytes 100000 | tf_op jit(solution)/shard_map/open/pallas_call | solution.py:659
  4.9 0.0 copy-start.9
  4.9 7.7 %all-to-all-start = ((f32[8,296,128]{2,1,0:T(8,128)}), f32[8,296,128]{2,1,0:T(8,128)S(1)}, u32[]{:S(2)}, u32[]{:S(2)}) async-start(f32[8,296,128]{2,1,0:T(8,128)} %bitcast.18), calls=%async_computation | async-start | bytes 2424832 | tf_op jit(solution)/shard_map/all_to_all | solution.py:676
  12.6 0.0 copy-done.9
  12.6 0.1 reshape.19
  12.7 0.1 pad_add_fusion.meta
  12.8 11.3 %local.1 = (f32[1536,128]{1,0:T(8,128)S(1)}, f32[1536,128]{1,0:T(8,128)S(1)}, f32[1536,128]{1,0:T(8,128)S(1)}, f32[1536,128]{1,0:T(8,128)S(1)}) custom-call(s32[26]{0:T(128)S(1)} %pad_add_fusion.meta, f32[256,768]{1,0:T(8,128)} %q.3, f32[256,768]{1,0:T(8,128)} %k.5, f32[256,768]{1,0:T(8,128)} %v.5, f32[256,768]{1,0:T(8,128)} %d.3), custom_call_target="tpu_custom_call" | custom-call | flops 100000000 | bytes 100000 | tf_op jit(solution)/shard_map/local/pallas_call | solution.py:659
  24.2 0.0 copy-start.1
  24.2 0.9 copy-done.1
  25.0 0.0 copy-start.3
  25.0 0.9 copy-done.3
  25.9 0.0 copy-start.5
  25.9 0.9 copy-done.5
  26.8 0.0 copy-start.7
  26.8 0.9 copy-done.7
  27.7 3.9 %all-to-all-done = f32[8,296,128]{2,1,0:T(8,128)S(1)} async-done(((f32[8,296,128]{2,1,0:T(8,128)}), f32[8,296,128]{2,1,0:T(8,128)S(1)}, u32[]{:S(2)}, u32[]{:S(2)}) %all-to-all-start) | async-done | bytes 1212448 | tf_op jit(solution)/shard_map/all_to_all | solution.py:676
  31.6 1.6 %spread.1 = f32[1024,128]{1,0:T(8,128)} custom-call(s32[26]{0:T(128)S(1)} %pad_add_fusion.meta, f32[2368,128]{1,0:T(8,128)S(1)} %bitcast.10), custom_call_target="tpu_custom_call" | custom-call | flops 100000000 | bytes 100000 | tf_op jit(solution)/shard_map/spread/pallas_call | solution.py:659
  33.2 5.0 %all-to-all-start.1 = ((f32[16,64,128]{2,1,0:T(8,128)}), f32[16,64,128]{2,1,0:T(8,128)S(1)}, u32[]{:S(2)}, u32[]{:S(2)}) async-start(f32[16,64,128]{2,1,0:T(8,128)} %bitcast.17), calls=%async_computation.1 | async-start | bytes 1048576 | tf_op jit(solution)/shard_map/all_to_all | solution.py:676
  38.2 2.4 %near_forward.1 = (f32[8,256]{1,0:T(8,128)S(1)}, f32[72,128]{1,0:T(8,128)S(1)}, f32[72,128]{1,0:T(8,128)S(1)}) custom-call(s32[26]{0:T(128)S(1)} %pad_add_fusion.meta, f32[2368,128]{1,0:T(8,128)S(1)} %bitcast.11), custom_call_target="tpu_custom_call" | custom-call | flops 100000000 | bytes 100000 | tf_op jit(solution)/shard_map/near_forward/pallas_call | solution.py:659
  40.6 0.4 collective-permute-start
  41.1 7.3 %live.1 = (bf16[5024,256]{1,0:T(8,128)(2,1)}, f32[16,128]{1,0:T(8,128)S(1)}) custom-call(s32[26]{0:T(128)S(1)} %pad_add_fusion.meta, f32[256,768]{1,0:T(8,128)} %k.5, f32[256,768]{1,0:T(8,128)} %v.5, f32[864,128]{1,0:T(8,128)S(1)} %get-tuple-element.35.live), custom_call_target="tpu_custom_call" | custom-call | flops 100000000 | bytes 100000 | tf_op jit(solution)/shard_map/live/pallas_call | solution.py:659
  48.3 0.7 all-to-all-done.1
  49.1 0.0 collective-permute-done.pair
  49.1 2.8 %far.1 = (f32[1024,128]{1,0:T(8,128)}, f32[72,128]{1,0:T(8,128)S(1)}, f32[72,128]{1,0:T(8,128)S(1)}) custom-call(s32[26]{0:T(128)S(1)} %pad_add_fusion.meta, f32[1024,128]{1,0:T(8,128)S(1)} %bitcast.14, f32[72,128]{1,0:T(8,128)S(1)} %get-tuple-element.43.mine, f32[72,128]{1,0:T(8,128)S(1)} %collective-permute-done.pair), custom_call_target="tpu_custom_call" | custom-call | flops 100000000 | bytes 100000 | tf_op jit(solution)/shard_map/far/pallas_call | solution.py:659
  51.9 4.8 %all-to-all-start.2 = ((f32[16,64,128]{2,1,0:T(8,128)}), f32[16,64,128]{2,1,0:T(8,128)S(1)}, u32[]{:S(2)}, u32[]{:S(2)}) async-start(f32[16,64,128]{2,1,0:T(8,128)} %bitcast.19), calls=%async_computation.2 | async-start | bytes 1048576 | tf_op jit(solution)/shard_map/all_to_all | solution.py:676
  56.7 0.4 collective-permute-start.1
  57.1 1.1 %collective-permute-done.1.back = f32[72,128]{1,0:T(8,128)S(1)} collective-permute-done((f32[72,128]{1,0:T(8,128)S(1)}, f32[72,128]{1,0:T(8,128)S(1)}, u32[]{:S(2)}, u32[]{:S(2)}) %collective-permute-start.1) | collective-permute-done | bytes 36896 | tf_op jit(solution)/shard_map/ppermute | solution.py:680
  58.2 3.6 %near_backward.1.near = f32[2368,128]{1,0:T(8,128)S(1)} custom-call(s32[26]{0:T(128)S(1)} %pad_add_fusion.meta, f32[2368,128]{1,0:T(8,128)S(1)} %bitcast.12, f32[8,256]{1,0:T(8,128)S(1)} %get-tuple-element.41.own, f32[72,128]{1,0:T(8,128)S(1)} %get-tuple-element.45.keep, f32[72,128]{1,0:T(8,128)S(1)} %collective-permute-done.1.back), custom_call_target="tpu_custom_call" | custom-call | flops 100000000 | bytes 100000 | tf_op jit(solution)/shard_map/near_backward/pallas_call | solution.py:659
  61.7 5.8 %all-to-all-done.2 = f32[16,64,128]{2,1,0:T(8,128)S(1)} async-done(((f32[16,64,128]{2,1,0:T(8,128)}), f32[16,64,128]{2,1,0:T(8,128)S(1)}, u32[]{:S(2)}, u32[]{:S(2)}) %all-to-all-start.2) | async-done | bytes 524320 | tf_op jit(solution)/shard_map/all_to_all | solution.py:676
  67.6 0.0 copy-start
  67.6 0.0 copy-start.8
  67.6 0.7 merge.1
  68.2 0.0 copy-start.2
  68.2 0.0 copy-start.4
  68.3 0.0 copy-start.6
  68.3 22.5 %all_to_all.46 = f32[8,296,128]{2,1,0:T(8,128)S(1)} all-to-all(f32[8,296,128]{2,1,0:T(8,128)S(1)} %bitcast.15), channel_id=1, replica_groups=mesh['seg'=16,'blk'=8] {'blk'}, dimensions={0} | all-to-all | bytes 2424832 | tf_op jit(solution)/shard_map/all_to_all | solution.py:676
  90.8 0.0 copy-done
  90.8 0.0 copy-done.8
  90.8 0.0 copy-done.2
  90.8 0.0 copy-done.4
  90.8 0.0 copy-done.6
  90.8 3.6 %close.1 = (f32[256,768]{1,0:T(8,128)}, f32[256,768]{1,0:T(8,128)}, f32[256,768]{1,0:T(8,128)}, f32[256,768]{1,0:T(8,128)}) custom-call(s32[26]{0:T(128)S(1)} %pad_add_fusion.meta, f32[1536,128]{1,0:T(8,128)S(1)} %copy-done.2, f32[1536,128]{1,0:T(8,128)S(1)} %copy-done.4, f32[1536,128]{1,0:T(8,128)S(1)} %copy-done.6, f32[1536,128]{1,0:T(8,128)S(1)} %copy-done.8, ...), custom_call_target="tpu_custom_call" | custom-call | flops 100000000 | bytes 100000 | tf_op jit(solution)/shard_map/close/pallas_call | solution.py:659
Async XLA Ops:
  4.9 7.7 %copy-start.9 = (s32[2,12]{1,0:T(2,128)S(1)}, s32[2,12]{1,0:T(2,128)}, u32[]{:S(2)}) copy-start(s32[2,12]{1,0:T(2,128)} %offsets.1) | copy-start | bytes 292
  4.9 26.7 %all-to-all-start = ((f32[8,296,128]{2,1,0:T(8,128)}), f32[8,296,128]{2,1,0:T(8,128)S(1)}, u32[]{:S(2)}, u32[]{:S(2)}) async-start(f32[8,296,128]{2,1,0:T(8,128)} %bitcast.18), calls=%async_computation | async-start | bytes 2424832 | tf_op jit(solution)/shard_map/all_to_all | solution.py:676
  24.2 0.9 copy-start.1
  25.0 0.9 copy-start.3
  25.9 0.9 copy-start.5
  26.8 0.9 copy-start.7
  33.2 15.9 %all-to-all-start.1 = ((f32[16,64,128]{2,1,0:T(8,128)}), f32[16,64,128]{2,1,0:T(8,128)S(1)}, u32[]{:S(2)}, u32[]{:S(2)}) async-start(f32[16,64,128]{2,1,0:T(8,128)} %bitcast.17), calls=%async_computation.1 | async-start | bytes 1048576 | tf_op jit(solution)/shard_map/all_to_all | solution.py:676
  40.6 8.4 %collective-permute-start = (f32[72,128]{1,0:T(8,128)S(1)}, f32[72,128]{1,0:T(8,128)S(1)}, u32[]{:S(2)}, u32[]{:S(2)}) collective-permute-start(f32[72,128]{1,0:T(8,128)S(1)} %get-tuple-element.44), channel_id=1, source_target_pairs={{0,8},{8,0},{16,24},{24,16},{32,40},{40,32},{48,56},{56,48},{64,72... | collective-permute-start | bytes 110600 | tf_op jit(solution)/shard_map/ppermute | solution.py:680
  51.9 15.6 %all-to-all-start.2 = ((f32[16,64,128]{2,1,0:T(8,128)}), f32[16,64,128]{2,1,0:T(8,128)S(1)}, u32[]{:S(2)}, u32[]{:S(2)}) async-start(f32[16,64,128]{2,1,0:T(8,128)} %bitcast.19), calls=%async_computation.2 | async-start | bytes 1048576 | tf_op jit(solution)/shard_map/all_to_all | solution.py:676
  56.7 1.5 %collective-permute-start.1 = (f32[72,128]{1,0:T(8,128)S(1)}, f32[72,128]{1,0:T(8,128)S(1)}, u32[]{:S(2)}, u32[]{:S(2)}) collective-permute-start(f32[72,128]{1,0:T(8,128)S(1)} %get-tuple-element.46), channel_id=1, source_target_pairs={{0,8},{8,0},{16,24},{24,16},{32,40},{40,32},{48,56},{56,48},{64,72... | collective-permute-start | bytes 110600 | tf_op jit(solution)/shard_map/ppermute | solution.py:680
  67.6 23.2 %copy-start = (bf16[5024,256]{1,0:T(8,128)(2,1)S(1)}, bf16[5024,256]{1,0:T(8,128)(2,1)}, u32[]{:S(2)}) copy-start(bf16[5024,256]{1,0:T(8,128)(2,1)} %get-tuple-element.39.weights) | copy-start | bytes 7716868
  67.6 23.2 %copy-start.8 = (f32[1536,128]{1,0:T(8,128)S(1)}, f32[1536,128]{1,0:T(8,128)}, u32[]{:S(2)}) copy-start(f32[1536,128]{1,0:T(8,128)} %copy-done.7) | copy-start | bytes 2359300
  68.2 22.6 %copy-start.2 = (f32[1536,128]{1,0:T(8,128)S(1)}, f32[1536,128]{1,0:T(8,128)}, u32[]{:S(2)}) copy-start(f32[1536,128]{1,0:T(8,128)} %copy-done.1) | copy-start | bytes 2359300
  68.2 22.6 %copy-start.4 = (f32[1536,128]{1,0:T(8,128)S(1)}, f32[1536,128]{1,0:T(8,128)}, u32[]{:S(2)}) copy-start(f32[1536,128]{1,0:T(8,128)} %copy-done.3) | copy-start | bytes 2359300
  68.3 22.6 %copy-start.6 = (f32[1536,128]{1,0:T(8,128)S(1)}, f32[1536,128]{1,0:T(8,128)}, u32[]{:S(2)}) copy-start(f32[1536,128]{1,0:T(8,128)} %copy-done.5) | copy-start | bytes 2359300

commit v6 on v5

--- a/solution.py
+++ b/solution.py
@@ -339,7 +339,14 @@
 
 
 def stat_rows(ref, n):
-    return ref[pl.ds(STAT_AT + n, 8, stride=MESSAGE), :]
+    rows = [MESSAGE * b + STAT_AT + n for b in range(8)]
+    return jnp.concatenate([ref[at : at + 1, :] for at in rows], axis=0)
+
+
+def write_stat_rows(ref, n, x):
+    for b in range(8):
+        at = MESSAGE * b + STAT_AT + n
+        ref[at : at + 1, :] = x[b : b + 1, :]
 
 
 def spread_kernel(meta, got, out, kv, sems):
@@ -477,8 +484,8 @@
         for e in range(2):
             tail = ((sub < 64) & (lane == LIVE3 * e + sub % 8)).astype(F32)
             rest = rest + exact(jnp.where(diagonal, far[e][66 + n : 67 + n], 0.0), tail)
-        out[pl.ds(STAT_AT + n, 8, stride=MESSAGE), :] = x
-        out[pl.ds(STAT_AT + 2 + n, 8, stride=MESSAGE), :] = rest
+        write_stat_rows(out, n, x)
+        write_stat_rows(out, 2 + n, rest)
     ats, qts, dks, dvs = [], [], [], []
     for e, parts in enumerate(near_blocks(got)):
         results = []
@@ -651,7 +658,7 @@
 SMEM = pl.BlockSpec(memory_space=pltpu.SMEM)
 HBM = pl.BlockSpec(memory_space=pltpu.HBM)
 VMEM = pl.BlockSpec(memory_space=pltpu.VMEM)
-PANEL = pltpu.VMEM((24 * ROWS, 128), F32)
+PANEL = pltpu.VMEM((24 * ROWS + R3, 128), F32)
 COPIES = pltpu.SemaphoreType.DMA((24,))
 
 

time: 95.1 us -> 95.1 us (level)
  no operation moved by 1% of the time
where the time goes in v6:
time: 95.1 us; the launch traced here: 94.6 us
  Pallas kernels  37.6 us (40%)
  blocking collectives  22.5 us (24%)
  starting transfers between devices  18.3 us (19%)
  waiting for transfers between devices  11.5 us (12%)
  local copies, waits for them, and re-layouts  3.62 us (4%)
    pallas_call x9, Pallas kernels, call(): pl.pallas_call(kernel, name=name, out_shape=[jax.ShapeDtypeStruct(x, F32)...  37.6 us
    all_to_all x1, blocking collectives, swap(): return lax.all_to_all(x, axis, 0, 0, tiled=True)  22.5 us
    all_to_all x3, starting transfers between devices, swap(): return lax.all_to_all(x, axis, 0, 0, tiled=True)  17.5 us
    all_to_all x3, waiting for transfers between devices, swap(): return lax.all_to_all(x, axis, 0, 0, tiled=True)  10.5 us
    unnamed x20, local copies, waits for them, and re-layouts  3.54 us
  transfers between devices with their start and end apart: 5, of which 4 were waited for; matrix products, arithmetic and copies ran while one was open for 0% of the time, Pallas kernels for 26%

profile of v6, /device:TPU:0, one launch (start us, length us, event | category | flops | bytes accessed | tf_op | source)
XLA Modules:
  0.0 94.6 jit_solution(17907491553409917957)
XLA Ops:
  0.6 4.3 %open.1 = (f32[2368,128]{1,0:T(8,128)}, f32[864,128]{1,0:T(8,128)S(1)}) custom-call(s32[2,12]{1,0:T(2,128)} %offsets.1, f32[256,768]{1,0:T(8,128)} %q.3, f32[256,768]{1,0:T(8,128)} %k.5, f32[256,768]{1,0:T(8,128)} %v.5, f32[256,768]{1,0:T(8,128)} %d.3), custom_call_target="tpu_custom_call" | custom-call | flops 100000000 | bytes 100000 | tf_op jit(solution)/shard_map/open/pallas_call | solution.py:666
  4.9 0.0 copy-start.9
  4.9 7.7 %all-to-all-start = ((f32[8,296,128]{2,1,0:T(8,128)}), f32[8,296,128]{2,1,0:T(8,128)S(1)}, u32[]{:S(2)}, u32[]{:S(2)}) async-start(f32[8,296,128]{2,1,0:T(8,128)} %bitcast.18), calls=%async_computation | async-start | bytes 2424832 | tf_op jit(solution)/shard_map/all_to_all | solution.py:683
  12.6 0.0 copy-done.9
  12.6 0.1 reshape.19
  12.7 0.1 pad_add_fusion.meta
  12.8 11.3 %local.1 = (f32[1536,128]{1,0:T(8,128)S(1)}, f32[1536,128]{1,0:T(8,128)S(1)}, f32[1536,128]{1,0:T(8,128)S(1)}, f32[1536,128]{1,0:T(8,128)S(1)}) custom-call(s32[26]{0:T(128)S(1)} %pad_add_fusion.meta, f32[256,768]{1,0:T(8,128)} %q.3, f32[256,768]{1,0:T(8,128)} %k.5, f32[256,768]{1,0:T(8,128)} %v.5, f32[256,768]{1,0:T(8,128)} %d.3), custom_call_target="tpu_custom_call" | custom-call | flops 100000000 | bytes 100000 | tf_op jit(solution)/shard_map/local/pallas_call | solution.py:666
  24.2 0.0 copy-start.1
  24.2 0.9 copy-done.1
  25.0 0.0 copy-start.3
  25.0 0.9 copy-done.3
  25.9 0.0 copy-start.5
  25.9 0.9 copy-done.5
  26.8 0.0 copy-start.7
  26.8 0.9 copy-done.7
  27.7 3.9 %all-to-all-done = f32[8,296,128]{2,1,0:T(8,128)S(1)} async-done(((f32[8,296,128]{2,1,0:T(8,128)}), f32[8,296,128]{2,1,0:T(8,128)S(1)}, u32[]{:S(2)}, u32[]{:S(2)}) %all-to-all-start) | async-done | bytes 1212448 | tf_op jit(solution)/shard_map/all_to_all | solution.py:683
  31.6 1.6 %spread.1 = f32[1024,128]{1,0:T(8,128)} custom-call(s32[26]{0:T(128)S(1)} %pad_add_fusion.meta, f32[2368,128]{1,0:T(8,128)S(1)} %bitcast.10), custom_call_target="tpu_custom_call" | custom-call | flops 100000000 | bytes 100000 | tf_op jit(solution)/shard_map/spread/pallas_call | solution.py:666
  33.2 5.0 %all-to-all-start.1 = ((f32[16,64,128]{2,1,0:T(8,128)}), f32[16,64,128]{2,1,0:T(8,128)S(1)}, u32[]{:S(2)}, u32[]{:S(2)}) async-start(f32[16,64,128]{2,1,0:T(8,128)} %bitcast.17), calls=%async_computation.1 | async-start | bytes 1048576 | tf_op jit(solution)/shard_map/all_to_all | solution.py:683
  38.2 2.4 %near_forward.1 = (f32[8,256]{1,0:T(8,128)S(1)}, f32[72,128]{1,0:T(8,128)S(1)}, f32[72,128]{1,0:T(8,128)S(1)}) custom-call(s32[26]{0:T(128)S(1)} %pad_add_fusion.meta, f32[2368,128]{1,0:T(8,128)S(1)} %bitcast.11), custom_call_target="tpu_custom_call" | custom-call | flops 100000000 | bytes 100000 | tf_op jit(solution)/shard_map/near_forward/pallas_call | solution.py:666
  40.6 0.4 collective-permute-start
  41.1 7.3 %live.1 = (bf16[5024,256]{1,0:T(8,128)(2,1)}, f32[16,128]{1,0:T(8,128)S(1)}) custom-call(s32[26]{0:T(128)S(1)} %pad_add_fusion.meta, f32[256,768]{1,0:T(8,128)} %k.5, f32[256,768]{1,0:T(8,128)} %v.5, f32[864,128]{1,0:T(8,128)S(1)} %get-tuple-element.35.live), custom_call_target="tpu_custom_call" | custom-call | flops 100000000 | bytes 100000 | tf_op jit(solution)/shard_map/live/pallas_call | solution.py:666
  48.3 0.7 all-to-all-done.1
  49.1 0.0 collective-permute-done.pair
  49.1 2.8 %far.1 = (f32[1024,128]{1,0:T(8,128)}, f32[72,128]{1,0:T(8,128)S(1)}, f32[72,128]{1,0:T(8,128)S(1)}) custom-call(s32[26]{0:T(128)S(1)} %pad_add_fusion.meta, f32[1024,128]{1,0:T(8,128)S(1)} %bitcast.14, f32[72,128]{1,0:T(8,128)S(1)} %get-tuple-element.43.mine, f32[72,128]{1,0:T(8,128)S(1)} %collective-permute-done.pair), custom_call_target="tpu_custom_call" | custom-call | flops 100000000 | bytes 100000 | tf_op jit(solution)/shard_map/far/pallas_call | solution.py:666
  51.9 4.8 %all-to-all-start.2 = ((f32[16,64,128]{2,1,0:T(8,128)}), f32[16,64,128]{2,1,0:T(8,128)S(1)}, u32[]{:S(2)}, u32[]{:S(2)}) async-start(f32[16,64,128]{2,1,0:T(8,128)} %bitcast.19), calls=%async_computation.2 | async-start | bytes 1048576 | tf_op jit(solution)/shard_map/all_to_all | solution.py:683
  56.7 0.4 collective-permute-start.1
  57.1 1.1 %collective-permute-done.1.back = f32[72,128]{1,0:T(8,128)S(1)} collective-permute-done((f32[72,128]{1,0:T(8,128)S(1)}, f32[72,128]{1,0:T(8,128)S(1)}, u32[]{:S(2)}, u32[]{:S(2)}) %collective-permute-start.1) | collective-permute-done | bytes 36896 | tf_op jit(solution)/shard_map/ppermute | solution.py:687
  58.2 3.6 %near_backward.1.near = f32[2368,128]{1,0:T(8,128)S(1)} custom-call(s32[26]{0:T(128)S(1)} %pad_add_fusion.meta, f32[2368,128]{1,0:T(8,128)S(1)} %bitcast.12, f32[8,256]{1,0:T(8,128)S(1)} %get-tuple-element.41.own, f32[72,128]{1,0:T(8,128)S(1)} %get-tuple-element.45.keep, f32[72,128]{1,0:T(8,128)S(1)} %collective-permute-done.1.back), custom_call_target="tpu_custom_call" | custom-call | flops 100000000 | bytes 100000 | tf_op jit(solution)/shard_map/near_backward/pallas_call | solution.py:666
  61.8 5.8 %all-to-all-done.2 = f32[16,64,128]{2,1,0:T(8,128)S(1)} async-done(((f32[16,64,128]{2,1,0:T(8,128)}), f32[16,64,128]{2,1,0:T(8,128)S(1)}, u32[]{:S(2)}, u32[]{:S(2)}) %all-to-all-start.2) | async-done | bytes 524320 | tf_op jit(solution)/shard_map/all_to_all | solution.py:683
  67.6 0.0 copy-start
  67.6 0.0 copy-start.8
  67.6 0.7 merge.1
  68.2 0.0 copy-start.2
  68.2 0.0 copy-start.4
  68.2 0.0 copy-start.6
  68.3 22.5 %all_to_all.46 = f32[8,296,128]{2,1,0:T(8,128)S(1)} all-to-all(f32[8,296,128]{2,1,0:T(8,128)S(1)} %bitcast.15), channel_id=1, replica_groups=mesh['seg'=16,'blk'=8] {'blk'}, dimensions={0} | all-to-all | bytes 2424832 | tf_op jit(solution)/shard_map/all_to_all | solution.py:683
  90.8 0.0 copy-done
  90.8 0.0 copy-done.8
  90.8 0.0 copy-done.2
  90.8 0.0 copy-done.4
  90.8 0.0 copy-done.6
  90.8 3.6 %close.1 = (f32[256,768]{1,0:T(8,128)}, f32[256,768]{1,0:T(8,128)}, f32[256,768]{1,0:T(8,128)}, f32[256,768]{1,0:T(8,128)}) custom-call(s32[26]{0:T(128)S(1)} %pad_add_fusion.meta, f32[1536,128]{1,0:T(8,128)S(1)} %copy-done.2, f32[1536,128]{1,0:T(8,128)S(1)} %copy-done.4, f32[1536,128]{1,0:T(8,128)S(1)} %copy-done.6, f32[1536,128]{1,0:T(8,128)S(1)} %copy-done.8, ...), custom_call_target="tpu_custom_call" | custom-call | flops 100000000 | bytes 100000 | tf_op jit(solution)/shard_map/close/pallas_call | solution.py:666
Async XLA Ops:
  4.9 7.7 %copy-start.9 = (s32[2,12]{1,0:T(2,128)S(1)}, s32[2,12]{1,0:T(2,128)}, u32[]{:S(2)}) copy-start(s32[2,12]{1,0:T(2,128)} %offsets.1) | copy-start | bytes 292
  4.9 26.7 %all-to-all-start = ((f32[8,296,128]{2,1,0:T(8,128)}), f32[8,296,128]{2,1,0:T(8,128)S(1)}, u32[]{:S(2)}, u32[]{:S(2)}) async-start(f32[8,296,128]{2,1,0:T(8,128)} %bitcast.18), calls=%async_computation | async-start | bytes 2424832 | tf_op jit(solution)/shard_map/all_to_all | solution.py:683
  24.2 0.9 copy-start.1
  25.0 0.9 copy-start.3
  25.9 0.9 copy-start.5
  26.8 0.9 copy-start.7
  33.2 15.9 %all-to-all-start.1 = ((f32[16,64,128]{2,1,0:T(8,128)}), f32[16,64,128]{2,1,0:T(8,128)S(1)}, u32[]{:S(2)}, u32[]{:S(2)}) async-start(f32[16,64,128]{2,1,0:T(8,128)} %bitcast.17), calls=%async_computation.1 | async-start | bytes 1048576 | tf_op jit(solution)/shard_map/all_to_all | solution.py:683
  40.6 8.4 %collective-permute-start = (f32[72,128]{1,0:T(8,128)S(1)}, f32[72,128]{1,0:T(8,128)S(1)}, u32[]{:S(2)}, u32[]{:S(2)}) collective-permute-start(f32[72,128]{1,0:T(8,128)S(1)} %get-tuple-element.44), channel_id=1, source_target_pairs={{0,8},{8,0},{16,24},{24,16},{32,40},{40,32},{48,56},{56,48},{64,72... | collective-permute-start | bytes 110600 | tf_op jit(solution)/shard_map/ppermute | solution.py:687
  51.9 15.6 %all-to-all-start.2 = ((f32[16,64,128]{2,1,0:T(8,128)}), f32[16,64,128]{2,1,0:T(8,128)S(1)}, u32[]{:S(2)}, u32[]{:S(2)}) async-start(f32[16,64,128]{2,1,0:T(8,128)} %bitcast.19), calls=%async_computation.2 | async-start | bytes 1048576 | tf_op jit(solution)/shard_map/all_to_all | solution.py:683
  56.7 1.5 %collective-permute-start.1 = (f32[72,128]{1,0:T(8,128)S(1)}, f32[72,128]{1,0:T(8,128)S(1)}, u32[]{:S(2)}, u32[]{:S(2)}) collective-permute-start(f32[72,128]{1,0:T(8,128)S(1)} %get-tuple-element.46), channel_id=1, source_target_pairs={{0,8},{8,0},{16,24},{24,16},{32,40},{40,32},{48,56},{56,48},{64,72... | collective-permute-start | bytes 110600 | tf_op jit(solution)/shard_map/ppermute | solution.py:687
  67.6 23.2 %copy-start = (bf16[5024,256]{1,0:T(8,128)(2,1)S(1)}, bf16[5024,256]{1,0:T(8,128)(2,1)}, u32[]{:S(2)}) copy-start(bf16[5024,256]{1,0:T(8,128)(2,1)} %get-tuple-element.39.weights) | copy-start | bytes 7716868
  67.6 23.2 %copy-start.8 = (f32[1536,128]{1,0:T(8,128)S(1)}, f32[1536,128]{1,0:T(8,128)}, u32[]{:S(2)}) copy-start(f32[1536,128]{1,0:T(8,128)} %copy-done.7) | copy-start | bytes 2359300
  68.2 22.6 %copy-start.2 = (f32[1536,128]{1,0:T(8,128)S(1)}, f32[1536,128]{1,0:T(8,128)}, u32[]{:S(2)}) copy-start(f32[1536,128]{1,0:T(8,128)} %copy-done.1) | copy-start | bytes 2359300
  68.2 22.6 %copy-start.4 = (f32[1536,128]{1,0:T(8,128)S(1)}, f32[1536,128]{1,0:T(8,128)}, u32[]{:S(2)}) copy-start(f32[1536,128]{1,0:T(8,128)} %copy-done.3) | copy-start | bytes 2359300
  68.2 22.6 %copy-start.6 = (f32[1536,128]{1,0:T(8,128)S(1)}, f32[1536,128]{1,0:T(8,128)}, u32[]{:S(2)}) copy-start(f32[1536,128]{1,0:T(8,128)} %copy-done.5) | copy-start | bytes 2359300

commit v7 on v6

--- a/solution.py
+++ b/solution.py
@@ -351,11 +351,10 @@
 
 def spread_kernel(meta, got, out, kv, sems):
     k, v = gather_rows(got, FAR_AT + 8, 8), gather_rows(got, FAR_AT + 16, 8)
-    kv[0] = both(k, turn(v))
-    kv[1] = both(turn(k), v)
+    kv[:64, :] = kv[128:192, :] = both(k, turn(v))
+    kv[64:128, :] = kv[192:, :] = both(turn(k), v)
     copies = [
-        pltpu.make_async_copy(kv.at[s % 2], out.at[pl.ds(64 * s, 64), :], sems.at[s])
-        for s in range(16)
+        pltpu.make_async_copy(kv, out.at[pl.ds(256 * s, 256), :], sems.at[s]) for s in range(4)
     ]
     for copy in copies:
         copy.start()
@@ -730,7 +729,7 @@
         (meta, got),
         10**8,
         8,
-        [pltpu.VMEM((2, 64, 128), F32), pltpu.SemaphoreType.DMA((16,))],
+        [pltpu.VMEM((256, 128), F32), pltpu.SemaphoreType.DMA((4,))],
         out_spec=HBM,
     )
     all_keys = swap(keys, "seg")

time: 95.1 us -> 95 us (level)
  no operation moved by 1% of the time
where the time goes in v7:
time: 95 us; the launch traced here: 94.5 us
  Pallas kernels  37.5 us (39%)
  blocking collectives  22.5 us (24%)
  starting transfers between devices  18.3 us (19%)
  waiting for transfers between devices  11.5 us (12%)
  local copies, waits for them, and re-layouts  3.62 us (4%)
    pallas_call x9, Pallas kernels, call(): pl.pallas_call(kernel, name=name, out_shape=[jax.ShapeDtypeStruct(x, F32)...  37.5 us
    all_to_all x1, blocking collectives, swap(): return lax.all_to_all(x, axis, 0, 0, tiled=True)  22.5 us
    all_to_all x3, starting transfers between devices, swap(): return lax.all_to_all(x, axis, 0, 0, tiled=True)  17.5 us
    all_to_all x3, waiting for transfers between devices, swap(): return lax.all_to_all(x, axis, 0, 0, tiled=True)  10.5 us
    unnamed x20, local copies, waits for them, and re-layouts  3.54 us
  transfers between devices with their start and end apart: 5, of which 4 were waited for; matrix products, arithmetic and copies ran while one was open for 0% of the time, Pallas kernels for 26%

profile of v7, /device:TPU:0, one launch (start us, length us, event | category | flops | bytes accessed | tf_op | source)
XLA Modules:
  0.0 94.5 jit_solution(11495233096145224796)
XLA Ops:
  0.6 4.3 %open.1 = (f32[2368,128]{1,0:T(8,128)}, f32[864,128]{1,0:T(8,128)S(1)}) custom-call(s32[2,12]{1,0:T(2,128)} %offsets.1, f32[256,768]{1,0:T(8,128)} %q.3, f32[256,768]{1,0:T(8,128)} %k.5, f32[256,768]{1,0:T(8,128)} %v.5, f32[256,768]{1,0:T(8,128)} %d.3), custom_call_target="tpu_custom_call" | custom-call | flops 100000000 | bytes 100000 | tf_op jit(solution)/shard_map/open/pallas_call | solution.py:665
  4.9 0.0 copy-start.9
  4.9 7.7 %all-to-all-start = ((f32[8,296,128]{2,1,0:T(8,128)}), f32[8,296,128]{2,1,0:T(8,128)S(1)}, u32[]{:S(2)}, u32[]{:S(2)}) async-start(f32[8,296,128]{2,1,0:T(8,128)} %bitcast.18), calls=%async_computation | async-start | bytes 2424832 | tf_op jit(solution)/shard_map/all_to_all | solution.py:682
  12.6 0.0 copy-done.9
  12.6 0.1 reshape.19
  12.7 0.1 pad_add_fusion.meta
  12.8 11.3 %local.1 = (f32[1536,128]{1,0:T(8,128)S(1)}, f32[1536,128]{1,0:T(8,128)S(1)}, f32[1536,128]{1,0:T(8,128)S(1)}, f32[1536,128]{1,0:T(8,128)S(1)}) custom-call(s32[26]{0:T(128)S(1)} %pad_add_fusion.meta, f32[256,768]{1,0:T(8,128)} %q.3, f32[256,768]{1,0:T(8,128)} %k.5, f32[256,768]{1,0:T(8,128)} %v.5, f32[256,768]{1,0:T(8,128)} %d.3), custom_call_target="tpu_custom_call" | custom-call | flops 100000000 | bytes 100000 | tf_op jit(solution)/shard_map/local/pallas_call | solution.py:665
  24.2 0.0 copy-start.1
  24.2 0.9 copy-done.1
  25.0 0.0 copy-start.3
  25.0 0.9 copy-done.3
  25.9 0.0 copy-start.5
  25.9 0.9 copy-done.5
  26.8 0.0 copy-start.7
  26.8 0.9 copy-done.7
  27.7 3.9 %all-to-all-done = f32[8,296,128]{2,1,0:T(8,128)S(1)} async-done(((f32[8,296,128]{2,1,0:T(8,128)}), f32[8,296,128]{2,1,0:T(8,128)S(1)}, u32[]{:S(2)}, u32[]{:S(2)}) %all-to-all-start) | async-done | bytes 1212448 | tf_op jit(solution)/shard_map/all_to_all | solution.py:682
  31.6 1.5 %spread.1 = f32[1024,128]{1,0:T(8,128)} custom-call(s32[26]{0:T(128)S(1)} %pad_add_fusion.meta, f32[2368,128]{1,0:T(8,128)S(1)} %bitcast.10), custom_call_target="tpu_custom_call" | custom-call | flops 100000000 | bytes 100000 | tf_op jit(solution)/shard_map/spread/pallas_call | solution.py:665
  33.1 5.0 %all-to-all-start.1 = ((f32[16,64,128]{2,1,0:T(8,128)}), f32[16,64,128]{2,1,0:T(8,128)S(1)}, u32[]{:S(2)}, u32[]{:S(2)}) async-start(f32[16,64,128]{2,1,0:T(8,128)} %bitcast.17), calls=%async_computation.1 | async-start | bytes 1048576 | tf_op jit(solution)/shard_map/all_to_all | solution.py:682
  38.1 2.4 %near_forward.1 = (f32[8,256]{1,0:T(8,128)S(1)}, f32[72,128]{1,0:T(8,128)S(1)}, f32[72,128]{1,0:T(8,128)S(1)}) custom-call(s32[26]{0:T(128)S(1)} %pad_add_fusion.meta, f32[2368,128]{1,0:T(8,128)S(1)} %bitcast.11), custom_call_target="tpu_custom_call" | custom-call | flops 100000000 | bytes 100000 | tf_op jit(solution)/shard_map/near_forward/pallas_call | solution.py:665
  40.5 0.4 collective-permute-start
  40.9 7.3 %live.1 = (bf16[5024,256]{1,0:T(8,128)(2,1)}, f32[16,128]{1,0:T(8,128)S(1)}) custom-call(s32[26]{0:T(128)S(1)} %pad_add_fusion.meta, f32[256,768]{1,0:T(8,128)} %k.5, f32[256,768]{1,0:T(8,128)} %v.5, f32[864,128]{1,0:T(8,128)S(1)} %get-tuple-element.35.live), custom_call_target="tpu_custom_call" | custom-call | flops 100000000 | bytes 100000 | tf_op jit(solution)/shard_map/live/pallas_call | solution.py:665
  48.2 0.7 all-to-all-done.1
  49.0 0.0 collective-permute-done.pair
  49.0 2.8 %far.1 = (f32[1024,128]{1,0:T(8,128)}, f32[72,128]{1,0:T(8,128)S(1)}, f32[72,128]{1,0:T(8,128)S(1)}) custom-call(s32[26]{0:T(128)S(1)} %pad_add_fusion.meta, f32[1024,128]{1,0:T(8,128)S(1)} %bitcast.14, f32[72,128]{1,0:T(8,128)S(1)} %get-tuple-element.43.mine, f32[72,128]{1,0:T(8,128)S(1)} %collective-permute-done.pair), custom_call_target="tpu_custom_call" | custom-call | flops 100000000 | bytes 100000 | tf_op jit(solution)/shard_map/far/pallas_call | solution.py:665
  51.8 4.8 %all-to-all-start.2 = ((f32[16,64,128]{2,1,0:T(8,128)}), f32[16,64,128]{2,1,0:T(8,128)S(1)}, u32[]{:S(2)}, u32[]{:S(2)}) async-start(f32[16,64,128]{2,1,0:T(8,128)} %bitcast.19), calls=%async_computation.2 | async-start | bytes 1048576 | tf_op jit(solution)/shard_map/all_to_all | solution.py:682
  56.6 0.4 collective-permute-start.1
  57.0 1.1 %collective-permute-done.1.back = f32[72,128]{1,0:T(8,128)S(1)} collective-permute-done((f32[72,128]{1,0:T(8,128)S(1)}, f32[72,128]{1,0:T(8,128)S(1)}, u32[]{:S(2)}, u32[]{:S(2)}) %collective-permute-start.1) | collective-permute-done | bytes 36896 | tf_op jit(solution)/shard_map/ppermute | solution.py:686
  58.1 3.6 %near_backward.1.near = f32[2368,128]{1,0:T(8,128)S(1)} custom-call(s32[26]{0:T(128)S(1)} %pad_add_fusion.meta, f32[2368,128]{1,0:T(8,128)S(1)} %bitcast.12, f32[8,256]{1,0:T(8,128)S(1)} %get-tuple-element.41.own, f32[72,128]{1,0:T(8,128)S(1)} %get-tuple-element.45.keep, f32[72,128]{1,0:T(8,128)S(1)} %collective-permute-done.1.back), custom_call_target="tpu_custom_call" | custom-call | flops 100000000 | bytes 100000 | tf_op jit(solution)/shard_map/near_backward/pallas_call | solution.py:665
  61.6 5.8 %all-to-all-done.2 = f32[16,64,128]{2,1,0:T(8,128)S(1)} async-done(((f32[16,64,128]{2,1,0:T(8,128)}), f32[16,64,128]{2,1,0:T(8,128)S(1)}, u32[]{:S(2)}, u32[]{:S(2)}) %all-to-all-start.2) | async-done | bytes 524320 | tf_op jit(solution)/shard_map/all_to_all | solution.py:682
  67.5 0.0 copy-start
  67.5 0.0 copy-start.8
  67.5 0.7 merge.1
  68.1 0.0 copy-start.2
  68.1 0.0 copy-start.4
  68.1 0.0 copy-start.6
  68.2 22.5 %all_to_all.46 = f32[8,296,128]{2,1,0:T(8,128)S(1)} all-to-all(f32[8,296,128]{2,1,0:T(8,128)S(1)} %bitcast.15), channel_id=1, replica_groups=mesh['seg'=16,'blk'=8] {'blk'}, dimensions={0} | all-to-all | bytes 2424832 | tf_op jit(solution)/shard_map/all_to_all | solution.py:682
  90.7 0.0 copy-done
  90.7 0.0 copy-done.8
  90.7 0.0 copy-done.2
  90.7 0.0 copy-done.4
  90.7 0.0 copy-done.6
  90.7 3.6 %close.1 = (f32[256,768]{1,0:T(8,128)}, f32[256,768]{1,0:T(8,128)}, f32[256,768]{1,0:T(8,128)}, f32[256,768]{1,0:T(8,128)}) custom-call(s32[26]{0:T(128)S(1)} %pad_add_fusion.meta, f32[1536,128]{1,0:T(8,128)S(1)} %copy-done.2, f32[1536,128]{1,0:T(8,128)S(1)} %copy-done.4, f32[1536,128]{1,0:T(8,128)S(1)} %copy-done.6, f32[1536,128]{1,0:T(8,128)S(1)} %copy-done.8, ...), custom_call_target="tpu_custom_call" | custom-call | flops 100000000 | bytes 100000 | tf_op jit(solution)/shard_map/close/pallas_call | solution.py:665
Async XLA Ops:
  4.9 7.7 %copy-start.9 = (s32[2,12]{1,0:T(2,128)S(1)}, s32[2,12]{1,0:T(2,128)}, u32[]{:S(2)}) copy-start(s32[2,12]{1,0:T(2,128)} %offsets.1) | copy-start | bytes 292
  4.9 26.7 %all-to-all-start = ((f32[8,296,128]{2,1,0:T(8,128)}), f32[8,296,128]{2,1,0:T(8,128)S(1)}, u32[]{:S(2)}, u32[]{:S(2)}) async-start(f32[8,296,128]{2,1,0:T(8,128)} %bitcast.18), calls=%async_computation | async-start | bytes 2424832 | tf_op jit(solution)/shard_map/all_to_all | solution.py:682
  24.2 0.9 copy-start.1
  25.0 0.9 copy-start.3
  25.9 0.9 copy-start.5
  26.8 0.9 copy-start.7
  33.1 15.9 %all-to-all-start.1 = ((f32[16,64,128]{2,1,0:T(8,128)}), f32[16,64,128]{2,1,0:T(8,128)S(1)}, u32[]{:S(2)}, u32[]{:S(2)}) async-start(f32[16,64,128]{2,1,0:T(8,128)} %bitcast.17), calls=%async_computation.1 | async-start | bytes 1048576 | tf_op jit(solution)/shard_map/all_to_all | solution.py:682
  40.5 8.4 %collective-permute-start = (f32[72,128]{1,0:T(8,128)S(1)}, f32[72,128]{1,0:T(8,128)S(1)}, u32[]{:S(2)}, u32[]{:S(2)}) collective-permute-start(f32[72,128]{1,0:T(8,128)S(1)} %get-tuple-element.44), channel_id=1, source_target_pairs={{0,8},{8,0},{16,24},{24,16},{32,40},{40,32},{48,56},{56,48},{64,72... | collective-permute-start | bytes 110600 | tf_op jit(solution)/shard_map/ppermute | solution.py:686
  51.8 15.6 %all-to-all-start.2 = ((f32[16,64,128]{2,1,0:T(8,128)}), f32[16,64,128]{2,1,0:T(8,128)S(1)}, u32[]{:S(2)}, u32[]{:S(2)}) async-start(f32[16,64,128]{2,1,0:T(8,128)} %bitcast.19), calls=%async_computation.2 | async-start | bytes 1048576 | tf_op jit(solution)/shard_map/all_to_all | solution.py:682
  56.6 1.5 %collective-permute-start.1 = (f32[72,128]{1,0:T(8,128)S(1)}, f32[72,128]{1,0:T(8,128)S(1)}, u32[]{:S(2)}, u32[]{:S(2)}) collective-permute-start(f32[72,128]{1,0:T(8,128)S(1)} %get-tuple-element.46), channel_id=1, source_target_pairs={{0,8},{8,0},{16,24},{24,16},{32,40},{40,32},{48,56},{56,48},{64,72... | collective-permute-start | bytes 110600 | tf_op jit(solution)/shard_map/ppermute | solution.py:686
  67.5 23.2 %copy-start = (bf16[5024,256]{1,0:T(8,128)(2,1)S(1)}, bf16[5024,256]{1,0:T(8,128)(2,1)}, u32[]{:S(2)}) copy-start(bf16[5024,256]{1,0:T(8,128)(2,1)} %get-tuple-element.39.weights) | copy-start | bytes 7716868
  67.5 23.2 %copy-start.8 = (f32[1536,128]{1,0:T(8,128)S(1)}, f32[1536,128]{1,0:T(8,128)}, u32[]{:S(2)}) copy-start(f32[1536,128]{1,0:T(8,128)} %copy-done.7) | copy-start | bytes 2359300
  68.1 22.6 %copy-start.2 = (f32[1536,128]{1,0:T(8,128)S(1)}, f32[1536,128]{1,0:T(8,128)}, u32[]{:S(2)}) copy-start(f32[1536,128]{1,0:T(8,128)} %copy-done.1) | copy-start | bytes 2359300
  68.1 22.6 %copy-start.4 = (f32[1536,128]{1,0:T(8,128)S(1)}, f32[1536,128]{1,0:T(8,128)}, u32[]{:S(2)}) copy-start(f32[1536,128]{1,0:T(8,128)} %copy-done.3) | copy-start | bytes 2359300
  68.1 22.6 %copy-start.6 = (f32[1536,128]{1,0:T(8,128)S(1)}, f32[1536,128]{1,0:T(8,128)}, u32[]{:S(2)}) copy-start(f32[1536,128]{1,0:T(8,128)} %copy-done.5) | copy-start | bytes 2359300
